TPU v7x, 256 devices: a whole 4x4x8 slice. The times are simulated.
256 devices in a mesh: dp: 8 (over x, y_hi), ctx: 32 (over z, y_lo, core).
Axes of the slice: x: 4, y: 4 (y_hi: 2, y_lo: 2; y = y_hi * 2 + y_lo), z: 8, core: 2. Of those that a mesh axis runs over, the one named last changes fastest.
Arguments:
- queries: bfloat16 [8, 4096, 2048], P('dp', 'ctx'), may hold values from -6 to 6
- key_states: bfloat16 [8, 4096, 2048], P('dp', 'ctx'), may hold values from -6 to 6
- value_states: bfloat16 [8, 4096, 2048], P('dp', 'ctx'), may hold values from -6 to 6
- cotangent: bfloat16 [8, 4096, 2048], P('dp', 'ctx'), may hold values from -6 to 6
- signal: bfloat16 [8, 4096, 128], P('dp', 'ctx'), may hold values from -1500 to 1500
- signal_weight: bfloat16 [2, 128, 4096], replicated, may hold values from -0.5 to 0.5
- embodiment: int32 [8, 4096], P('dp', 'ctx'), may hold values from 0 to 15
- token_type: int32 [8, 4096], P('dp', 'ctx'), may hold values from 0 to 2
- earliest: int32 [8, 4096], P('dp', 'ctx'), may hold values from 0 to 4095, as said below
- prior_mean: float32 [16, 128], replicated, may hold values from -4 to 4
- prior_var: float32 [16, 128], replicated, may hold values from 0.5 to 4
- prior_count: float32 [16], replicated, may hold values from 1000 to 8000
Outputs:
- attended: bfloat16 [8, 4096, 2048], P('dp', 'ctx')
- d_queries: bfloat16 [8, 4096, 2048], P('dp', 'ctx')
- d_keys: bfloat16 [8, 4096, 2048], P('dp', 'ctx')
- d_values: bfloat16 [8, 4096, 2048], P('dp', 'ctx')
- d_signal_weight: bfloat16 [2, 128, 4096], replicated
Inputs may be any that keep to these rules, and one draw needn't show every extreme that they name: In every episode, max(0, t - 384) <= earliest[t] <= t for position t, and the lower bound t - 384 is reached in every draw.
All inputs are finite; a program needn't handle non-finite values.
Results may differ from a plain program's by a relative error of at most 0.005.
The roundings to bfloat16 on the way count: a program that leaves them out, or rounds other values in their place, can miss the bound.
Values may be sent and summed in bfloat16 or wider, within the bound.
No kernel may reach another device: no remote copies, remote signals or barrier semaphores. Data moves between devices by JAX's collectives and lax.ppermute only.
A program may use at most 128 MiB of HBM per device.

v0:
```python
import math

import jax
import jax.numpy as jnp
from jax import lax
from jax.sharding import PartitionSpec as P

HEAD_DIM = 128
HOPS = 3


norm_eps = 1e-05
high_prec = lax.Precision.HIGHEST


def shifted(value, axis, steps):
    count = lax.axis_size(axis)
    leading, last = (max(0, -steps), min(count, count - steps))
    return lax.ppermute(value, axis, [(source, source + steps) for source in range(leading, last)])


def head_groups(query_rows, key_win, value_win, grad_rows, visible, head_count):
    row_count = query_rows.shape[0]
    span_rows = key_win.shape[0]
    group_size = math.gcd(4, head_count)
    group_count = head_count // group_size
    score_scale = 1.0 / math.sqrt(HEAD_DIM)

    def split_heads(array_in, length_rows):
        return jnp.moveaxis(array_in.reshape(length_rows, group_count, group_size, HEAD_DIM), 1, 0)

    def group_step(group_parts):
        query_g, key_g, value_g, grad_g = group_parts
        scores = (
            jnp.einsum("thd,whd->htw", query_g, key_g, preferred_element_type=jnp.float32)
            * score_scale
        )
        scores = jnp.where(visible[None], scores, jnp.float32(-1e30))
        row_max = jnp.max(scores, axis=-1, keepdims=True)
        exponent = jnp.exp(scores - row_max)
        row_total = jnp.sum(exponent, axis=-1, keepdims=True)
        probs_full = exponent / row_total
        probs_low = probs_full.astype(jnp.bfloat16)
        output = jnp.einsum("htw,whd->thd", probs_low, value_g, preferred_element_type=jnp.float32)
        dprobs = jnp.einsum("thd,whd->htw", grad_g, value_g, preferred_element_type=jnp.float32)
        dvalue = jnp.einsum("htw,thd->whd", probs_low, grad_g, preferred_element_type=jnp.float32)
        inner_sum = jnp.sum(probs_full * dprobs, axis=-1, keepdims=True)
        dscore = (probs_full * (dprobs - inner_sum)).astype(jnp.bfloat16)
        dquery = (
            jnp.einsum("htw,whd->thd", dscore, key_g, preferred_element_type=jnp.float32)
            * score_scale
        )
        key_grad = (
            jnp.einsum("htw,thd->whd", dscore, query_g, preferred_element_type=jnp.float32)
            * score_scale
        )
        return (
            output.astype(jnp.bfloat16),
            dquery.astype(jnp.bfloat16),
            key_grad,
            dvalue,
            row_max[..., 0],
            row_total[..., 0],
            inner_sum[..., 0],
        )

    results = lax.map(
        group_step,
        (
            split_heads(query_rows, row_count),
            split_heads(key_win, span_rows),
            split_heads(value_win, span_rows),
            split_heads(grad_rows, row_count),
        ),
    )

    def join_heads(array_in, length_rows):
        return jnp.moveaxis(array_in, 0, 1).reshape(length_rows, head_count * HEAD_DIM)

    return (
        join_heads(results[0], row_count),
        join_heads(results[1], row_count),
        join_heads(results[2], span_rows),
        join_heads(results[3], span_rows),
        results[4].reshape(head_count, row_count),
        results[5].reshape(head_count, row_count),
        results[6].reshape(head_count, row_count),
    )


def on_device(
    queries,
    key_states,
    value_states,
    cotangent,
    signal,
    signal_weight,
    embodiment,
    token_type,
    earliest,
    prior_mean,
    prior_var,
    prior_count,
):
    row_count = queries.shape[1]
    model_width = queries.shape[2]
    sig_width = signal.shape[2]
    kind_count = prior_mean.shape[0]
    head_count = model_width // HEAD_DIM
    sig_values = signal[0].astype(jnp.float32)
    kind_row = token_type[0]
    sig_mask = (kind_row < 2).astype(jnp.float32)
    onehot = (embodiment[0][:, None] == jnp.arange(kind_count, dtype=jnp.int32)[None, :]).astype(
        jnp.float32
    )
    picked = onehot * sig_mask[:, None]
    counts, sum_first, second = lax.psum(
        (
            jnp.sum(picked, axis=0),
            jnp.dot(picked.T, sig_values, precision=high_prec),
            jnp.dot(picked.T, sig_values * sig_values, precision=high_prec),
        ),
        ("dp", "ctx"),
    )
    total_weight = prior_count + counts
    new_mean = (prior_count[:, None] * prior_mean + sum_first) / total_weight[:, None]
    new_square = (
        prior_count[:, None] * (prior_var + prior_mean * prior_mean) + second
    ) / total_weight[:, None]
    inv_std = lax.rsqrt(new_square - new_mean * new_mean + norm_eps)
    token_mean = jnp.dot(onehot, new_mean, precision=high_prec)
    token_inv = jnp.dot(onehot, inv_std, precision=high_prec)
    normed = (sig_values - token_mean) * token_inv
    stacked = jnp.concatenate(
        [
            normed * (kind_row == 0).astype(jnp.float32)[:, None],
            normed * (kind_row == 1).astype(jnp.float32)[:, None],
        ],
        axis=1,
    ).astype(jnp.bfloat16)
    embedded = jnp.dot(
        stacked,
        signal_weight.reshape(2 * sig_width, 2 * model_width),
        preferred_element_type=jnp.float32,
    )
    key_rows = (key_states[0] + embedded[:, :model_width]).astype(jnp.bfloat16)
    value_rows = (value_states[0] + embedded[:, model_width:]).astype(jnp.bfloat16)
    own_block = jnp.stack((key_rows, value_rows))
    blocks = [own_block]
    moving = own_block
    for hop_index in range(HOPS):
        moving = shifted(moving, "ctx", 1)
        blocks.append(moving)
    window = jnp.concatenate(blocks[::-1], axis=1)
    position = lax.axis_index("ctx")
    query_pos = position * row_count + jnp.arange(row_count, dtype=jnp.int32)
    key_pos = (position - HOPS) * row_count + jnp.arange((HOPS + 1) * row_count, dtype=jnp.int32)
    early = earliest[0]
    visible = (key_pos[None, :] >= early[:, None]) & (key_pos[None, :] <= query_pos[:, None])
    attended, dquery, key_grad, dvalue, row_max, row_total, inner_rows = head_groups(
        queries[0], window[0], window[1], cotangent[0], visible, head_count
    )
    pieces = []
    for hop_index in range(HOPS + 1):
        lower = (HOPS - hop_index) * row_count
        pieces.append(
            jnp.stack((key_grad[lower : lower + row_count], dvalue[lower : lower + row_count]))
        )
    grad_total = pieces[HOPS]
    for hop_index in range(HOPS - 1, -1, -1):
        grad_total = shifted(grad_total, "ctx", -1) + pieces[hop_index]
    d_embed = jnp.concatenate([grad_total[0], grad_total[1]], axis=1).astype(jnp.bfloat16)
    partial_term = lax.dot_general(
        stacked, d_embed, (((0,), (0,)), ((), ())), preferred_element_type=jnp.float32
    )
    summed = lax.psum(partial_term, ("dp", "ctx"))
    tokens_all = row_count * lax.axis_size("ctx") * lax.axis_size("dp") * queries.shape[0]
    d_weight = (
        (summed * (1.0 / math.sqrt(tokens_all)))
        .astype(jnp.bfloat16)
        .reshape(2, sig_width, 2 * model_width)
    )
    return (
        attended[None],
        dquery[None],
        grad_total[0].astype(jnp.bfloat16)[None],
        grad_total[1].astype(jnp.bfloat16)[None],
        d_weight,
    )


def solution(mesh):
    return jax.shard_map(
        on_device,
        mesh=mesh,
        in_specs=(
            P("dp", "ctx", None),
            P("dp", "ctx", None),
            P("dp", "ctx", None),
            P("dp", "ctx", None),
            P("dp", "ctx", None),
            P(),
            P("dp", "ctx"),
            P("dp", "ctx"),
            P("dp", "ctx"),
            P(),
            P(),
            P(),
        ),
        out_specs=(
            P("dp", "ctx", None),
            P("dp", "ctx", None),
            P("dp", "ctx", None),
            P("dp", "ctx", None),
            P(),
        ),
        check_vma=False,
    )
```

profile of v0, /device:TPU:1, one launch (start us, length us, event | category | flops | bytes accessed | tf_op | source)
XLA Modules:
  0.0 593.0 jit_solution(6671068451899003200)
XLA Ops:
  11.4 81.6 %all-reduce = (f32[16,128]{1,0:T(8,128)S(1)}, f32[16]{0:T(128)S(1)}, f32[16,128]{1,0:T(8,128)S(1)}) all-reduce(f32[16,128]{1,0:T(8,128)S(1)} %fusion.78, f32[16]{0:T(128)S(1)} %select_reduce_fusion, f32[16,128]{1,0:T(8,128)S(1)} %fusion.76), channel_id=1, replica_groups=mesh['dp'=8,'ctx'=32] {'dp','ctx'}, use_global_device_ids=true, to_apply=%region_0.0 | all-reduce | flops 4112 | bytes 32896 | tf_op jit(solution)/shard_map/psum | solution.py:117
  99.3 11.7 %collective-permute-done = bf16[2,128,2048]{2,1,0:T(8,128)(2,1)S(1)} collective-permute-done((bf16[2,128,2048]{2,1,0:T(8,128)(2,1)S(1)}, bf16[2,128,2048]{2,1,0:T(8,128)(2,1)S(1)}, u32[]{:S(2)}, u32[]{:S(2)}) %collective-permute-start) | collective-permute-done | bytes 1048608 | tf_op jit(solution)/shard_map/ppermute | solution.py:19
  111.0 4.4 collective-permute-start.1
  115.4 11.7 %collective-permute-done.1 = bf16[2,128,2048]{2,1,0:T(8,128)(2,1)S(1)} collective-permute-done((bf16[2,128,2048]{2,1,0:T(8,128)(2,1)S(1)}, bf16[2,128,2048]{2,1,0:T(8,128)(2,1)S(1)}, u32[]{:S(2)}, u32[]{:S(2)}) %collective-permute-start.1) | collective-permute-done | bytes 1048608 | tf_op jit(solution)/shard_map/ppermute | solution.py:19
  127.2 4.4 collective-permute-start.2
  135.7 7.6 %collective-permute-done.2 = bf16[2,128,2048]{2,1,0:T(8,128)(2,1)} collective-permute-done((bf16[2,128,2048]{2,1,0:T(8,128)(2,1)S(1)}, bf16[2,128,2048]{2,1,0:T(8,128)(2,1)}, u32[]{:S(2)}, u32[]{:S(2)}) %collective-permute-start.2) | collective-permute-done | bytes 1048608 | tf_op jit(solution)/shard_map/ppermute | solution.py:19
  146.6 2.7 reshape_squeeze.14
  151.5 3.9 copy.80
  155.4 47.2 %while.17 = (s32[]{:T(128)}, bf16[4,128,4,128]{1,3,2,0:T(8,128)(2,1)}, bf16[4,128,4,128]{1,3,2,0:T(8,128)(2,1)}, f32[4,512,4,128]{1,3,2,0:T(8,128)}, f32[4,512,4...) while((s32[]{:T(128)}, ...), condition=%wide.region_8.9_spmd.clone, body=%wide.region_4.8_spmd.clone.sunk | while | flops 543033344 | bytes 13395077 | solution.py:67
  157.1 2.5 fusion.157
  162.3 2.2 fusion.159
  164.5 2.7 fusion.160
  168.8 2.5 fusion.157
  174.1 2.2 fusion.159
  176.3 2.7 fusion.160
  180.7 2.5 fusion.157
  186.0 2.2 fusion.159
  188.2 2.7 fusion.160
  192.5 2.5 fusion.157
  197.8 2.2 fusion.159
  200.0 2.7 fusion.160
  202.7 4.0 fusion.117
  207.0 4.3 fusion.116
  219.5 23.4 %collective-permute-done.3 = f32[2,128,2048]{2,1,0:T(8,128)} collective-permute-done((f32[2,128,2048]{2,1,0:T(8,128)}, f32[2,128,2048]{2,1,0:T(8,128)}, u32[]{:S(2)}, u32[]{:S(2)}) %collective-permute-start.3) | collective-permute-done | bytes 2097184 | tf_op jit(solution)/shard_map/ppermute | solution.py:19
  242.9 3.2 maximum_add_fusion
  251.2 22.6 %collective-permute-done.4 = f32[2,128,2048]{2,1,0:T(8,128)} collective-permute-done((f32[2,128,2048]{2,1,0:T(8,128)}, f32[2,128,2048]{2,1,0:T(8,128)}, u32[]{:S(2)}, u32[]{:S(2)}) %collective-permute-start.4) | collective-permute-done | bytes 2097184 | tf_op jit(solution)/shard_map/ppermute | solution.py:19
  273.8 3.2 maximum_add_fusion.1
  281.1 23.7 %collective-permute-done.5 = f32[2,128,2048]{2,1,0:T(8,128)} collective-permute-done((f32[2,128,2048]{2,1,0:T(8,128)}, f32[2,128,2048]{2,1,0:T(8,128)}, u32[]{:S(2)}, u32[]{:S(2)}) %collective-permute-start.5) | collective-permute-done | bytes 2097184 | tf_op jit(solution)/shard_map/ppermute | solution.py:19
  306.7 2.7 fusion.70
  311.4 2.2 copy.82
  313.6 268.7 %all-reduce.3.cloned.1.call-done = f32[256,4096]{1,0:T(8,128)} async-done(((f32[256,4096]{1,0:T(8,128)}), f32[256,4096]{1,0:T(8,128)}) %all-reduce.3.cloned.1.call-update) | async-done | bytes 4194320 | tf_op jit(solution)/shard_map/psum | solution.py:176
  582.3 3.9 multiply_convert_fusion.1
  (76 shorter events, 59.1 us)
Async XLA Ops:
  7.2 88.6 %copy-start = (bf16[2,128,4096]{2,1,0:T(8,128)(2,1)S(1)}, bf16[2,128,4096]{2,1,0:T(8,128)(2,1)}, u32[]{:S(2)}) copy-start(bf16[2,128,4096]{2,1,0:T(8,128)(2,1)} %param.19) | copy-start | bytes 6291460
  7.2 575.1 %all-reduce.3.cloned.1.call-start = ((), (), s32[]{:S(2)}) async-start(), calls=%async_computation | async-start | bytes 8388608 | tf_op jit(solution)/shard_map/psum | solution.py:176
  95.8 1.0 copy-start.5
  95.8 1.2 copy-start.6
  97.4 13.7 %collective-permute-start = (bf16[2,128,2048]{2,1,0:T(8,128)(2,1)S(1)}, bf16[2,128,2048]{2,1,0:T(8,128)(2,1)S(1)}, u32[]{:S(2)}, u32[]{:S(2)}) collective-permute-start(bf16[2,128,2048]{2,1,0:T(8,128)(2,1)S(1)} %pad_maximum_fusion.1), channel_id=1, source_target_pairs={{0,1},{1,2},{2,3},{3,4},{4,5},{5,6},{6,7},{7,8},{8,9},{9,10},{10,1... | collective-permute-start | bytes 3145736 | tf_op jit(solution)/shard_map/ppermute | solution.py:19
  111.0 16.1 %collective-permute-start.1 = (bf16[2,128,2048]{2,1,0:T(8,128)(2,1)S(1)}, bf16[2,128,2048]{2,1,0:T(8,128)(2,1)S(1)}, u32[]{:S(2)}, u32[]{:S(2)}) collective-permute-start(bf16[2,128,2048]{2,1,0:T(8,128)(2,1)S(1)} %collective-permute-done), channel_id=1, source_target_pairs={{0,1},{1,2},{2,3},{3,4},{4,5},{5,6},{6,7},{7,8},{8,9},{9,10},{10,1... | collective-permute-start | bytes 3145736 | tf_op jit(solution)/shard_map/ppermute | solution.py:19
  127.2 16.1 %collective-permute-start.2 = (bf16[2,128,2048]{2,1,0:T(8,128)(2,1)S(1)}, bf16[2,128,2048]{2,1,0:T(8,128)(2,1)}, u32[]{:S(2)}, u32[]{:S(2)}) collective-permute-start(bf16[2,128,2048]{2,1,0:T(8,128)(2,1)S(1)} %collective-permute-done.1), channel_id=1, source_target_pairs={{0,1},{1,2},{2,3},{3,4},{4,5},{5,6},{6,7},{7,8},{8,9},{9,10},{10,1... | collective-permute-start | bytes 3145736 | tf_op jit(solution)/shard_map/ppermute | solution.py:19
  151.5 3.9 copy-start.7
  214.5 28.5 %collective-permute-start.3 = (f32[2,128,2048]{2,1,0:T(8,128)}, f32[2,128,2048]{2,1,0:T(8,128)}, u32[]{:S(2)}, u32[]{:S(2)}) collective-permute-start(f32[2,128,2048]{2,1,0:T(8,128)} %pad_maximum_fusion), channel_id=1, source_target_pairs={{1,0},{2,1},{3,2},{4,3},{5,4},{6,5},{7,6},{8,7},{9,8},{10,9},{11,1... | collective-permute-start | bytes 6291464 | tf_op jit(solution)/shard_map/ppermute | solution.py:19
  246.2 27.7 %collective-permute-start.4 = (f32[2,128,2048]{2,1,0:T(8,128)}, f32[2,128,2048]{2,1,0:T(8,128)}, u32[]{:S(2)}, u32[]{:S(2)}) collective-permute-start(f32[2,128,2048]{2,1,0:T(8,128)} %maximum_add_fusion), channel_id=1, source_target_pairs={{1,0},{2,1},{3,2},{4,3},{5,4},{6,5},{7,6},{8,7},{9,8},{10,9},{11,1... | collective-permute-start | bytes 6291464 | tf_op jit(solution)/shard_map/ppermute | solution.py:19
  277.1 27.7 %collective-permute-start.5 = (f32[2,128,2048]{2,1,0:T(8,128)}, f32[2,128,2048]{2,1,0:T(8,128)}, u32[]{:S(2)}, u32[]{:S(2)}) collective-permute-start(f32[2,128,2048]{2,1,0:T(8,128)} %maximum_add_fusion.1), channel_id=1, source_target_pairs={{1,0},{2,1},{3,2},{4,3},{5,4},{6,5},{7,6},{8,7},{9,8},{10,9},{11,1... | collective-permute-start | bytes 6291464 | tf_op jit(solution)/shard_map/ppermute | solution.py:19
  306.7 2.7 copy-start.2
  306.7 2.7 copy-start.3
  309.4 1.0 copy-start.4
  311.4 274.7 %copy-start.1 = (bf16[2,128,4096]{2,1,0:T(8,128)(2,1)S(1)}, bf16[2,128,4096]{2,1,0:T(8,128)(2,1)}, u32[]{:S(2)}) copy-start(bf16[2,128,4096]{2,1,0:T(8,128)(2,1)} %param.19) | copy-start | bytes 6291460
Sparse Core Ops, SparseCore 0:
  309.5 272.7 all-reduce.2
where the time goes:
time: 595 us; the launch traced here: 593 us
  waiting for transfers between devices  369 us (62%)
  blocking collectives  81.6 us (14%)
  matrix products  52.7 us (9%)
  local copies, waits for them, and re-layouts  39 us (7%)
  other arithmetic  19.3 us (3%)
  starting transfers between devices  16.6 us (3%)
  between operations  14.3 us (2%)
    psum x1, waiting for transfers between devices, on_device(): summed = lax.psum(partial_term, ('dp', 'ctx'))  269 us
    ppermute x6, waiting for transfers between devices, shifted(): lax.ppermute(value, axis, [(source, source + steps) for source in range(l...  101 us
    psum x1, blocking collectives, on_device(): lax.psum((jnp.sum(picked, axis=0), jnp.dot(picked.T, sig_values, precisio...  81.6 us
    ppermute x6, starting transfers between devices, shifted(): lax.ppermute(value, axis, [(source, source + steps) for source in range(l...  16.6 us
  transfers between devices with their start and end apart: 7, of which 7 were waited for; matrix products, arithmetic and copies ran while one was open for 3% of the time, Pallas kernels for 0%

commit v1 on v0

v1 whole, which is shorter than its diff:
```python
import math

import jax
import jax.numpy as jnp
from jax import lax
from jax.experimental import pallas as pl
from jax.experimental.pallas import tpu as pltpu
from jax.sharding import Mesh
from jax.sharding import PartitionSpec as P

D = 128
F = 128
E = 16
T = 128
HOPS = 3
G = 4
BAND = (HOPS + 1) * T
WIN = HOPS + G
STAT_ROWS = 2 * E + 8
NORM_EPS = 1e-5
LOG2E = math.log2(math.e)

bf16, f32 = jnp.bfloat16, jnp.float32
NN = (((1,), (0,)), ((), ()))
NT = (((1,), (1,)), ((), ()))
TN = (((0,), (0,)), ((), ()))


def dot(a, b, dims=NN):
    return lax.dot_general(a, b, dims, preferred_element_type=f32)


def stats_kernel(sig_ref, emb_ref, typ_ref, out_ref):
    sig = sig_ref[...]
    picked = (lax.broadcasted_iota(jnp.int32, (T, T), 0) == emb_ref[...]) & (typ_ref[...] < 2)
    pick = jnp.where(picked, 1.0, 0.0).astype(bf16)
    square = sig.astype(f32) * sig.astype(f32)
    high = square.astype(bf16)
    low = (square - high.astype(f32)).astype(bf16)
    first = dot(pick[:E], sig)
    second = dot(pick[:E], high) + dot(pick[:E], low)
    counts = dot(jnp.ones((8, T), bf16), pick, NT)
    for copy in range(out_ref.shape[0]):
        out_ref[copy, 0:E] = first
        out_ref[copy, E : 2 * E] = second
        out_ref[copy, 2 * E :] = counts


def resum_kernel(in_ref, out_ref):
    total = in_ref[0]
    for part in range(1, in_ref.shape[0]):
        total = total + in_ref[part]
    for copy in range(out_ref.shape[0]):
        out_ref[copy] = total


def split3(value):
    high = value.astype(bf16)
    rest = value - high.astype(f32)
    mid = rest.astype(bf16)
    return high, mid, (rest - mid.astype(f32)).astype(bf16)


def main_kernel(
    stat_ref, pmean_ref, pvar_ref, pcount_ref, sig_h_ref, sig_o_ref,
    kh_ref, ko_ref, vh_ref, vo_ref, q_ref, g_ref, wk_ref, wv_ref,
    att_ref, dq_ref, dkh_ref, dko_ref, dvh_ref, dvo_ref, dw_ref,
    stacked_ref, stacked_t_ref, bias_ref, k_ref, v_ref, dk_ref, dv_ref,
):
    scale = 1.0 / math.sqrt(D)

    @pl.when(pl.program_id(0) == 0)
    def _():
        stat = stat_ref[0]
        for part in range(1, stat_ref.shape[0]):
            stat = stat + stat_ref[part]
        diag = lax.broadcasted_iota(jnp.int32, (E, T), 0) == lax.broadcasted_iota(
            jnp.int32, (E, T), 1
        )
        counts = jnp.sum(
            jnp.where(diag, jnp.broadcast_to(stat[2 * E : 2 * E + 1], (E, T)), 0.0),
            axis=1, keepdims=True,
        )
        prior = jnp.sum(
            jnp.where(diag, jnp.broadcast_to(pcount_ref[...], (E, T)), 0.0), axis=1, keepdims=True
        )
        pmean = pmean_ref[...]
        total = prior + counts
        mean = (prior * pmean + stat[0:E]) / total
        square = (prior * (pvar_ref[...] + pmean * pmean) + stat[E : 2 * E]) / total
        inv = lax.rsqrt(square - mean * mean + NORM_EPS)
        zero = jnp.zeros_like(inv)
        table = jnp.concatenate(
            [
                jnp.concatenate([mean, inv, zero], axis=1),
                jnp.concatenate([mean, zero, inv], axis=1),
            ],
            axis=0,
        )
        pieces = split3(table)
        row = lax.broadcasted_iota(jnp.int32, (2 * E, T), 0)
        for b in range(WIN):
            src = sig_h_ref[b] if b < HOPS else sig_o_ref[b - HOPS]
            info = src[T : T + 16].astype(f32)
            code = (info[0:1] + E * info[1:2]).astype(jnp.int32)
            pick = jnp.where(row == code, 1.0, 0.0).astype(bf16)
            per_token = dot(pick, pieces[0], TN) + dot(pick, pieces[1], TN) + dot(pick, pieces[2], TN)
            centred = src[0:T].astype(f32) - per_token[:, 0:F]
            stacked = jnp.concatenate(
                [centred * per_token[:, F : 2 * F], centred * per_token[:, 2 * F :]], axis=1
            )
            stacked_ref[b * T : (b + 1) * T] = stacked.astype(bf16)
            stacked_t_ref[:, b * T : (b + 1) * T] = stacked.T.astype(bf16)
        key_row = lax.broadcasted_iota(jnp.int32, (BAND, T), 0)
        last = lax.broadcasted_iota(jnp.int32, (BAND, T), 1) + HOPS * T
        for b in range(G):
            info = sig_o_ref[b][T : T + 16].astype(f32)
            reach = (16.0 * info[2:3] + info[3:4]).astype(jnp.int32)
            visible = (key_row <= last) & (key_row >= last - reach)
            bias_ref[b] = jnp.where(visible, 0.0, -1e30)

    embed_k = dot(stacked_ref[...], wk_ref[...])
    embed_v = dot(stacked_ref[...], wv_ref[...])
    for b in range(WIN):
        rows = slice(b * T, (b + 1) * T)
        raw_k = kh_ref[b] if b < HOPS else ko_ref[b - HOPS]
        raw_v = vh_ref[b] if b < HOPS else vo_ref[b - HOPS]
        k_ref[rows] = (raw_k.astype(f32) + embed_k[rows]).astype(bf16)
        v_ref[rows] = (raw_v.astype(f32) + embed_v[rows]).astype(bf16)
    for b in range(G):
        band = slice(b * T, b * T + BAND)
        q, g = q_ref[b], g_ref[b]
        key, value = k_ref[band], v_ref[band]
        score = dot(key, q, NT) * (scale * LOG2E) + bias_ref[b]
        expo = jnp.exp2(score - jnp.max(score, axis=0, keepdims=True))
        probs = expo * (1.0 / jnp.sum(expo, axis=0, keepdims=True))
        probs_low = probs.astype(bf16)
        dprobs = dot(value, g, NT)
        inner = jnp.sum(probs * dprobs, axis=0, keepdims=True)
        dscore = (probs * (dprobs - inner)).astype(bf16)
        att_ref[b] = dot(probs_low, value, TN).astype(bf16)
        dq_ref[b] = (dot(dscore, key, TN) * scale).astype(bf16)
        dkey = dot(dscore, q) * scale
        dvalue = dot(probs_low, g)
        if b == 0:
            dk_ref[band], dv_ref[band] = dkey, dvalue
        else:
            old = slice(b * T, b * T + BAND - T)
            new = slice(b * T + BAND - T, b * T + BAND)
            dk_ref[old] += dkey[: BAND - T]
            dv_ref[old] += dvalue[: BAND - T]
            dk_ref[new] = dkey[BAND - T :]
            dv_ref[new] = dvalue[BAND - T :]
    for b in range(WIN):
        rows = slice(b * T, (b + 1) * T)
        if b < HOPS:
            dkh_ref[b] = dk_ref[rows].astype(bf16)
            dvh_ref[b] = dv_ref[rows].astype(bf16)
        else:
            dko_ref[b - HOPS] = dk_ref[rows]
            dvo_ref[b - HOPS] = dv_ref[rows]
    dw_ref[0, 0] = dot(stacked_t_ref[...], dk_ref[...].astype(bf16)).astype(bf16)
    dw_ref[1, 0] = dot(stacked_t_ref[...], dv_ref[...].astype(bf16)).astype(bf16)


def main_call(stat, pmean, pvar, pcount, sig_h, sig_o, kh, ko, vh, vo, q, g, wk, wv):
    heads = ko.shape[2] // D
    whole = lambda a: pl.BlockSpec(a.shape, lambda h: (0,) * a.ndim)
    part = lambda n: pl.BlockSpec((n, T, D), lambda h: (0, 0, h))
    wide = pl.BlockSpec((2 * F, D), lambda h: (0, h))
    shape = lambda n, t: jax.ShapeDtypeStruct((n, T, heads * D), t)
    return pl.pallas_call(
        main_kernel,
        grid=(heads,),
        in_specs=[
            whole(stat), whole(pmean), whole(pvar), whole(pcount), whole(sig_h), whole(sig_o),
            part(HOPS), part(G), part(HOPS), part(G), part(G), part(G), wide, wide,
        ],
        out_specs=[
            part(G), part(G), part(HOPS), part(G), part(HOPS), part(G),
            pl.BlockSpec((2, 1, 2 * F, D), lambda h: (0, h, 0, 0)),
        ],
        out_shape=[
            shape(G, bf16), shape(G, bf16), shape(HOPS, bf16), shape(G, f32),
            shape(HOPS, bf16), shape(G, f32),
            jax.ShapeDtypeStruct((2, heads, 2 * F, D), bf16),
        ],
        scratch_shapes=[
            pltpu.VMEM((WIN * T, 2 * F), bf16),
            pltpu.VMEM((2 * F, WIN * T), bf16),
            pltpu.VMEM((G, BAND, T), f32),
            pltpu.VMEM((WIN * T, D), bf16),
            pltpu.VMEM((WIN * T, D), bf16),
            pltpu.VMEM((WIN * T, D), f32),
            pltpu.VMEM((WIN * T, D), f32),
        ],
        compiler_params=pltpu.CompilerParams(
            dimension_semantics=("arbitrary",), vmem_limit_bytes=32 * 1024 * 1024
        ),
        cost_estimate=pl.CostEstimate(
            flops=3_000_000_000, bytes_accessed=12_000_000, transcendentals=1_000_000
        ),
    )(stat, pmean, pvar, pcount, sig_h, sig_o, kh, ko, vh, vo, q, g, wk, wv)


def exchange(value, axes):
    return lax.all_to_all(value, axes, 0, 0)


def copies(value, axes, count):
    return exchange(jnp.broadcast_to(value[None], (count,) + value.shape), axes)


def by_group(rows):
    return jnp.moveaxis(rows.reshape(T, G, -1), 1, 0)


def by_rows(parts):
    return jnp.moveaxis(parts, 0, 1).reshape(1, T, -1)


def on_device(
    queries, key_states, value_states, cotangent, signal, signal_weight,
    embodiment, token_type, earliest, prior_mean, prior_var, prior_count,
):
    XY, ZC, GROUP = ("x", "yh", "yl"), ("z", "c"), ("yl", "c")
    n_x, n_z = lax.axis_size("x"), lax.axis_size("z")
    n_xh = n_x * lax.axis_size("yh")
    n_xy, n_zc = n_xh * lax.axis_size("yl"), n_z * lax.axis_size("c")
    width = queries.shape[2]
    own = lax.axis_index(GROUP)
    up = [(i, i + 1) for i in range(n_z - 1)]
    down = [(i + 1, i) for i in range(n_z - 1)]

    stat = pl.pallas_call(
        stats_kernel, out_shape=jax.ShapeDtypeStruct((n_xy, STAT_ROWS, T), f32)
    )(signal[0], embodiment, token_type)
    stat = pl.pallas_call(
        resum_kernel, out_shape=jax.ShapeDtypeStruct((n_zc, STAT_ROWS, T), f32)
    )(exchange(stat, XY))
    stat = exchange(stat, ZC)

    ko = exchange(by_group(key_states[0]), GROUP)
    vo = exchange(by_group(value_states[0]), GROUP)
    kh = lax.ppermute(ko[1:], "z", up)
    vh = lax.ppermute(vo[1:], "z", up)
    position = lax.axis_index(("z", "yl", "c")) * T + jnp.arange(T, dtype=jnp.int32)
    reach = position[None] - earliest
    info = jnp.concatenate([embodiment, token_type, reach // 16, reach % 16], axis=0)
    packed = jnp.concatenate([signal[0], jnp.pad(info, ((0, 12), (0, 0))).astype(bf16)], axis=0)
    sig_o = copies(packed, GROUP, G)
    sig_h = lax.ppermute(sig_o[1:], "z", up)
    q = exchange(by_group(queries[0]), GROUP)
    g = exchange(by_group(cotangent[0]), GROUP)
    weight = signal_weight.reshape(2 * F, 2 * width)
    share = width // G
    wk = lax.dynamic_slice_in_dim(weight, own * share, share, 1)
    wv = lax.dynamic_slice_in_dim(weight, width + own * share, share, 1)

    att, dq, dkh, dko, dvh, dvo, dw = main_call(
        stat, prior_mean, prior_var, jnp.pad(prior_count, (0, T - E))[None],
        sig_h, sig_o, kh, ko, vh, vo, q, g, wk, wv,
    )

    dw = dw.reshape(n_xh, 2 * F, D)
    dw = jnp.sum(exchange(dw, ("x", "yh")).astype(f32), axis=0)
    dw = exchange(dw.astype(bf16).reshape(n_z, 2 * F // n_z, D), ("z",))
    tokens = T * lax.axis_size(("x", "yh", "z", "yl", "c"))
    dw = (jnp.sum(dw.astype(f32), axis=0) * (1.0 / math.sqrt(tokens))).astype(bf16)
    dw = copies(dw, ("z",), n_z).reshape(2 * F, D)
    dw = copies(dw, XY, n_xy)
    other = lax.ppermute(dw, "c", [(0, 1), (1, 0)])
    first_core = lax.axis_index("c") == 0
    both = jnp.stack([jnp.where(first_core, dw, other), jnp.where(first_core, other, dw)])
    heads = share // D
    both = both.reshape(2, 2, heads, 2, 2 * F, D)
    d_weight = jnp.transpose(both, (4, 1, 3, 0, 2, 5)).reshape(2, F, 2 * width)

    dk_back = lax.ppermute(dkh, "z", down)
    dv_back = lax.ppermute(dvh, "z", down)
    front = ((1, 0), (0, 0), (0, 0))
    dk = (dko + jnp.pad(dk_back, front).astype(f32)).astype(bf16)
    dv = (dvo + jnp.pad(dv_back, front).astype(f32)).astype(bf16)
    return (
        by_rows(exchange(att, GROUP)),
        by_rows(exchange(dq, GROUP)),
        by_rows(exchange(dk, GROUP)),
        by_rows(exchange(dv, GROUP)),
        d_weight,
    )


def solution(mesh):
    split = Mesh(mesh.devices.reshape(4, 2, 8, 2, 2), ("x", "yh", "z", "yl", "c"))
    dp, ctx = ("x", "yh"), ("z", "yl", "c")
    rows = P(dp, ctx, None)
    return jax.shard_map(
        on_device,
        mesh=split,
        in_specs=(rows, rows, rows, rows, rows, P(), P(dp, ctx), P(dp, ctx), P(dp, ctx), P(), P(), P()),
        out_specs=(rows, rows, rows, rows, P()),
        check_vma=False,
    )
```

time: 595 us -> 266 us (0.45)
  waiting for transfers between devices: 369 us -> 82.7 us
  starting transfers between devices: 16.6 us -> 79.6 us
  matrix products: 52.7 us -> 0 us
  blocking collectives: 81.6 us -> 37.2 us
  Pallas kernels: 0 us -> 18.1 us
  between operations: 14.3 us -> 0.87 us
  other arithmetic: 19.3 us -> 8.6 us
    psum x1 -> x0, waiting for transfers between devices: 269 us -> none  [on_device(): summed = lax.psum(partial_term, ('dp', 'ctx'))]
    ppermute x6, waiting for transfers between devices: 101 us -> 13.7 us  [the longest x1 13.4 us: on_device(): sig_h = lax.ppermute(sig_o[1:], 'z', up)]
    psum x1 -> x0, blocking collectives: 81.6 us -> none  [on_device(): lax.psum((jnp.sum(picked, axis=0), jnp.dot(picked.T, sig_values, precisio...]
    all_to_all x0 -> x12, waiting for transfers between devices: none -> 69 us  [exchange(): return lax.all_to_all(value, axes, 0, 0)]
    all_to_all x0 -> x12, starting transfers between devices: none -> 67.4 us  [exchange(): return lax.all_to_all(value, axes, 0, 0)]
    dot_general x26 -> x0, matrix products: 46.7 us -> none  [the longest x4 10.8 us: group_step(): jnp.einsum('htw,thd->whd', probs_low, grad_g, preferred_element_type=jnp....]
    all_to_all x0 -> x3, blocking collectives: none -> 37.2 us  [exchange(): return lax.all_to_all(value, axes, 0, 0)]
    pallas_call x0 -> x3, Pallas kernels: none -> 18.1 us  [the longest x1 14.6 us: main_call(): pl.pallas_call(main_kernel, grid=(heads,), in_specs=[whole(stat), whole(p...]
  transfers between devices with their start and end apart: 7 -> 18, of which waited for: 7 -> 13; matrix products, arithmetic and copies ran while one was open for 3% -> 8% of each run, Pallas kernels for 0% -> 1%
where the time goes in v1:
time: 266 us; the launch traced here: 264 us
  waiting for transfers between devices  82.7 us (31%)
  starting transfers between devices  79.6 us (30%)
  local copies, waits for them, and re-layouts  37.4 us (14%)
  blocking collectives  37.2 us (14%)
  Pallas kernels  18.1 us (7%)
  other arithmetic  8.6 us (3%)
    all_to_all x12, waiting for transfers between devices, exchange(): return lax.all_to_all(value, axes, 0, 0)  69 us
    all_to_all x12, starting transfers between devices, exchange(): return lax.all_to_all(value, axes, 0, 0)  67.4 us
    all_to_all x3, blocking collectives, exchange(): return lax.all_to_all(value, axes, 0, 0)  37.2 us
    unnamed x64, local copies, waits for them, and re-layouts  21.1 us
    pallas_call x1, Pallas kernels, main_call(): pl.pallas_call(main_kernel, grid=(heads,), in_specs=[whole(stat), whole(p...  14.6 us
    ppermute x1, waiting for transfers between devices, on_device(): sig_h = lax.ppermute(sig_o[1:], 'z', up)  13.4 us
  transfers between devices with their start and end apart: 18, of which 13 were waited for; matrix products, arithmetic and copies ran while one was open for 8% of the time, Pallas kernels for 1%

profile of v1, /device:TPU:1, one launch (start us, length us, event | category | flops | bytes accessed | tf_op | source)
XLA Modules:
  0.0 264.4 jit_solution(8988228965474094466)
XLA Ops:
  4.1 6.5 %all-to-all-start.2 = ((bf16[4,144,128]{2,1,0:T(8,128)(2,1)}), bf16[4,144,128]{2,1,0:T(8,128)(2,1)S(1)}, u32[]{:S(2)}, u32[]{:S(2)}) async-start(bf16[4,144,128]{2,1,0:T(8,128)(2,1)} %broadcast_in_dim.11), calls=%async_computation.2 | async-start | bytes 294912 | tf_op jit(solution)/shard_map/all_to_all | solution.py:207
  12.4 2.0 all-to-all-done.2.sig_o_ref
  14.4 5.0 %all-to-all-start = ((f32[16,40,128]{2,1,0:T(8,128)}), f32[16,40,128]{2,1,0:T(8,128)S(1)}, u32[]{:S(2)}, u32[]{:S(2)}) async-start(f32[16,40,128]{2,1,0:T(8,128)} %shard_map.155), calls=%async_computation | async-start | bytes 655360 | tf_op jit(solution)/shard_map/all_to_all | solution.py:207
  21.7 5.5 %all-to-all-done.in_ref = f32[16,40,128]{2,1,0:T(8,128)S(1)} async-done(((f32[16,40,128]{2,1,0:T(8,128)}), f32[16,40,128]{2,1,0:T(8,128)S(1)}, u32[]{:S(2)}, u32[]{:S(2)}) %all-to-all-start) | async-done | bytes 327712 | tf_op jit(solution)/shard_map/all_to_all | solution.py:207
  27.3 5.9 %all-to-all-start.5 = ((bf16[4,128,512]{2,1,0:T(8,128)(2,1)}), bf16[4,128,512]{2,1,0:T(8,128)(2,1)S(1)}, u32[]{:S(2)}, u32[]{:S(2)}) async-start(bf16[4,128,512]{2,1,0:T(8,128)(2,1)} %bitcast.7), calls=%async_computation.5 | async-start | bytes 1048576 | tf_op jit(solution)/shard_map/all_to_all | solution.py:207
  34.5 6.7 %all-to-all-done.5.q_ref = bf16[4,128,512]{2,1,0:T(8,128)(2,1)S(1)} async-done(((bf16[4,128,512]{2,1,0:T(8,128)(2,1)}), bf16[4,128,512]{2,1,0:T(8,128)(2,1)S(1)}, u32[]{:S(2)}, u32[]{:S(2)}) %all-to-all-start.5) | async-done | bytes 524320 | tf_op jit(solution)/shard_map/all_to_all | solution.py:207
  41.9 4.4 %all-to-all-start.3 = ((bf16[4,128,512]{2,1,0:T(8,128)(2,1)}), bf16[4,128,512]{2,1,0:T(8,128)(2,1)S(1)}, u32[]{:S(2)}, u32[]{:S(2)}) async-start(bf16[4,128,512]{2,1,0:T(8,128)(2,1)} %bitcast.3), calls=%async_computation.3 | async-start | bytes 1048576 | tf_op jit(solution)/shard_map/all_to_all | solution.py:207
  47.7 6.7 %all-to-all-done.3.ko_ref = bf16[4,128,512]{2,1,0:T(8,128)(2,1)S(1)} async-done(((bf16[4,128,512]{2,1,0:T(8,128)(2,1)}), bf16[4,128,512]{2,1,0:T(8,128)(2,1)S(1)}, u32[]{:S(2)}, u32[]{:S(2)}) %all-to-all-start.3) | async-done | bytes 524320 | tf_op jit(solution)/shard_map/all_to_all | solution.py:207
  54.4 4.3 %all-to-all-start.4 = ((bf16[4,128,512]{2,1,0:T(8,128)(2,1)}), bf16[4,128,512]{2,1,0:T(8,128)(2,1)S(1)}, u32[]{:S(2)}, u32[]{:S(2)}) async-start(bf16[4,128,512]{2,1,0:T(8,128)(2,1)} %bitcast.5), calls=%async_computation.4 | async-start | bytes 1048576 | tf_op jit(solution)/shard_map/all_to_all | solution.py:207
  60.0 6.7 %all-to-all-done.4.vo_ref = bf16[4,128,512]{2,1,0:T(8,128)(2,1)S(1)} async-done(((bf16[4,128,512]{2,1,0:T(8,128)(2,1)}), bf16[4,128,512]{2,1,0:T(8,128)(2,1)S(1)}, u32[]{:S(2)}, u32[]{:S(2)}) %all-to-all-start.4) | async-done | bytes 524320 | tf_op jit(solution)/shard_map/all_to_all | solution.py:207
  66.7 4.3 %all-to-all-start.6 = ((bf16[4,128,512]{2,1,0:T(8,128)(2,1)}), bf16[4,128,512]{2,1,0:T(8,128)(2,1)S(1)}, u32[]{:S(2)}, u32[]{:S(2)}) async-start(bf16[4,128,512]{2,1,0:T(8,128)(2,1)} %bitcast.9), calls=%async_computation.6 | async-start | bytes 1048576 | tf_op jit(solution)/shard_map/all_to_all | solution.py:207
  72.7 6.2 %all-to-all-done.6.g_ref = bf16[4,128,512]{2,1,0:T(8,128)(2,1)S(1)} async-done(((bf16[4,128,512]{2,1,0:T(8,128)(2,1)}), bf16[4,128,512]{2,1,0:T(8,128)(2,1)S(1)}, u32[]{:S(2)}, u32[]{:S(2)}) %all-to-all-start.6) | async-done | bytes 524320 | tf_op jit(solution)/shard_map/all_to_all | solution.py:207
  78.9 9.3 %all-to-all-start.1 = ((f32[16,40,128]{2,1,0:T(8,128)}), f32[16,40,128]{2,1,0:T(8,128)S(1)}, u32[]{:S(2)}, u32[]{:S(2)}) async-start(f32[16,40,128]{2,1,0:T(8,128)} %shard_map.156), calls=%async_computation.1 | async-start | bytes 655360 | tf_op jit(solution)/shard_map/all_to_all | solution.py:207
  89.1 3.3 %collective-permute-start.1 = (bf16[3,128,512]{2,1,0:T(8,128)(2,1)}, bf16[3,128,512]{2,1,0:T(8,128)(2,1)S(1)}, u32[]{:S(2)}, u32[]{:S(2)}) collective-permute-start(bf16[3,128,512]{2,1,0:T(8,128)(2,1)} %slice.13), channel_id=1, source_target_pairs={{0,4},{4,8},{8,12},{12,16},{16,20},{20,24},{24,28},{1,5},{5,9},{9,... | collective-permute-start | bytes 1179656 | tf_op jit(solution)/shard_map/ppermute | solution.py:245
  93.2 3.1 %collective-permute-start.2 = (bf16[3,128,512]{2,1,0:T(8,128)(2,1)}, bf16[3,128,512]{2,1,0:T(8,128)(2,1)S(1)}, u32[]{:S(2)}, u32[]{:S(2)}) collective-permute-start(bf16[3,128,512]{2,1,0:T(8,128)(2,1)} %slice.14), channel_id=1, source_target_pairs={{0,4},{4,8},{8,12},{12,16},{16,20},{20,24},{24,28},{1,5},{5,9},{9,... | collective-permute-start | bytes 1179656 | tf_op jit(solution)/shard_map/ppermute | solution.py:246
  98.0 3.1 %collective-permute-start = (bf16[3,144,128]{2,1,0:T(8,128)(2,1)S(1)}, bf16[3,144,128]{2,1,0:T(8,128)(2,1)S(1)}, u32[]{:S(2)}, u32[]{:S(2)}) collective-permute-start(bf16[3,144,128]{2,1,0:T(8,128)(2,1)S(1)} %slice.12), channel_id=1, source_target_pairs={{0,4},{4,8},{8,12},{12,16},{16,20},{20,24},{24,28},{1,5},{5,9},{9,... | collective-permute-start | bytes 331784 | tf_op jit(solution)/shard_map/ppermute | solution.py:252
  101.7 13.4 %collective-permute-done.sig_h_ref = bf16[3,144,128]{2,1,0:T(8,128)(2,1)S(1)} collective-permute-done((bf16[3,144,128]{2,1,0:T(8,128)(2,1)S(1)}, bf16[3,144,128]{2,1,0:T(8,128)(2,1)S(1)}, u32[]{:S(2)}, u32[]{:S(2)}) %collective-permute-start) | collective-permute-done | bytes 110624 | tf_op jit(solution)/shard_map/ppermute | solution.py:252
  126.9 14.6 %shard_map.157 = (bf16[4,128,512]{2,1,0:T(8,128)(2,1)S(1)}, bf16[4,128,512]{2,1,0:T(8,128)(2,1)}, bf16[3,128,512]{2,1,0:T(8,128)(2,1)S(1)}, f32[4,128,512]{2,1,0...) custom-call(f32[16,40,128]{2,1,0:T(8,128)S(1)} %copy-done.6, ...), custom_call_target="tpu_custom_call" | custom-call | flops 3000000000 | bytes 12000000 | tf_op jit(solution)/shard_map/pallas_call | solution.py:172
  143.8 12.8 %all_to_all.75 = bf16[8,256,128]{2,1,0:T(8,128)(2,1)S(1)} all-to-all(bf16[8,256,128]{2,1,0:T(8,128)(2,1)S(1)} %bitcast.27), channel_id=1, replica_groups=mesh['x'=4,'yh'=2,'z'=8,'yl'=2,'c'=2] {'x','yh'}, dimensions={0} | all-to-all | bytes 1048576 | tf_op jit(solution)/shard_map/all_to_all | solution.py:207
  156.7 14.6 %all_to_all.76 = bf16[8,32,128]{2,1,0:T(8,128)(2,1)S(1)} all-to-all(bf16[8,32,128]{2,1,0:T(8,128)(2,1)S(1)} %bitcast.42), channel_id=1, replica_groups=mesh['x'=4,'yh'=2,'z'=8,'yl'=2,'c'=2] {'z'}, dimensions={0} | all-to-all | bytes 131072 | tf_op jit(solution)/shard_map/all_to_all | solution.py:207
  171.3 7.4 %all-to-all-start.7 = ((bf16[4,128,512]{2,1,0:T(8,128)(2,1)}), bf16[4,128,512]{2,1,0:T(8,128)(2,1)S(1)}, u32[]{:S(2)}, u32[]{:S(2)}) async-start(bf16[4,128,512]{2,1,0:T(8,128)(2,1)} %copy-done.4), calls=%async_computation.7 | async-start | bytes 1048576 | tf_op jit(solution)/shard_map/all_to_all | solution.py:207
  178.7 8.0 %all-to-all-done.7 = bf16[4,128,512]{2,1,0:T(8,128)(2,1)S(1)} async-done(((bf16[4,128,512]{2,1,0:T(8,128)(2,1)}), bf16[4,128,512]{2,1,0:T(8,128)(2,1)S(1)}, u32[]{:S(2)}, u32[]{:S(2)}) %all-to-all-start.7) | async-done | bytes 524320 | tf_op jit(solution)/shard_map/all_to_all | solution.py:207
  186.7 9.7 %all_to_all.77 = bf16[8,32,128]{2,1,0:T(8,128)(2,1)S(1)} all-to-all(bf16[8,32,128]{2,1,0:T(8,128)(2,1)S(1)} %broadcast_in_dim.12), channel_id=1, replica_groups=mesh['x'=4,'yh'=2,'z'=8,'yl'=2,'c'=2] {'z'}, dimensions={0} | all-to-all | bytes 131072 | tf_op jit(solution)/shard_map/all_to_all | solution.py:207
  197.6 4.4 %all-to-all-start.14 = ((bf16[16,256,128]{2,1,0:T(8,128)(2,1)}), bf16[16,256,128]{2,1,0:T(8,128)(2,1)}, u32[]{:S(2)}, u32[]{:S(2)}) async-start(bf16[16,256,128]{2,1,0:T(8,128)(2,1)} %broadcast_in_dim.27), calls=%async_computation.14 | async-start | bytes 2097152 | tf_op jit(solution)/shard_map/all_to_all | solution.py:207
  203.3 13.7 %all-to-all-done.14 = bf16[16,256,128]{2,1,0:T(8,128)(2,1)} async-done(((bf16[16,256,128]{2,1,0:T(8,128)(2,1)}), bf16[16,256,128]{2,1,0:T(8,128)(2,1)}, u32[]{:S(2)}, u32[]{:S(2)}) %all-to-all-start.14) | async-done | bytes 1048608 | tf_op jit(solution)/shard_map/all_to_all | solution.py:207
  217.0 7.2 %all-to-all-start.8 = ((bf16[4,128,512]{2,1,0:T(8,128)(2,1)}), bf16[4,128,512]{2,1,0:T(8,128)(2,1)}, u32[]{:S(2)}, u32[]{:S(2)}) async-start(bf16[4,128,512]{2,1,0:T(8,128)(2,1)} %get-tuple-element.13), calls=%async_computation.8 | async-start | bytes 1048576 | tf_op jit(solution)/shard_map/all_to_all | solution.py:207
  227.5 4.7 %all-to-all-done.8 = bf16[4,128,512]{2,1,0:T(8,128)(2,1)} async-done(((bf16[4,128,512]{2,1,0:T(8,128)(2,1)}), bf16[4,128,512]{2,1,0:T(8,128)(2,1)}, u32[]{:S(2)}, u32[]{:S(2)}) %all-to-all-start.8) | async-done | bytes 524320 | tf_op jit(solution)/shard_map/all_to_all | solution.py:207
  232.2 4.3 %all-to-all-start.9 = ((bf16[4,128,512]{2,1,0:T(8,128)(2,1)}), bf16[4,128,512]{2,1,0:T(8,128)(2,1)S(1)}, u32[]{:S(2)}, u32[]{:S(2)}) async-start(bf16[4,128,512]{2,1,0:T(8,128)(2,1)} %add_convert_fusion.1), calls=%async_computation.9 | async-start | bytes 1048576 | tf_op jit(solution)/shard_map/all_to_all | solution.py:207
  238.7 5.8 %all-to-all-done.9 = bf16[4,128,512]{2,1,0:T(8,128)(2,1)S(1)} async-done(((bf16[4,128,512]{2,1,0:T(8,128)(2,1)}), bf16[4,128,512]{2,1,0:T(8,128)(2,1)S(1)}, u32[]{:S(2)}, u32[]{:S(2)}) %all-to-all-start.9) | async-done | bytes 524320 | tf_op jit(solution)/shard_map/all_to_all | solution.py:207
  244.5 4.3 %all-to-all-start.10 = ((bf16[4,128,512]{2,1,0:T(8,128)(2,1)}), bf16[4,128,512]{2,1,0:T(8,128)(2,1)S(1)}, u32[]{:S(2)}, u32[]{:S(2)}) async-start(bf16[4,128,512]{2,1,0:T(8,128)(2,1)} %add_convert_fusion), calls=%async_computation.10 | async-start | bytes 1048576 | tf_op jit(solution)/shard_map/all_to_all | solution.py:207
  253.7 3.1 %all-to-all-done.10 = bf16[4,128,512]{2,1,0:T(8,128)(2,1)S(1)} async-done(((bf16[4,128,512]{2,1,0:T(8,128)(2,1)}), bf16[4,128,512]{2,1,0:T(8,128)(2,1)S(1)}, u32[]{:S(2)}, u32[]{:S(2)}) %all-to-all-start.10) | async-done | bytes 524320 | tf_op jit(solution)/shard_map/all_to_all | solution.py:207
  261.6 2.8 %reshape.59 = bf16[2,128,4096]{2,1,0:T(8,128)(2,1)} reshape(bf16[256,2,2,2,4,128]{5,4,3,2,1,0:T(4,128)(2,1)S(1)} %copy.62) | data formatting | bytes 4194304 | tf_op jit(solution)/shard_map/reshape | solution.py:277
  (105 shorter events, 49.7 us)
Async XLA Ops:
  4.1 10.3 %all-to-all-start.2 = ((bf16[4,144,128]{2,1,0:T(8,128)(2,1)}), bf16[4,144,128]{2,1,0:T(8,128)(2,1)S(1)}, u32[]{:S(2)}, u32[]{:S(2)}) async-start(bf16[4,144,128]{2,1,0:T(8,128)(2,1)} %broadcast_in_dim.11), calls=%async_computation.2 | async-start | bytes 294912 | tf_op jit(solution)/shard_map/all_to_all | solution.py:207
  10.6 22.5 %copy-start.24 = (bf16[1,128,2048]{2,1,0:T(8,128)(2,1)S(1)}, bf16[1,128,2048]{2,1,0:T(8,128)(2,1)}, u32[]{:S(2)}) copy-start(bf16[1,128,2048]{2,1,0:T(8,128)(2,1)} %param.13) | copy-start | bytes 1572868
  14.4 12.9 %all-to-all-start = ((f32[16,40,128]{2,1,0:T(8,128)}), f32[16,40,128]{2,1,0:T(8,128)S(1)}, u32[]{:S(2)}, u32[]{:S(2)}) async-start(f32[16,40,128]{2,1,0:T(8,128)} %shard_map.155), calls=%async_computation | async-start | bytes 655360 | tf_op jit(solution)/shard_map/all_to_all | solution.py:207
  27.3 14.7 %copy-start.23 = (f32[16,40,128]{2,1,0:T(8,128)}, f32[16,40,128]{2,1,0:T(8,128)S(1)}, u32[]{:S(2)}) copy-start(f32[16,40,128]{2,1,0:T(8,128)S(1)} %all-to-all-done.in_ref) | copy-start | bytes 983044
  27.3 19.1 %copy-start.25 = (bf16[1,128,2048]{2,1,0:T(8,128)(2,1)S(1)}, bf16[1,128,2048]{2,1,0:T(8,128)(2,1)}, u32[]{:S(2)}) copy-start(bf16[1,128,2048]{2,1,0:T(8,128)(2,1)} %param.14) | copy-start | bytes 1572868
  27.3 13.9 %all-to-all-start.5 = ((bf16[4,128,512]{2,1,0:T(8,128)(2,1)}), bf16[4,128,512]{2,1,0:T(8,128)(2,1)S(1)}, u32[]{:S(2)}, u32[]{:S(2)}) async-start(bf16[4,128,512]{2,1,0:T(8,128)(2,1)} %bitcast.7), calls=%async_computation.5 | async-start | bytes 1048576 | tf_op jit(solution)/shard_map/all_to_all | solution.py:207
  41.9 16.7 %copy-start.26 = (bf16[1,128,2048]{2,1,0:T(8,128)(2,1)S(1)}, bf16[1,128,2048]{2,1,0:T(8,128)(2,1)}, u32[]{:S(2)}) copy-start(bf16[1,128,2048]{2,1,0:T(8,128)(2,1)} %param.15) | copy-start | bytes 1572868
  41.9 12.4 %all-to-all-start.3 = ((bf16[4,128,512]{2,1,0:T(8,128)(2,1)}), bf16[4,128,512]{2,1,0:T(8,128)(2,1)S(1)}, u32[]{:S(2)}, u32[]{:S(2)}) async-start(bf16[4,128,512]{2,1,0:T(8,128)(2,1)} %bitcast.3), calls=%async_computation.3 | async-start | bytes 1048576 | tf_op jit(solution)/shard_map/all_to_all | solution.py:207
  54.4 12.3 %all-to-all-start.4 = ((bf16[4,128,512]{2,1,0:T(8,128)(2,1)}), bf16[4,128,512]{2,1,0:T(8,128)(2,1)S(1)}, u32[]{:S(2)}, u32[]{:S(2)}) async-start(bf16[4,128,512]{2,1,0:T(8,128)(2,1)} %bitcast.5), calls=%async_computation.4 | async-start | bytes 1048576 | tf_op jit(solution)/shard_map/all_to_all | solution.py:207
  66.7 12.3 %all-to-all-start.6 = ((bf16[4,128,512]{2,1,0:T(8,128)(2,1)}), bf16[4,128,512]{2,1,0:T(8,128)(2,1)S(1)}, u32[]{:S(2)}, u32[]{:S(2)}) async-start(bf16[4,128,512]{2,1,0:T(8,128)(2,1)} %bitcast.9), calls=%async_computation.6 | async-start | bytes 1048576 | tf_op jit(solution)/shard_map/all_to_all | solution.py:207
  71.0 30.2 %copy-start.27 = (f32[16]{0:T(128)S(1)}, f32[16]{0:T(128)}, u32[]{:S(2)}) copy-start(f32[16]{0:T(128)} %param.23) | copy-start | bytes 196
  78.9 39.0 %copy-start.2 = (bf16[4,128,512]{2,1,0:T(8,128)(2,1)}, bf16[4,128,512]{2,1,0:T(8,128)(2,1)S(1)}, u32[]{:S(2)}) copy-start(bf16[4,128,512]{2,1,0:T(8,128)(2,1)S(1)} %all-to-all-done.6.g_ref) | copy-start | bytes 1572868
  78.9 38.3 %all-to-all-start.1 = ((f32[16,40,128]{2,1,0:T(8,128)}), f32[16,40,128]{2,1,0:T(8,128)S(1)}, u32[]{:S(2)}, u32[]{:S(2)}) async-start(f32[16,40,128]{2,1,0:T(8,128)} %shard_map.156), calls=%async_computation.1 | async-start | bytes 655360 | tf_op jit(solution)/shard_map/all_to_all | solution.py:207
  89.1 26.6 %collective-permute-start.1 = (bf16[3,128,512]{2,1,0:T(8,128)(2,1)}, bf16[3,128,512]{2,1,0:T(8,128)(2,1)S(1)}, u32[]{:S(2)}, u32[]{:S(2)}) collective-permute-start(bf16[3,128,512]{2,1,0:T(8,128)(2,1)} %slice.13), channel_id=1, source_target_pairs={{0,4},{4,8},{8,12},{12,16},{16,20},{20,24},{24,28},{1,5},{5,9},{9,... | collective-permute-start | bytes 1179656 | tf_op jit(solution)/shard_map/ppermute | solution.py:245
  93.2 23.3 %collective-permute-start.2 = (bf16[3,128,512]{2,1,0:T(8,128)(2,1)}, bf16[3,128,512]{2,1,0:T(8,128)(2,1)S(1)}, u32[]{:S(2)}, u32[]{:S(2)}) collective-permute-start(bf16[3,128,512]{2,1,0:T(8,128)(2,1)} %slice.14), channel_id=1, source_target_pairs={{0,4},{4,8},{8,12},{12,16},{16,20},{20,24},{24,28},{1,5},{5,9},{9,... | collective-permute-start | bytes 1179656 | tf_op jit(solution)/shard_map/ppermute | solution.py:246
  98.0 17.0 %collective-permute-start = (bf16[3,144,128]{2,1,0:T(8,128)(2,1)S(1)}, bf16[3,144,128]{2,1,0:T(8,128)(2,1)S(1)}, u32[]{:S(2)}, u32[]{:S(2)}) collective-permute-start(bf16[3,144,128]{2,1,0:T(8,128)(2,1)S(1)} %slice.12), channel_id=1, source_target_pairs={{0,4},{4,8},{8,12},{12,16},{16,20},{20,24},{24,28},{1,5},{5,9},{9,... | collective-permute-start | bytes 331784 | tf_op jit(solution)/shard_map/ppermute | solution.py:252
  117.9 1.0 copy-start.1
  119.0 1.0 copy-start.3
  121.9 1.0 copy-start.13
  122.9 1.0 copy-start.15
  171.3 30.6 %copy-start.11 = (bf16[3,128,512]{2,1,0:T(8,128)(2,1)S(1)}, bf16[3,128,512]{2,1,0:T(8,128)(2,1)}, u32[]{:S(2)}) copy-start(bf16[3,128,512]{2,1,0:T(8,128)(2,1)} %copy-done.10) | copy-start | bytes 1179652
  171.3 15.4 %all-to-all-start.7 = ((bf16[4,128,512]{2,1,0:T(8,128)(2,1)}), bf16[4,128,512]{2,1,0:T(8,128)(2,1)S(1)}, u32[]{:S(2)}, u32[]{:S(2)}) async-start(bf16[4,128,512]{2,1,0:T(8,128)(2,1)} %copy-done.4), calls=%async_computation.7 | async-start | bytes 1048576 | tf_op jit(solution)/shard_map/all_to_all | solution.py:207
  186.7 9.7 %copy-start.21 = (bf16[4,128,512]{2,1,0:T(8,128)(2,1)}, bf16[4,128,512]{2,1,0:T(8,128)(2,1)S(1)}, u32[]{:S(2)}) copy-start(bf16[4,128,512]{2,1,0:T(8,128)(2,1)S(1)} %all-to-all-done.7) | copy-start | bytes 1572868
  196.4 27.7 %copy-start.9 = (bf16[3,128,512]{2,1,0:T(8,128)(2,1)S(1)}, bf16[3,128,512]{2,1,0:T(8,128)(2,1)}, u32[]{:S(2)}) copy-start(bf16[3,128,512]{2,1,0:T(8,128)(2,1)} %copy-done.8) | copy-start | bytes 1179652
  197.6 19.4 %all-to-all-start.14 = ((bf16[16,256,128]{2,1,0:T(8,128)(2,1)}), bf16[16,256,128]{2,1,0:T(8,128)(2,1)}, u32[]{:S(2)}, u32[]{:S(2)}) async-start(bf16[16,256,128]{2,1,0:T(8,128)(2,1)} %broadcast_in_dim.27), calls=%async_computation.14 | async-start | bytes 2097152 | tf_op jit(solution)/shard_map/all_to_all | solution.py:207
  202.0 23.6 %collective-permute-start.3 = (bf16[3,128,512]{2,1,0:T(8,128)(2,1)S(1)}, bf16[3,128,512]{2,1,0:T(8,128)(2,1)}, u32[]{:S(2)}, u32[]{:S(2)}) collective-permute-start(bf16[3,128,512]{2,1,0:T(8,128)(2,1)S(1)} %copy-done.11), channel_id=1, source_target_pairs={{4,0},{8,4},{12,8},{16,12},{20,16},{24,20},{28,24},{5,1},{9,5},{13... | collective-permute-start | bytes 1179656 | tf_op jit(solution)/shard_map/ppermute | solution.py:279
  217.0 15.3 %all-to-all-start.8 = ((bf16[4,128,512]{2,1,0:T(8,128)(2,1)}), bf16[4,128,512]{2,1,0:T(8,128)(2,1)}, u32[]{:S(2)}, u32[]{:S(2)}) async-start(bf16[4,128,512]{2,1,0:T(8,128)(2,1)} %get-tuple-element.13), calls=%async_computation.8 | async-start | bytes 1048576 | tf_op jit(solution)/shard_map/all_to_all | solution.py:207
  224.1 12.7 %collective-permute-start.4 = (bf16[3,128,512]{2,1,0:T(8,128)(2,1)S(1)}, bf16[3,128,512]{2,1,0:T(8,128)(2,1)}, u32[]{:S(2)}, u32[]{:S(2)}) collective-permute-start(bf16[3,128,512]{2,1,0:T(8,128)(2,1)S(1)} %copy-done.9), channel_id=1, source_target_pairs={{4,0},{8,4},{12,8},{16,12},{20,16},{24,20},{28,24},{5,1},{9,5},{13... | collective-permute-start | bytes 1179656 | tf_op jit(solution)/shard_map/ppermute | solution.py:280
  225.4 32.7 %collective-permute-start.5 = (bf16[16,256,128]{2,1,0:T(8,128)(2,1)}, bf16[16,256,128]{2,1,0:T(8,128)(2,1)}, u32[]{:S(2)}, u32[]{:S(2)}) collective-permute-start(bf16[16,256,128]{2,1,0:T(8,128)(2,1)} %all-to-all-done.14), channel_id=1, source_target_pairs={{0,1},{1,0},{2,3},{3,2},{4,5},{5,4},{6,7},{7,6},{8,9},{9,8},{10,11... | collective-permute-start | bytes 3145736 | tf_op jit(solution)/shard_map/ppermute | solution.py:272
  227.5 21.3 %copy-start.22 = (bf16[4,128,512]{2,1,0:T(8,128)(2,1)S(1)}, bf16[4,128,512]{2,1,0:T(8,128)(2,1)}, u32[]{:S(2)}) copy-start(bf16[4,128,512]{2,1,0:T(8,128)(2,1)} %copy-done.21) | copy-start | bytes 1572868
  232.2 12.3 %all-to-all-start.9 = ((bf16[4,128,512]{2,1,0:T(8,128)(2,1)}), bf16[4,128,512]{2,1,0:T(8,128)(2,1)S(1)}, u32[]{:S(2)}, u32[]{:S(2)}) async-start(bf16[4,128,512]{2,1,0:T(8,128)(2,1)} %add_convert_fusion.1), calls=%async_computation.9 | async-start | bytes 1048576 | tf_op jit(solution)/shard_map/all_to_all | solution.py:207
  244.5 12.3 %all-to-all-start.10 = ((bf16[4,128,512]{2,1,0:T(8,128)(2,1)}), bf16[4,128,512]{2,1,0:T(8,128)(2,1)S(1)}, u32[]{:S(2)}, u32[]{:S(2)}) async-start(bf16[4,128,512]{2,1,0:T(8,128)(2,1)} %add_convert_fusion), calls=%async_computation.10 | async-start | bytes 1048576 | tf_op jit(solution)/shard_map/all_to_all | solution.py:207
  (14 other events, 10.8 us)

commit v2 on v1

v2 whole, which is shorter than its diff:
```python
import math

import jax
import jax.numpy as jnp
from jax import lax
from jax.experimental import pallas as pl
from jax.experimental.pallas import tpu as pltpu
from jax.sharding import Mesh
from jax.sharding import PartitionSpec as P

D = 128
F = 128
E = 16
T = 128
HOPS = 3
HEADS_AT_ONCE = 1
SWAPS = 4
G = 4
BAND = (HOPS + 1) * T
WIN = HOPS + G
STAT_ROWS = 2 * E + 8
SIG_ROWS = T // G
PIECE_ROWS = 2 * T + SIG_ROWS + 16
NORM_EPS = 1e-5
LOG2E = math.log2(math.e)

bf16, f32 = jnp.bfloat16, jnp.float32
NN = (((1,), (0,)), ((), ()))
NT = (((1,), (1,)), ((), ()))
TN = (((0,), (0,)), ((), ()))
SCALAR = pl.BlockSpec(memory_space=pltpu.SMEM)


def dot(a, b, dims=NN):
    return lax.dot_general(a, b, dims, preferred_element_type=f32)


def stats_kernel(sig_ref, emb_ref, typ_ref, *refs):
    out_ref = refs[-1]
    sig = sig_ref[...]
    picked = (lax.broadcasted_iota(jnp.int32, (T, T), 0) == emb_ref[...]) & (typ_ref[...] < 2)
    pick = jnp.where(picked, 1.0, 0.0).astype(bf16)
    square = sig.astype(f32) * sig.astype(f32)
    high = square.astype(bf16)
    low = (square - high.astype(f32)).astype(bf16)
    first = dot(pick[:E], sig)
    second = dot(pick[:E], high) + dot(pick[:E], low)
    counts = dot(jnp.ones((8, T), bf16), pick, NT)
    for copy in range(out_ref.shape[0]):
        out_ref[copy, 0:E] = first
        out_ref[copy, E : 2 * E] = second
        out_ref[copy, 2 * E :] = counts


def resum_kernel(scale, in_ref, *refs):
    out_ref = refs[-1]
    total = in_ref[0].astype(f32)
    for part in range(1, in_ref.shape[0]):
        total = total + in_ref[part].astype(f32)
    total = (total * scale).astype(out_ref.dtype)
    for copy in range(out_ref.shape[0]):
        out_ref[copy] = total


def resum(parts, count, scale=1.0, after=()):
    return pl.pallas_call(
        lambda *refs: resum_kernel(scale, *refs),
        in_specs=[pl.BlockSpec(parts.shape)] + [pl.BlockSpec(memory_space=pl.ANY)] * len(after),
        out_shape=jax.ShapeDtypeStruct((count,) + parts.shape[1:], parts.dtype),
    )(parts, *after)


def columns_of(own_ref, s, width):
    return pl.ds(pl.multiple_of(lax.bitwise_xor(own_ref[0], s) * width, width), width)


def piece_at(refs, s):
    return refs[s] if s < 2 else refs[2].at[s - 2]


def got_at(refs, s):
    return refs[2].at[0] if s == 2 else refs[s]


def pieces_of(shape):
    return 2 * [jax.ShapeDtypeStruct(shape, bf16)] + [jax.ShapeDtypeStruct((2,) + shape, bf16)]


def pack_kernel(own_ref, k_ref, v_ref, q_ref, g_ref, sig_ref, emb_ref, typ_ref, early_ref, *rest):
    kv_refs, qg_refs = rest[:3], rest[3:]
    width = kv_refs[0].shape[1]
    sig = [sig_ref[j * SIG_ROWS : (j + 1) * SIG_ROWS] for j in range(G)]
    reach = own_ref[2] + lax.broadcasted_iota(jnp.int32, (1, T), 1) - early_ref[...]
    lines = (emb_ref[...], typ_ref[...], lax.shift_right_logical(reach, 4), reach & 15)
    info = jnp.concatenate(list(lines) + [jnp.zeros((12, T), jnp.int32)], axis=0)
    info = info.astype(f32).astype(bf16)
    tail = [jnp.concatenate([sig[j], info if j == 0 else jnp.zeros_like(info)], axis=0) for j in range(G)]
    tail = jnp.concatenate(tail, axis=1)
    for s in range(G):
        columns = columns_of(own_ref, s, width)
        kv_ref, qg_ref = piece_at(kv_refs, s), piece_at(qg_refs, s)
        kv_ref[0:T] = k_ref[:, columns]
        kv_ref[T : 2 * T] = v_ref[:, columns]
        kv_ref[2 * T :] = tail
        qg_ref[0:T] = q_ref[:, columns]
        qg_ref[T : 2 * T] = g_ref[:, columns]


def pack(own, *args):
    width = args[0].shape[1] // G
    shapes = pieces_of((PIECE_ROWS, width)) + pieces_of((2 * T, width))
    out = pl.pallas_call(
        pack_kernel,
        in_specs=[SCALAR] + [pl.BlockSpec(a.shape) for a in args],
        out_shape=shapes,
    )(own, *args)
    return out[:3], out[3:]


def line_up_kernel(own_ref, *refs):
    out_ref = refs[-1]
    for s in range(G):
        block = lax.bitwise_xor(own_ref[0], s)

        @pl.when(block > 0)
        def _():
            out_ref[jnp.maximum(block - 1, 0)] = got_at(refs, s)[...]


def line_up(own, pieces, after):
    return pl.pallas_call(
        line_up_kernel,
        in_specs=[SCALAR]
        + [pl.BlockSpec(a.shape) for a in pieces]
        + [pl.BlockSpec(memory_space=pl.ANY)] * len(after),
        out_shape=jax.ShapeDtypeStruct((HOPS,) + pieces[0].shape, bf16),
    )(own, *pieces, *after)


def second_kernel(in_ref, *refs):
    refs[-1][...] = in_ref[1]


def second_of(pair, after):
    return pl.pallas_call(
        second_kernel,
        in_specs=[pl.BlockSpec(pair.shape)] + [pl.BlockSpec(memory_space=pl.ANY)] * len(after),
        out_shape=jax.ShapeDtypeStruct(pair.shape[1:], pair.dtype),
    )(pair, *after)


def unpack_kernel(own_ref, *refs):
    pieces, (a_ref, b_ref) = refs[:G], refs[-2:]
    width = pieces[0].shape[2]
    for s in range(G):
        columns = columns_of(own_ref, s, width)
        piece = got_at(pieces, s)
        a_ref[:, columns] = piece[0]
        b_ref[:, columns] = piece[1]


def unpack(own, pieces, after=()):
    shape = jax.ShapeDtypeStruct((T, pieces[0].shape[2] * G), bf16)
    return pl.pallas_call(
        unpack_kernel,
        in_specs=[SCALAR]
        + [pl.BlockSpec(a.shape) for a in pieces]
        + [pl.BlockSpec(memory_space=pl.ANY)] * len(after),
        out_shape=[shape, shape],
    )(own, *pieces, *after)


def add_kernel(own_ref, mine_ref, back_ref, *out_refs):
    for s in range(G):
        block = lax.bitwise_xor(own_ref[0], s)
        for kv in range(2):

            @pl.when(block == 0)
            def _():
                piece_at(out_refs, s)[kv] = mine_ref[kv, 0].astype(bf16)

            @pl.when(block > 0)
            def _():
                back = back_ref[kv, jnp.maximum(block - 1, 0)].astype(f32)
                piece_at(out_refs, s)[kv] = (mine_ref[kv, block] + back).astype(bf16)


def add_back(own, mine, back):
    return pl.pallas_call(
        add_kernel,
        in_specs=[SCALAR, pl.BlockSpec(mine.shape), pl.BlockSpec(back.shape)],
        out_shape=pieces_of((2, T, mine.shape[3])),
    )(own, mine, back)


def spread_kernel(heads, place_ref, *refs):
    mine_ref, other_refs, out_ref = refs[0], refs[1:-1], refs[-1]
    core, width = place_ref[1], heads * D
    size = other_refs[0].shape[0]
    for half in range(2):
        base = (core if half == 0 else 1 - core) * width
        for j in range(mine_ref.shape[0]):
            kv, h, y_lo = j // (2 * heads), (j // 2) % heads, j % 2
            column = base + ((kv * 2 + y_lo) * 2 * width + h * D)
            part = mine_ref[j] if half == 0 else other_refs[j // size][j % size]
            out_ref[:, pl.ds(pl.multiple_of(column, D), D)] = part


def spread(place, mine, others, heads):
    return pl.pallas_call(
        lambda *refs: spread_kernel(heads, *refs),
        in_specs=[SCALAR] + [pl.BlockSpec(a.shape) for a in (mine, *others)],
        out_shape=jax.ShapeDtypeStruct((2 * F, 2 * mine.shape[0] * D), bf16),
    )(place, mine, *others)


def split3(value):
    high = value.astype(bf16)
    rest = value - high.astype(f32)
    mid = rest.astype(bf16)
    return high, mid, (rest - mid.astype(f32)).astype(bf16)


def prologue(own, stat_ref, pmean_ref, pvar_ref, pcount_ref, sig_refs, stacked_ref, stacked_t_ref, bias_ref):
    stat = stat_ref[0]
    for part in range(1, stat_ref.shape[0]):
        stat = stat + stat_ref[part]
    diag = lax.broadcasted_iota(jnp.int32, (E, T), 0) == lax.broadcasted_iota(jnp.int32, (E, T), 1)
    column = lambda line: jnp.sum(
        jnp.where(diag, jnp.broadcast_to(line, (E, T)), 0.0), axis=1, keepdims=True
    )
    counts, prior, pmean = column(stat[2 * E : 2 * E + 1]), column(pcount_ref[...]), pmean_ref[...]
    total = prior + counts
    mean = (prior * pmean + stat[0:E]) / total
    square = (prior * (pvar_ref[...] + pmean * pmean) + stat[E : 2 * E]) / total
    inv = lax.rsqrt(square - mean * mean + NORM_EPS)
    zero = jnp.zeros_like(inv)
    table = jnp.concatenate(
        [jnp.concatenate([mean, inv, zero], axis=1), jnp.concatenate([mean, zero, inv], axis=1)], axis=0
    )
    pieces = split3(table)
    row = lax.broadcasted_iota(jnp.int32, (2 * E, T), 0)
    key_row = lax.broadcasted_iota(jnp.int32, (BAND, T), 0)
    last = lax.broadcasted_iota(jnp.int32, (BAND, T), 1) + HOPS * T
    for i, ref in enumerate(sig_refs):
        block = i if i < HOPS else HOPS + lax.bitwise_xor(own, i - HOPS)
        tail = ref[0 : SIG_ROWS + 16]
        info = tail[SIG_ROWS:, 0:T].astype(f32)
        sig = jnp.concatenate([tail[0:SIG_ROWS, j * F : (j + 1) * F] for j in range(G)], axis=0)
        code = (info[0:1] + E * info[1:2]).astype(jnp.int32)
        pick = jnp.where(row == code, 1.0, 0.0).astype(bf16)
        per_token = dot(pick, pieces[0], TN) + dot(pick, pieces[1], TN) + dot(pick, pieces[2], TN)
        centred = sig.astype(f32) - per_token[:, 0:F]
        stacked = jnp.concatenate(
            [centred * per_token[:, F : 2 * F], centred * per_token[:, 2 * F :]], axis=1
        )
        stacked_ref[i * T : (i + 1) * T] = stacked.astype(bf16)
        place = pl.ds(i * T if i < HOPS else pl.multiple_of(block * T, T), T)
        stacked_t_ref[:, place] = stacked.T.astype(bf16)
        if i >= HOPS:
            reach = (16.0 * info[2:3] + info[3:4]).astype(jnp.int32)
            visible = (key_row <= last) & (key_row >= last - reach)
            bias_ref[block - HOPS] = jnp.where(visible, 0.0, -1e30)


def main_kernel(own_ref, stat_ref, pmean_ref, pvar_ref, pcount_ref, *refs):
    halo_in, kv_in, refs = refs[0], refs[1 : 1 + G], refs[1 + G :]
    halo_sig, sig_in, refs = refs[0], refs[1 : 1 + G], refs[1 + G :]
    qg_in, w_ref, refs = refs[:G], refs[G], refs[G + 1 :]
    first_out, halo_ref, mine_ref, dw_ref, refs = refs[:3], refs[3], refs[4], refs[5], refs[6:]
    stacked_ref, stacked_t_ref, bias_ref, kv_ref, grad_ref, pair_ref, a_ref, b_ref = refs
    scale = 1.0 / math.sqrt(D)
    own = own_ref[0]

    @pl.when(pl.program_id(0) == 0)
    def _():
        tails = [halo_sig.at[i] for i in range(HOPS)] + [got_at(sig_in, s) for s in range(G)]
        prologue(
            own, stat_ref, pmean_ref, pvar_ref, pcount_ref, tails, stacked_ref, stacked_t_ref, bias_ref
        )

        pair_ref[...] = jnp.zeros_like(pair_ref)

    pieces = [halo_in.at[i] for i in range(HOPS)] + [got_at(kv_in, s) for s in range(G)]
    for head in range(HEADS_AT_ONCE):
        lanes = slice(head * D, (head + 1) * D)
        embed = dot(stacked_ref[...], jnp.concatenate([w_ref[0, :, lanes], w_ref[1, :, lanes]], axis=1))
        for i in range(WIN):
            rows = slice(i * T, (i + 1) * T)
            block = i if i < HOPS else HOPS + lax.bitwise_xor(own, i - HOPS)
            place = pl.ds(i * T if i < HOPS else pl.multiple_of(block * T, T), T)
            raw = jnp.concatenate([pieces[i][0:T, lanes], pieces[i][T : 2 * T, lanes]], axis=1)
            kv_ref[head, place] = (raw.astype(f32) + embed[rows]).astype(bf16)
        for s in range(G):
            block = lax.bitwise_xor(own, s)
            piece = got_at(qg_in, s)
            pair_ref[head, block, 0:T, 0:D] = piece[0:T, lanes]
            pair_ref[head, block, T:, D:] = piece[T : 2 * T, lanes]
        for b in range(G):
            band = slice(b * T, b * T + BAND)
            both = kv_ref[head, band]
            pair = pair_ref[head, b]
            product = dot(both, pair, NT)
            score, dprobs = product[:, :T] * (scale * LOG2E) + bias_ref[b], product[:, T:]
            expo = jnp.exp2(score - jnp.max(score, axis=0, keepdims=True))
            probs = expo * (1.0 / jnp.sum(expo, axis=0, keepdims=True))
            probs_low = probs.astype(bf16)
            inner = jnp.sum(probs * dprobs, axis=0, keepdims=True)
            dscore = (probs * (dprobs - inner)).astype(bf16)
            a_ref[head, b] = dot(probs_low, both[:, D:], TN).astype(bf16)
            b_ref[head, b] = (dot(dscore, both[:, :D], TN) * scale).astype(bf16)
            grad = dot(jnp.concatenate([dscore, probs_low], axis=1), pair)
            old = slice(b * T, b * T + BAND - T)
            new = slice(b * T + BAND - T, b * T + BAND)
            if b == 0:
                grad_ref[head, old] = grad[: BAND - T]
            else:
                grad_ref[head, old] += grad[: BAND - T]
            grad_ref[head, new] = grad[BAND - T :]
        for s in range(G):
            block = lax.bitwise_xor(own, s)
            piece = piece_at(first_out, s)
            piece[0, :, lanes] = a_ref[head, block]
            piece[1, :, lanes] = b_ref[head, block]
        grad = grad_ref[head]
        low = jnp.concatenate([grad[:, :D] * scale, grad[:, D:]], axis=1).astype(bf16)
        for b in range(WIN):
            for kv in range(2):
                part = low[b * T : (b + 1) * T, kv * D : (kv + 1) * D]
                if b < HOPS:
                    halo_ref[kv, b, :, lanes] = part
                else:
                    mine_ref[kv, b - HOPS, :, lanes] = part
        dw = dot(stacked_t_ref[...], low).astype(bf16)
        dw_ref[0, head] = dw[:, :D]
        dw_ref[1, head] = dw[:, D:]


def main_call(own, stat, pmean, pvar, pcount, halo, kv, qg, w):
    width = w.shape[2]
    heads, lanes = width // D, HEADS_AT_ONCE * D
    whole = lambda a: pl.BlockSpec(a.shape, lambda h, own: (0,) * a.ndim)
    rows = pl.BlockSpec((2 * T, lanes), lambda h, own: (0, h))
    third = pl.BlockSpec((1, 2 * T, lanes), lambda h, own: (0, 0, h))
    early = pl.BlockSpec((HOPS, 2 * T, lanes), lambda h, own: (0, 0, h))
    sig = pl.BlockSpec((T, width), lambda h, own: (2, 0))
    third_sig = pl.BlockSpec((1, T, width), lambda h, own: (0, 2, 0))
    early_sig = pl.BlockSpec((HOPS, T, width), lambda h, own: (0, 2, 0))
    got = lambda spec, third: [spec, spec, third, spec]
    grads = lambda n: pl.BlockSpec((2, n, T, lanes), lambda h, own: (0, 0, 0, h))
    per_head = lambda *shape: pltpu.VMEM((HEADS_AT_ONCE,) + shape[:-1], shape[-1])
    out = pl.pallas_call(
        main_kernel,
        grid_spec=pltpu.PrefetchScalarGridSpec(
            num_scalar_prefetch=1,
            grid=(heads // HEADS_AT_ONCE,),
            in_specs=[whole(stat), whole(pmean), whole(pvar), whole(pcount)]
            + [early] + got(rows, third) + [early_sig] + got(sig, third_sig) + got(rows, third)
            + [pl.BlockSpec((2, 2 * F, lanes), lambda h, own: (0, 0, h))],
            out_specs=2 * [pl.BlockSpec((2, T, lanes), lambda h, own: (0, 0, h))]
            + [pl.BlockSpec((2, 2, T, lanes), lambda h, own: (0, 0, 0, h))]
            + [grads(HOPS), grads(G)]
            + [pl.BlockSpec((2, HEADS_AT_ONCE, 2 * F, D), lambda h, own: (0, h, 0, 0))],
            scratch_shapes=[
                pltpu.VMEM((WIN * T, 2 * F), bf16),
                pltpu.VMEM((2 * F, WIN * T), bf16),
                pltpu.VMEM((G, BAND, T), f32),
                per_head(WIN * T, 2 * D, bf16),
                per_head(WIN * T, 2 * D, f32),
                per_head(G, 2 * T, 2 * D, bf16),
                per_head(G, T, D, bf16),
                per_head(G, T, D, bf16),
            ],
        ),
        out_shape=pieces_of((2, T, width))
        + [
            jax.ShapeDtypeStruct((2, HOPS, T, width), bf16),
            jax.ShapeDtypeStruct((2, G, T, width), bf16),
            jax.ShapeDtypeStruct((2, heads, 2 * F, D), bf16),
        ],
        compiler_params=pltpu.CompilerParams(
            dimension_semantics=("arbitrary",), vmem_limit_bytes=56 * 1024 * 1024
        ),
        cost_estimate=pl.CostEstimate(
            flops=3_000_000_000, bytes_accessed=12_000_000, transcendentals=1_000_000
        ),
    )(own, stat, pmean, pvar, pcount, halo, *kv, halo, *kv, *qg, w)
    return out[:3], out[3], out[4], out[5]


def exchange(value, axes):
    return lax.all_to_all(value, axes, 0, 0)


def on_device(
    queries, key_states, value_states, cotangent, signal, signal_weight,
    embodiment, token_type, earliest, prior_mean, prior_var, prior_count,
):
    XY, Z, GROUP, CTX = ("x", "yh", "yl"), ("zh", "zl"), ("yl", "c"), ("zh", "zl", "yl", "c")
    ZC, PARTS, GATHER = Z + ("c",), ("x", "yh", "zl"), ("x", "yh", "yl", "zl")
    n_xy, n_zc, n_z = lax.axis_size(XY), lax.axis_size(ZC), lax.axis_size(Z)
    width = queries.shape[2]
    share = width // G
    place = [lax.axis_index(GROUP), lax.axis_index("c"), lax.axis_index(CTX) * T]
    place = jnp.stack(place).astype(jnp.int32)

    def swap(value):
        return lax.ppermute(value, "c", [(0, 1), (1, 0)])

    def across(pieces):
        return lax.ppermute(pieces[2], "yl", [(0, 1), (1, 0)])

    def regroup(pieces, crossed, after=()):
        second = second_of(crossed, after) if after else crossed[1]
        return [pieces[0], swap(pieces[1]), crossed, swap(second)]

    kv, qg = pack(
        place, key_states[0], value_states[0], queries[0], cotangent[0], signal[0],
        embodiment, token_type, earliest,
    )
    kv, qg = regroup(kv, across(kv)), regroup(qg, across(qg))

    stat = pl.pallas_call(
        stats_kernel,
        in_specs=[pl.BlockSpec((T, F)), pl.BlockSpec((1, T)), pl.BlockSpec((1, T))]
        + [pl.BlockSpec(memory_space=pl.ANY)],
        out_shape=jax.ShapeDtypeStruct((n_zc, STAT_ROWS, T), f32),
    )(signal[0], embodiment, token_type, kv[1])
    stat = exchange(stat, ZC)
    halo = lax.ppermute(line_up(place, kv, [stat]), Z, [(z, z + 1) for z in range(n_z - 1)])
    stat = exchange(resum(stat, n_xy, after=[qg[2]]), XY)

    weight = signal_weight.reshape(2 * F, 2 * width)
    weight = weight.reshape(2 * F, 2, width)
    weight = jnp.moveaxis(lax.dynamic_slice_in_dim(weight, place[0] * share, share, 2), 1, 0)
    first, back, mine, dw = main_call(
        place, stat, prior_mean, prior_var, jnp.pad(prior_count, (0, T - E))[None], halo, kv, qg, weight
    )

    back = lax.ppermute(back, Z, [(z + 1, z) for z in range(n_z - 1)])
    added = add_back(place, mine, back)
    crossed = across(first)

    heads = share // D
    tokens = T * lax.axis_size(("x", "yh") + CTX)
    n_parts = lax.axis_size(PARTS)
    dw = dw.reshape(n_parts, 2 * heads * 2 * F // n_parts, D)
    dw = resum(exchange(dw, PARTS), lax.axis_size("zh"))
    first = regroup(first, crossed, [dw])
    dw = exchange(dw, ("zh",))
    dw = resum(dw, lax.axis_size(GATHER), 1.0 / math.sqrt(tokens), after=[added[0], crossed])
    dw = exchange(dw, GATHER).reshape(n_xy, 2 * F, D)
    d_weight = spread(place, dw, [swap(part) for part in jnp.split(dw, SWAPS)], heads)
    attended, d_queries = unpack(place, first, after=[d_weight])
    d_keys, d_values = unpack(place, regroup(added, across(added), [d_weight]))
    d_weight = d_weight.reshape(2, F, 2 * width)
    return attended[None], d_queries[None], d_keys[None], d_values[None], d_weight


def solution(mesh):
    split = Mesh(mesh.devices.reshape(4, 2, 4, 2, 2, 2), ("x", "yh", "zh", "zl", "yl", "c"))
    dp, ctx = ("x", "yh"), ("zh", "zl", "yl", "c")
    rows = P(dp, ctx, None)
    return jax.shard_map(
        on_device,
        mesh=split,
        in_specs=(rows, rows, rows, rows, rows, P(), P(dp, ctx), P(dp, ctx), P(dp, ctx), P(), P(), P()),
        out_specs=(rows, rows, rows, rows, P()),
        check_vma=False,
    )
```

time: 266 us -> 157 us (0.59)
  blocking collectives: 37.2 us -> 0 us
  waiting for transfers between devices: 82.7 us -> 46.4 us
  starting transfers between devices: 79.6 us -> 50.8 us
  Pallas kernels: 18.1 us -> 42 us
  local copies, waits for them, and re-layouts: 37.4 us -> 15.6 us
  other arithmetic: 8.6 us -> 0.61 us
    all_to_all x3 -> x0, blocking collectives: 37.2 us -> none  [exchange(): return lax.all_to_all(value, axes, 0, 0)]
    all_to_all x12 -> x5, waiting for transfers between devices: 69 us -> 33.3 us  [exchange(): return lax.all_to_all(value, axes, 0, 0)]
    all_to_all x12 -> x5, starting transfers between devices: 67.4 us -> 34.2 us  [exchange(): return lax.all_to_all(value, axes, 0, 0)]
    pallas_call x3 -> x13, Pallas kernels: 18.1 us -> 42 us  [the longest x1 15 us: main_call(): pl.pallas_call(main_kernel, grid_spec=pltpu.PrefetchScalarGridSpec(num_sc...]
    unnamed x64 -> x47, local copies, waits for them, and re-layouts: 21.1 us -> 9.38 us
    ppermute x6 -> x18, starting transfers between devices: 12.2 us -> 16.6 us  [the longest x12 8.06 us: swap(): return lax.ppermute(value, 'c', [(0, 1), (1, 0)])]
    convert_element_type x3 -> x0, other arithmetic: 3.86 us -> none  [the longest x1 1.93 us: on_device(): dk = (dko + jnp.pad(dk_back, front).astype(f32)).astype(bf16)]
    transpose x5 -> x0, local copies, waits for them, and re-layouts: 3.74 us -> none  [the longest x4 2.11 us: by_rows(): return jnp.moveaxis(parts, 0, 1).reshape(1, T, -1)]
  transfers between devices with their start and end apart: 18 -> 23, of which waited for: 13 -> 7; matrix products, arithmetic and copies ran while one was open for 8% -> 5% of each run, Pallas kernels for 1% -> 13%
where the time goes in v2:
time: 157 us; the launch traced here: 156 us
  starting transfers between devices  50.8 us (32%)
  waiting for transfers between devices  46.4 us (30%)
  Pallas kernels  42 us (27%)
  local copies, waits for them, and re-layouts  15.6 us (10%)
    all_to_all x5, starting transfers between devices, exchange(): return lax.all_to_all(value, axes, 0, 0)  34.2 us
    all_to_all x5, waiting for transfers between devices, exchange(): return lax.all_to_all(value, axes, 0, 0)  33.3 us
    pallas_call x1, Pallas kernels, main_call(): pl.pallas_call(main_kernel, grid_spec=pltpu.PrefetchScalarGridSpec(num_sc...  15 us
    ppermute x1, waiting for transfers between devices, on_device(): back = lax.ppermute(back, Z, [(z + 1, z) for z in range(n_z - 1)])  9.4 us
    unnamed x47, local copies, waits for them, and re-layouts  9.38 us
    ppermute x12, starting transfers between devices, swap(): return lax.ppermute(value, 'c', [(0, 1), (1, 0)])  8.06 us
    pallas_call x3, Pallas kernels, resum(): pl.pallas_call(lambda *refs: resum_kernel(scale, *refs), in_specs=[pl.Blo...  5.49 us
    ppermute x4, starting transfers between devices, across(): return lax.ppermute(pieces[2], 'yl', [(0, 1), (1, 0)])  5.02 us
  transfers between devices with their start and end apart: 23, of which 7 were waited for; matrix products, arithmetic and copies ran while one was open for 5% of the time, Pallas kernels for 13%

profile of v2, /device:TPU:1, one launch (start us, length us, event | category | flops | bytes accessed | tf_op | source)
XLA Modules:
  0.0 156.1 jit_solution(7806307140168372507)
XLA Ops:
  1.3 3.1 %shard_map.155 = (bf16[304,512]{1,0:T(8,128)(2,1)}, bf16[304,512]{1,0:T(8,128)(2,1)}, bf16[2,304,512]{2,1,0:T(8,128)(2,1)}, bf16[256,512]{1,0:T(8,128)(2,1)}, bf...) custom-call(s32[3]{0:T(128)} %pad_add_fusion.own_ref.refs_0_, bf16[128,2048]{1,0:T(8,128)(2,1)} %bitcast.30, ...), custom_call_target="tpu_custom_call" | custom-call | tf_op jit(solution)/shard_map/pallas_call | solution.py:112
  4.3 2.1 %collective-permute-start.2 = (bf16[2,304,512]{2,1,0:T(8,128)(2,1)}, bf16[2,304,512]{2,1,0:T(8,128)(2,1)S(1)}, u32[]{:S(2)}, u32[]{:S(2)}) collective-permute-start(bf16[2,304,512]{2,1,0:T(8,128)(2,1)} %get-tuple-element.27), channel_id=1, source_target_pairs={{0,2},{2,0},{1,3},{3,1},{4,6},{6,4},{5,7},{7,5},{8,10},{10,8},{9,1... | collective-permute-start | bytes 1867784 | tf_op jit(solution)/shard_map/ppermute | solution.py:411
  7.7 1.4 collective-permute-done.refs_0_.refs_1_.refs_2_.refs_7_
  9.8 1.7 %shard_map.156 = f32[16,40,128]{2,1,0:T(8,128)} custom-call(bf16[128,128]{1,0:T(8,128)(2,1)} %bitcast.40, s32[1,128]{1,0:T(1,128)} %emb_ref.3, s32[1,128]{1,0:T(1,128)} %typ_ref.3, bf16[304,512]{1,0:T(8,128)(2,1)} %copy-done.6), custom_call_target="tpu_custom_call" | custom-call | tf_op jit(solution)/shard_map/pallas_call | solution.py:423
  11.5 8.7 %all-to-all-start = ((f32[16,40,128]{2,1,0:T(8,128)}), f32[16,40,128]{2,1,0:T(8,128)S(1)}, u32[]{:S(2)}, u32[]{:S(2)}) async-start(f32[16,40,128]{2,1,0:T(8,128)} %shard_map.156), calls=%async_computation | async-start | bytes 655360 | tf_op jit(solution)/shard_map/all_to_all | solution.py:392
  20.3 1.5 collective-permute-start.3
  21.8 1.5 collective-permute-start.1
  23.3 10.1 %all-to-all-done.refs_0_.refs_4_ = f32[16,40,128]{2,1,0:T(8,128)S(1)} async-done(((f32[16,40,128]{2,1,0:T(8,128)}), f32[16,40,128]{2,1,0:T(8,128)S(1)}, u32[]{:S(2)}, u32[]{:S(2)}) %all-to-all-start) | async-done | bytes 327712 | tf_op jit(solution)/shard_map/all_to_all | solution.py:392
  34.2 2.4 %shard_map.158 = bf16[3,304,512]{2,1,0:T(8,128)(2,1)} custom-call(s32[3]{0:T(128)} %pad_add_fusion.own_ref.refs_0_, bf16[304,512]{1,0:T(8,128)(2,1)} %get-tuple-element.26.refs_0_.refs_1_.refs_6_, bf16[304,512]{1,0:T(8,128)(2,1)} %copy-done.6, bf16[2,304,512]{2,1,0:T(8,128)(2,1)} %copy-done.5, bf16[304,512]{1,0:T(8,128)(2,1)} %copy-done.11, ...), custom_call_target="tpu_custom_call" | custom-call | tf_op jit(solution)/shard_map/pallas_call | solution.py:131
  36.5 2.3 %collective-permute-start.4 = (bf16[3,304,512]{2,1,0:T(8,128)(2,1)}, bf16[3,304,512]{2,1,0:T(8,128)(2,1)}, u32[]{:S(2)}, u32[]{:S(2)}) collective-permute-start(bf16[3,304,512]{2,1,0:T(8,128)(2,1)} %shard_map.158), channel_id=1, source_target_pairs={{0,4},{4,8},{8,12},{12,16},{16,20},{20,24},{24,28},{1,5},{5,9},{9,... | collective-permute-start | bytes 2801672 | tf_op jit(solution)/shard_map/ppermute | solution.py:430
  39.9 1.7 %shard_map.157 = f32[16,40,128]{2,1,0:T(8,128)} custom-call(f32[16,40,128]{2,1,0:T(8,128)} %copy-done.2, bf16[2,256,512]{2,1,0:T(8,128)(2,1)} %copy-done.7), custom_call_target="tpu_custom_call" | custom-call | tf_op jit(solution)/shard_map/pallas_call | solution.py:66
  41.6 6.5 %all-to-all-start.1 = ((f32[16,40,128]{2,1,0:T(8,128)}), f32[16,40,128]{2,1,0:T(8,128)S(1)}, u32[]{:S(2)}, u32[]{:S(2)}) async-start(f32[16,40,128]{2,1,0:T(8,128)} %shard_map.157), calls=%async_computation.1 | async-start | bytes 655360 | tf_op jit(solution)/shard_map/all_to_all | solution.py:392
  49.6 3.3 %reshape_reshape.3 = bf16[256,2,2048]{2,1,0:T(2,128)(2,1)S(1)} reshape(bf16[2,128,4096]{2,1,0:T(8,128)(2,1)} %param.17) | data formatting | bytes 4194304 | tf_op jit(solution)/shard_map/reshape;reshape | solution.py:434
  56.0 2.2 %collective-permute-done.4.refs_0_.refs_5_ = bf16[3,304,512]{2,1,0:T(8,128)(2,1)} collective-permute-done((bf16[3,304,512]{2,1,0:T(8,128)(2,1)}, bf16[3,304,512]{2,1,0:T(8,128)(2,1)}, u32[]{:S(2)}, u32[]{:S(2)}) %collective-permute-start.4) | collective-permute-done | bytes 933920 | tf_op jit(solution)/shard_map/ppermute | solution.py:430
  58.3 15.0 %shard_map.159 = (bf16[2,128,512]{2,1,0:T(8,128)(2,1)}, bf16[2,128,512]{2,1,0:T(8,128)(2,1)}, bf16[2,2,128,512]{3,2,1,0:T(8,128)(2,1)}, bf16[2,3,128,512]{3,2,1,...) custom-call(s32[3]{0:T(128)} %pad_add_fusion.own_ref.refs_0_, ...), custom_call_target="tpu_custom_call" | custom-call | flops 3000000000 | bytes 12000000 | tf_op jit(solution)/shard_map/pallas_call | solution.py:352
  73.3 8.4 %all-to-all-start.2 = ((bf16[16,128,128]{2,1,0:T(8,128)(2,1)}), bf16[16,128,128]{2,1,0:T(8,128)(2,1)S(1)}, u32[]{:S(2)}, u32[]{:S(2)}) async-start(bf16[16,128,128]{2,1,0:T(8,128)(2,1)} %bitcast.35), calls=%async_computation.2 | async-start | bytes 1048576 | tf_op jit(solution)/shard_map/all_to_all | solution.py:392
  81.7 1.3 collective-permute-start.10
  83.1 7.3 %all-to-all-done.2.refs_0_ = bf16[16,128,128]{2,1,0:T(8,128)(2,1)S(1)} async-done(((bf16[16,128,128]{2,1,0:T(8,128)(2,1)}), bf16[16,128,128]{2,1,0:T(8,128)(2,1)S(1)}, u32[]{:S(2)}, u32[]{:S(2)}) %all-to-all-start.2) | async-done | bytes 524320 | tf_op jit(solution)/shard_map/all_to_all | solution.py:392
  91.1 1.8 %shard_map.160.refs_0_ = bf16[4,128,128]{2,1,0:T(8,128)(2,1)} custom-call(bf16[16,128,128]{2,1,0:T(8,128)(2,1)} %copy-done.3), custom_call_target="tpu_custom_call" | custom-call | tf_op jit(solution)/shard_map/pallas_call | solution.py:66
  92.9 3.9 %all-to-all-start.3 = ((bf16[4,128,128]{2,1,0:T(8,128)(2,1)}), bf16[4,128,128]{2,1,0:T(8,128)(2,1)S(1)}, u32[]{:S(2)}, u32[]{:S(2)}) async-start(bf16[4,128,128]{2,1,0:T(8,128)(2,1)} %shard_map.160.refs_0_), calls=%async_computation.3 | async-start | bytes 262144 | tf_op jit(solution)/shard_map/all_to_all | solution.py:392
  96.8 9.4 %collective-permute-done.10.back_ref = bf16[2,3,128,512]{3,2,1,0:T(8,128)(2,1)S(1)} collective-permute-done((bf16[2,3,128,512]{3,2,1,0:T(8,128)(2,1)}, bf16[2,3,128,512]{3,2,1,0:T(8,128)(2,1)S(1)}, u32[]{:S(2)}, u32[]{:S(2)}) %collective-permute-start.10) | collective-permute-done | bytes 786464 | tf_op jit(solution)/shard_map/ppermute | solution.py:440
  107.1 2.7 %shard_map.162 = (bf16[2,128,512]{2,1,0:T(8,128)(2,1)}, bf16[2,128,512]{2,1,0:T(8,128)(2,1)}, bf16[2,2,128,512]{3,2,1,0:T(8,128)(2,1)}) custom-call(s32[3]{0:T(128)} %pad_add_fusion.own_ref.refs_0_, bf16[2,4,128,512]{3,2,1,0:T(8,128)(2,1)} %get-tuple-element.34.mine_ref, bf16[2,3,128,512]{3,2,1,0:T(8,128)(2,1)} %copy-done.8), custom_call_target="tpu_custom_call" | custom-call | tf_op jit(solution)/shard_map/pallas_call | solution.py:189
  110.6 2.0 %shard_map.163 = bf16[32,128,128]{2,1,0:T(8,128)(2,1)} custom-call(bf16[4,128,128]{2,1,0:T(8,128)(2,1)} %copy-done.9, bf16[2,128,512]{2,1,0:T(8,128)(2,1)} %get-tuple-element.36.refs_1_.refs_0_, bf16[2,2,128,512]{3,2,1,0:T(8,128)(2,1)} %copy-done.1), custom_call_target="tpu_custom_call" | custom-call | tf_op jit(solution)/shard_map/pallas_call | solution.py:66
  112.6 6.8 %all-to-all-start.4 = ((bf16[32,128,128]{2,1,0:T(8,128)(2,1)}), bf16[32,128,128]{2,1,0:T(8,128)(2,1)S(1)}, u32[]{:S(2)}, u32[]{:S(2)}) async-start(bf16[32,128,128]{2,1,0:T(8,128)(2,1)} %shard_map.163), calls=%async_computation.4 | async-start | bytes 2097152 | tf_op jit(solution)/shard_map/all_to_all | solution.py:392
  119.4 1.3 collective-permute-start.16
  120.7 14.7 %all-to-all-done.4 = bf16[32,128,128]{2,1,0:T(8,128)(2,1)S(1)} async-done(((bf16[32,128,128]{2,1,0:T(8,128)(2,1)}), bf16[32,128,128]{2,1,0:T(8,128)(2,1)S(1)}, u32[]{:S(2)}, u32[]{:S(2)}) %all-to-all-start.4) | async-done | bytes 1048608 | tf_op jit(solution)/shard_map/all_to_all | solution.py:392
  136.3 2.9 %collective-permute-start.13 = (bf16[4,256,128]{2,1,0:T(8,128)(2,1)S(1)}, bf16[4,256,128]{2,1,0:T(8,128)(2,1)S(1)}, u32[]{:S(2)}, u32[]{:S(2)}) collective-permute-start(bf16[4,256,128]{2,1,0:T(8,128)(2,1)S(1)} %bitcast.38), channel_id=1, source_target_pairs={{0,1},{1,0},{2,3},{3,2},{4,5},{5,4},{6,7},{7,6},{8,9},{9,8},{10,11... | collective-permute-start | bytes 786440 | tf_op jit(solution)/shard_map/ppermute | solution.py:408
  139.7 1.8 %shard_map.161 = bf16[2,128,512]{2,1,0:T(8,128)(2,1)} custom-call(bf16[2,2,128,512]{3,2,1,0:T(8,128)(2,1)} %copy-done.1, bf16[4,128,128]{2,1,0:T(8,128)(2,1)} %shard_map.160.refs_0_), custom_call_target="tpu_custom_call" | custom-call | tf_op jit(solution)/shard_map/pallas_call | solution.py:145
  143.2 3.5 %shard_map.164.refs_4_.refs_0_ = bf16[256,4096]{1,0:T(8,128)(2,1)} custom-call(s32[3]{0:T(128)} %pad_add_fusion.own_ref.refs_0_, bf16[16,256,128]{2,1,0:T(8,128)(2,1)} %bitcast.29, bf16[4,256,128]{2,1,0:T(8,128)(2,1)} %copy-done.17, bf16[4,256,128]{2,1,0:T(8,128)(2,1)} %copy-done.16, bf16[4,256,128]{2,1,0:T(8,128)(2,1)} %copy-done.14, ...), custom_call_target="tpu_custom_call" | custom-call | tf_op jit(solution)/shard_map/pallas_call | solution.py:210
  147.5 1.8 %shard_map.166 = bf16[2,128,512]{2,1,0:T(8,128)(2,1)} custom-call(bf16[2,2,128,512]{3,2,1,0:T(8,128)(2,1)} %copy-done.4, bf16[256,4096]{1,0:T(8,128)(2,1)} %shard_map.164.refs_4_.refs_0_), custom_call_target="tpu_custom_call" | custom-call | tf_op jit(solution)/shard_map/pallas_call | solution.py:145
  150.1 2.3 %shard_map.165 = (bf16[128,2048]{1,0:T(8,128)(2,1)}, bf16[128,2048]{1,0:T(8,128)(2,1)}) custom-call(s32[3]{0:T(128)} %pad_add_fusion.own_ref.refs_0_, bf16[2,128,512]{2,1,0:T(8,128)(2,1)} %get-tuple-element.30.refs_0_, bf16[2,128,512]{2,1,0:T(8,128)(2,1)} %copy-done.13, bf16[2,2,128,512]{3,2,1,0:T(8,128)(2,1)} %copy-done.1, bf16[2,128,512]{2,1,0:T(8,128)(2,1)} %copy-done.18, ...), custom_call_target="tpu_custom_call" | custom-call | tf_op jit(solution)/shard_map/pallas_call | solution.py:164
  153.8 2.3 %shard_map.167 = (bf16[128,2048]{1,0:T(8,128)(2,1)}, bf16[128,2048]{1,0:T(8,128)(2,1)}) custom-call(s32[3]{0:T(128)} %pad_add_fusion.own_ref.refs_0_, bf16[2,128,512]{2,1,0:T(8,128)(2,1)} %get-tuple-element.36.refs_1_.refs_0_, bf16[2,128,512]{2,1,0:T(8,128)(2,1)} %copy-done.12, bf16[2,2,128,512]{3,2,1,0:T(8,128)(2,1)} %copy-done.4, ...), custom_call_target="tpu_custom_call" | custom-call | tf_op jit(solution)/shard_map/pallas_call | solution.py:164
  (81 shorter events, 18.0 us)
Async XLA Ops:
  4.3 15.9 %collective-permute-start.2 = (bf16[2,304,512]{2,1,0:T(8,128)(2,1)}, bf16[2,304,512]{2,1,0:T(8,128)(2,1)S(1)}, u32[]{:S(2)}, u32[]{:S(2)}) collective-permute-start(bf16[2,304,512]{2,1,0:T(8,128)(2,1)} %get-tuple-element.27), channel_id=1, source_target_pairs={{0,2},{2,0},{1,3},{3,1},{4,6},{6,4},{5,7},{7,5},{8,10},{10,8},{9,1... | collective-permute-start | bytes 1867784 | tf_op jit(solution)/shard_map/ppermute | solution.py:411
  6.5 2.6 %collective-permute-start = (bf16[304,512]{1,0:T(8,128)(2,1)}, bf16[304,512]{1,0:T(8,128)(2,1)S(1)}, u32[]{:S(2)}, u32[]{:S(2)}) collective-permute-start(bf16[304,512]{1,0:T(8,128)(2,1)} %get-tuple-element.24), channel_id=1, source_target_pairs={{0,1},{1,0},{2,3},{3,2},{4,5},{5,4},{6,7},{7,6},{8,9},{9,8},{10,11... | collective-permute-start | bytes 933896 | tf_op jit(solution)/shard_map/ppermute | solution.py:408
  11.5 27.3 %copy-start.20 = (bf16[256,512]{1,0:T(8,128)(2,1)S(1)}, bf16[256,512]{1,0:T(8,128)(2,1)}, u32[]{:S(2)}) copy-start(bf16[256,512]{1,0:T(8,128)(2,1)} %get-tuple-element.29) | copy-start | bytes 786436
  11.5 21.8 %all-to-all-start = ((f32[16,40,128]{2,1,0:T(8,128)}), f32[16,40,128]{2,1,0:T(8,128)S(1)}, u32[]{:S(2)}, u32[]{:S(2)}) async-start(f32[16,40,128]{2,1,0:T(8,128)} %shard_map.156), calls=%async_computation | async-start | bytes 655360 | tf_op jit(solution)/shard_map/all_to_all | solution.py:392
  20.3 13.1 %copy-start.5 = (bf16[2,304,512]{2,1,0:T(8,128)(2,1)}, bf16[2,304,512]{2,1,0:T(8,128)(2,1)S(1)}, u32[]{:S(2)}) copy-start(bf16[2,304,512]{2,1,0:T(8,128)(2,1)S(1)} %collective-permute-done.2.refs_2_.refs_3_.refs_8_) | copy-start | bytes 1867780
  20.3 13.0 %collective-permute-start.3 = (bf16[304,512]{1,0:T(8,128)(2,1)S(1)}, bf16[304,512]{1,0:T(8,128)(2,1)S(1)}, u32[]{:S(2)}, u32[]{:S(2)}) collective-permute-start(bf16[304,512]{1,0:T(8,128)(2,1)S(1)} %slice_bitcast_fusion), channel_id=1, source_target_pairs={{0,1},{1,0},{2,3},{3,2},{4,5},{5,4},{6,7},{7,6},{8,9},{9,8},{10,11... | collective-permute-start | bytes 933896 | tf_op jit(solution)/shard_map/ppermute | solution.py:408
  21.8 17.3 %collective-permute-start.1 = (bf16[2,256,512]{2,1,0:T(8,128)(2,1)}, bf16[2,256,512]{2,1,0:T(8,128)(2,1)S(1)}, u32[]{:S(2)}, u32[]{:S(2)}) collective-permute-start(bf16[2,256,512]{2,1,0:T(8,128)(2,1)} %get-tuple-element.25), channel_id=1, source_target_pairs={{0,2},{2,0},{1,3},{3,1},{4,6},{6,4},{5,7},{7,5},{8,10},{10,8},{9,1... | collective-permute-start | bytes 1572872 | tf_op jit(solution)/shard_map/ppermute | solution.py:411
  33.3 0.8 copy-start.11
  36.5 21.7 %collective-permute-start.4 = (bf16[3,304,512]{2,1,0:T(8,128)(2,1)}, bf16[3,304,512]{2,1,0:T(8,128)(2,1)}, u32[]{:S(2)}, u32[]{:S(2)}) collective-permute-start(bf16[3,304,512]{2,1,0:T(8,128)(2,1)} %shard_map.158), channel_id=1, source_target_pairs={{0,4},{4,8},{8,12},{12,16},{16,20},{20,24},{24,28},{1,5},{5,9},{9,... | collective-permute-start | bytes 2801672 | tf_op jit(solution)/shard_map/ppermute | solution.py:430
  38.8 16.0 %collective-permute-start.5 = (bf16[256,512]{1,0:T(8,128)(2,1)S(1)}, bf16[256,512]{1,0:T(8,128)(2,1)S(1)}, u32[]{:S(2)}, u32[]{:S(2)}) collective-permute-start(bf16[256,512]{1,0:T(8,128)(2,1)S(1)} %copy-done.20), channel_id=1, source_target_pairs={{0,1},{1,0},{2,3},{3,2},{4,5},{5,4},{6,7},{7,6},{8,9},{9,8},{10,11... | collective-permute-start | bytes 786440 | tf_op jit(solution)/shard_map/ppermute | solution.py:408
  41.6 14.4 %all-to-all-start.1 = ((f32[16,40,128]{2,1,0:T(8,128)}), f32[16,40,128]{2,1,0:T(8,128)S(1)}, u32[]{:S(2)}, u32[]{:S(2)}) async-start(f32[16,40,128]{2,1,0:T(8,128)} %shard_map.157), calls=%async_computation.1 | async-start | bytes 655360 | tf_op jit(solution)/shard_map/all_to_all | solution.py:392
  49.1 5.7 %collective-permute-start.6 = (bf16[256,512]{1,0:T(8,128)(2,1)S(1)}, bf16[256,512]{1,0:T(8,128)(2,1)}, u32[]{:S(2)}, u32[]{:S(2)}) collective-permute-start(bf16[256,512]{1,0:T(8,128)(2,1)S(1)} %slice_bitcast_fusion.1), channel_id=1, source_target_pairs={{0,1},{1,0},{2,3},{3,2},{4,5},{5,4},{6,7},{7,6},{8,9},{9,8},{10,11... | collective-permute-start | bytes 786440 | tf_op jit(solution)/shard_map/ppermute | solution.py:408
  53.0 1.2 copy-start.22
  54.8 3.5 %copy-start.21 = (bf16[256,512]{1,0:T(8,128)(2,1)}, bf16[256,512]{1,0:T(8,128)(2,1)S(1)}, u32[]{:S(2)}) copy-start(bf16[256,512]{1,0:T(8,128)(2,1)S(1)} %collective-permute-done.5.refs_11_) | copy-start | bytes 786436
  56.0 2.2 %copy-start.10 = (f32[16,40,128]{2,1,0:T(8,128)}, f32[16,40,128]{2,1,0:T(8,128)S(1)}, u32[]{:S(2)}) copy-start(f32[16,40,128]{2,1,0:T(8,128)S(1)} %all-to-all-done.1.stat_ref) | copy-start | bytes 983044
  73.3 17.1 %all-to-all-start.2 = ((bf16[16,128,128]{2,1,0:T(8,128)(2,1)}), bf16[16,128,128]{2,1,0:T(8,128)(2,1)S(1)}, u32[]{:S(2)}, u32[]{:S(2)}) async-start(bf16[16,128,128]{2,1,0:T(8,128)(2,1)} %bitcast.35), calls=%async_computation.2 | async-start | bytes 1048576 | tf_op jit(solution)/shard_map/all_to_all | solution.py:392
  81.7 24.5 %collective-permute-start.10 = (bf16[2,3,128,512]{3,2,1,0:T(8,128)(2,1)}, bf16[2,3,128,512]{3,2,1,0:T(8,128)(2,1)S(1)}, u32[]{:S(2)}, u32[]{:S(2)}) collective-permute-start(bf16[2,3,128,512]{3,2,1,0:T(8,128)(2,1)} %get-tuple-element.35), channel_id=1, source_target_pairs={{4,0},{8,4},{12,8},{16,12},{20,16},{24,20},{28,24},{5,1},{9,5},{13... | collective-permute-start | bytes 2359304 | tf_op jit(solution)/shard_map/ppermute | solution.py:440
  83.0 26.8 %collective-permute-start.8 = (bf16[2,2,128,512]{3,2,1,0:T(8,128)(2,1)}, bf16[2,2,128,512]{3,2,1,0:T(8,128)(2,1)S(1)}, u32[]{:S(2)}, u32[]{:S(2)}) collective-permute-start(bf16[2,2,128,512]{3,2,1,0:T(8,128)(2,1)} %get-tuple-element.32), channel_id=1, source_target_pairs={{0,2},{2,0},{1,3},{3,1},{4,6},{6,4},{5,7},{7,5},{8,10},{10,8},{9,1... | collective-permute-start | bytes 1572872 | tf_op jit(solution)/shard_map/ppermute | solution.py:411
  92.9 16.9 %all-to-all-start.3 = ((bf16[4,128,128]{2,1,0:T(8,128)(2,1)}), bf16[4,128,128]{2,1,0:T(8,128)(2,1)S(1)}, u32[]{:S(2)}, u32[]{:S(2)}) async-start(bf16[4,128,128]{2,1,0:T(8,128)(2,1)} %shard_map.160.refs_0_), calls=%async_computation.3 | async-start | bytes 262144 | tf_op jit(solution)/shard_map/all_to_all | solution.py:392
  106.2 0.9 copy-start.8
  112.6 22.8 %all-to-all-start.4 = ((bf16[32,128,128]{2,1,0:T(8,128)(2,1)}), bf16[32,128,128]{2,1,0:T(8,128)(2,1)S(1)}, u32[]{:S(2)}, u32[]{:S(2)}) async-start(bf16[32,128,128]{2,1,0:T(8,128)(2,1)} %shard_map.163), calls=%async_computation.4 | async-start | bytes 2097152 | tf_op jit(solution)/shard_map/all_to_all | solution.py:392
  119.4 27.3 %collective-permute-start.16 = (bf16[2,2,128,512]{3,2,1,0:T(8,128)(2,1)}, bf16[2,2,128,512]{3,2,1,0:T(8,128)(2,1)S(1)}, u32[]{:S(2)}, u32[]{:S(2)}) collective-permute-start(bf16[2,2,128,512]{3,2,1,0:T(8,128)(2,1)} %get-tuple-element.40), channel_id=1, source_target_pairs={{0,2},{2,0},{1,3},{3,1},{4,6},{6,4},{5,7},{7,5},{8,10},{10,8},{9,1... | collective-permute-start | bytes 1572872 | tf_op jit(solution)/shard_map/ppermute | solution.py:411
  135.4 7.1 %copy-start = (bf16[32,128,128]{2,1,0:T(8,128)(2,1)}, bf16[32,128,128]{2,1,0:T(8,128)(2,1)S(1)}, u32[]{:S(2)}) copy-start(bf16[32,128,128]{2,1,0:T(8,128)(2,1)S(1)} %all-to-all-done.4) | copy-start | bytes 3145732
  136.3 5.2 %collective-permute-start.13 = (bf16[4,256,128]{2,1,0:T(8,128)(2,1)S(1)}, bf16[4,256,128]{2,1,0:T(8,128)(2,1)S(1)}, u32[]{:S(2)}, u32[]{:S(2)}) collective-permute-start(bf16[4,256,128]{2,1,0:T(8,128)(2,1)S(1)} %bitcast.38), channel_id=1, source_target_pairs={{0,1},{1,0},{2,3},{3,2},{4,5},{5,4},{6,7},{7,6},{8,9},{9,8},{10,11... | collective-permute-start | bytes 786440 | tf_op jit(solution)/shard_map/ppermute | solution.py:408
  139.2 2.8 %collective-permute-start.14 = (bf16[4,256,128]{2,1,0:T(8,128)(2,1)S(1)}, bf16[4,256,128]{2,1,0:T(8,128)(2,1)S(1)}, u32[]{:S(2)}, u32[]{:S(2)}) collective-permute-start(bf16[4,256,128]{2,1,0:T(8,128)(2,1)S(1)} %bitcast.37), channel_id=1, source_target_pairs={{0,1},{1,0},{2,3},{3,2},{4,5},{5,4},{6,7},{7,6},{8,9},{9,8},{10,11... | collective-permute-start | bytes 786440 | tf_op jit(solution)/shard_map/ppermute | solution.py:408
  139.2 2.9 %collective-permute-start.12 = (bf16[4,256,128]{2,1,0:T(8,128)(2,1)S(1)}, bf16[4,256,128]{2,1,0:T(8,128)(2,1)S(1)}, u32[]{:S(2)}, u32[]{:S(2)}) collective-permute-start(bf16[4,256,128]{2,1,0:T(8,128)(2,1)S(1)} %bitcast.36), channel_id=1, source_target_pairs={{0,1},{1,0},{2,3},{3,2},{4,5},{5,4},{6,7},{7,6},{8,9},{9,8},{10,11... | collective-permute-start | bytes 786440 | tf_op jit(solution)/shard_map/ppermute | solution.py:408
  139.7 2.8 %collective-permute-start.11 = (bf16[4,256,128]{2,1,0:T(8,128)(2,1)}, bf16[4,256,128]{2,1,0:T(8,128)(2,1)S(1)}, u32[]{:S(2)}, u32[]{:S(2)}) collective-permute-start(bf16[4,256,128]{2,1,0:T(8,128)(2,1)} %bitcast.14), channel_id=1, source_target_pairs={{0,1},{1,0},{2,3},{3,2},{4,5},{5,4},{6,7},{7,6},{8,9},{9,8},{10,11... | collective-permute-start | bytes 786440 | tf_op jit(solution)/shard_map/ppermute | solution.py:408
  141.5 1.0 copy-start.14
  141.5 7.9 %collective-permute-start.7 = (bf16[2,128,512]{2,1,0:T(8,128)(2,1)}, bf16[2,128,512]{2,1,0:T(8,128)(2,1)S(1)}, u32[]{:S(2)}, u32[]{:S(2)}) collective-permute-start(bf16[2,128,512]{2,1,0:T(8,128)(2,1)} %get-tuple-element.31), channel_id=1, source_target_pairs={{0,1},{1,0},{2,3},{3,2},{4,5},{5,4},{6,7},{7,6},{8,9},{9,8},{10,11... | collective-permute-start | bytes 786440 | tf_op jit(solution)/shard_map/ppermute | solution.py:408
  142.0 10.5 %collective-permute-start.15 = (bf16[2,128,512]{2,1,0:T(8,128)(2,1)}, bf16[2,128,512]{2,1,0:T(8,128)(2,1)S(1)}, u32[]{:S(2)}, u32[]{:S(2)}) collective-permute-start(bf16[2,128,512]{2,1,0:T(8,128)(2,1)} %get-tuple-element.39), channel_id=1, source_target_pairs={{0,1},{1,0},{2,3},{3,2},{4,5},{5,4},{6,7},{7,6},{8,9},{9,8},{10,11... | collective-permute-start | bytes 786440 | tf_op jit(solution)/shard_map/ppermute | solution.py:408
  142.1 7.3 %collective-permute-start.9 = (bf16[2,128,512]{2,1,0:T(8,128)(2,1)}, bf16[2,128,512]{2,1,0:T(8,128)(2,1)S(1)}, u32[]{:S(2)}, u32[]{:S(2)}) collective-permute-start(bf16[2,128,512]{2,1,0:T(8,128)(2,1)} %shard_map.161), channel_id=1, source_target_pairs={{0,1},{1,0},{2,3},{3,2},{4,5},{5,4},{6,7},{7,6},{8,9},{9,8},{10,11... | collective-permute-start | bytes 786440 | tf_op jit(solution)/shard_map/ppermute | solution.py:408
  149.2 3.2 %collective-permute-start.17 = (bf16[2,128,512]{2,1,0:T(8,128)(2,1)}, bf16[2,128,512]{2,1,0:T(8,128)(2,1)S(1)}, u32[]{:S(2)}, u32[]{:S(2)}) collective-permute-start(bf16[2,128,512]{2,1,0:T(8,128)(2,1)} %shard_map.166), channel_id=1, source_target_pairs={{0,1},{1,0},{2,3},{3,2},{4,5},{5,4},{6,7},{7,6},{8,9},{9,8},{10,11... | collective-permute-start | bytes 786440 | tf_op jit(solution)/shard_map/ppermute | solution.py:408
  (14 other events, 10.5 us)

commit v3 on v2

--- a/solution.py
+++ b/solution.py
@@ -14,7 +14,6 @@
 T = 128
 HOPS = 3
 HEADS_AT_ONCE = 1
-SWAPS = 4
 G = 4
 BAND = (HOPS + 1) * T
 WIN = HOPS + G
@@ -29,6 +28,10 @@
 NT = (((1,), (1,)), ((), ()))
 TN = (((0,), (0,)), ((), ()))
 SCALAR = pl.BlockSpec(memory_space=pltpu.SMEM)
+
+
+def takes(microseconds):
+    return pl.CostEstimate(flops=0, bytes_accessed=int(microseconds * 3.6e6), transcendentals=0)
 
 
 def dot(a, b, dims=NN):
@@ -66,6 +69,7 @@
     return pl.pallas_call(
         lambda *refs: resum_kernel(scale, *refs),
         in_specs=[pl.BlockSpec(parts.shape)] + [pl.BlockSpec(memory_space=pl.ANY)] * len(after),
+        cost_estimate=takes(1.9),
         out_shape=jax.ShapeDtypeStruct((count,) + parts.shape[1:], parts.dtype),
     )(parts, *after)
 
@@ -86,35 +90,37 @@
     return 2 * [jax.ShapeDtypeStruct(shape, bf16)] + [jax.ShapeDtypeStruct((2,) + shape, bf16)]
 
 
-def pack_kernel(own_ref, k_ref, v_ref, q_ref, g_ref, sig_ref, emb_ref, typ_ref, early_ref, *rest):
-    kv_refs, qg_refs = rest[:3], rest[3:]
-    width = kv_refs[0].shape[1]
-    sig = [sig_ref[j * SIG_ROWS : (j + 1) * SIG_ROWS] for j in range(G)]
-    reach = own_ref[2] + lax.broadcasted_iota(jnp.int32, (1, T), 1) - early_ref[...]
-    lines = (emb_ref[...], typ_ref[...], lax.shift_right_logical(reach, 4), reach & 15)
-    info = jnp.concatenate(list(lines) + [jnp.zeros((12, T), jnp.int32)], axis=0)
-    info = info.astype(f32).astype(bf16)
-    tail = [jnp.concatenate([sig[j], info if j == 0 else jnp.zeros_like(info)], axis=0) for j in range(G)]
-    tail = jnp.concatenate(tail, axis=1)
+def pack_kernel(own_ref, a_ref, b_ref, *refs):
+    extra, outs = refs[:-3], refs[-3:]
+    width = outs[0].shape[1]
+    if extra:
+        sig_ref, emb_ref, typ_ref, early_ref = extra
+        reach = own_ref[2] + lax.broadcasted_iota(jnp.int32, (1, T), 1) - early_ref[...]
+        lines = (emb_ref[...], typ_ref[...], lax.shift_right_logical(reach, 4), reach & 15)
+        info = jnp.concatenate(list(lines) + [jnp.zeros((12, T), jnp.int32)], axis=0)
+        info = info.astype(f32).astype(bf16)
+        tail = []
+        for j in range(G):
+            sig = sig_ref[j * SIG_ROWS : (j + 1) * SIG_ROWS]
+            tail.append(jnp.concatenate([sig, info if j == 0 else jnp.zeros_like(info)], axis=0))
+        tail = jnp.concatenate(tail, axis=1)
     for s in range(G):
         columns = columns_of(own_ref, s, width)
-        kv_ref, qg_ref = piece_at(kv_refs, s), piece_at(qg_refs, s)
-        kv_ref[0:T] = k_ref[:, columns]
-        kv_ref[T : 2 * T] = v_ref[:, columns]
-        kv_ref[2 * T :] = tail
-        qg_ref[0:T] = q_ref[:, columns]
-        qg_ref[T : 2 * T] = g_ref[:, columns]
+        piece = piece_at(outs, s)
+        piece[0:T] = a_ref[:, columns]
+        piece[T : 2 * T] = b_ref[:, columns]
+        if extra:
+            piece[2 * T :] = tail
 
 
 def pack(own, *args):
-    width = args[0].shape[1] // G
-    shapes = pieces_of((PIECE_ROWS, width)) + pieces_of((2 * T, width))
-    out = pl.pallas_call(
+    rows = PIECE_ROWS if len(args) > 2 else 2 * T
+    return pl.pallas_call(
         pack_kernel,
         in_specs=[SCALAR] + [pl.BlockSpec(a.shape) for a in args],
-        out_shape=shapes,
+        cost_estimate=takes(2),
+        out_shape=pieces_of((rows, args[0].shape[1] // G)),
     )(own, *args)
-    return out[:3], out[3:]
 
 
 def line_up_kernel(own_ref, *refs):
@@ -133,6 +139,7 @@
         in_specs=[SCALAR]
         + [pl.BlockSpec(a.shape) for a in pieces]
         + [pl.BlockSpec(memory_space=pl.ANY)] * len(after),
+        cost_estimate=takes(2.4),
         out_shape=jax.ShapeDtypeStruct((HOPS,) + pieces[0].shape, bf16),
     )(own, *pieces, *after)
 
@@ -145,6 +152,7 @@
     return pl.pallas_call(
         second_kernel,
         in_specs=[pl.BlockSpec(pair.shape)] + [pl.BlockSpec(memory_space=pl.ANY)] * len(after),
+        cost_estimate=takes(1.7),
         out_shape=jax.ShapeDtypeStruct(pair.shape[1:], pair.dtype),
     )(pair, *after)
 
@@ -166,6 +174,7 @@
         in_specs=[SCALAR]
         + [pl.BlockSpec(a.shape) for a in pieces]
         + [pl.BlockSpec(memory_space=pl.ANY)] * len(after),
+        cost_estimate=takes(2.2),
         out_shape=[shape, shape],
     )(own, *pieces, *after)
 
@@ -189,8 +198,19 @@
     return pl.pallas_call(
         add_kernel,
         in_specs=[SCALAR, pl.BlockSpec(mine.shape), pl.BlockSpec(back.shape)],
+        cost_estimate=takes(2.7),
         out_shape=pieces_of((2, T, mine.shape[3])),
     )(own, mine, back)
+
+
+def once(value, after):
+    return pl.pallas_call(
+        lambda *refs: None,
+        in_specs=[pl.BlockSpec(memory_space=pl.ANY)] * (1 + len(after)),
+        out_specs=pl.BlockSpec(memory_space=pl.ANY),
+        out_shape=jax.ShapeDtypeStruct(value.shape, value.dtype),
+        input_output_aliases={0: 0},
+    )(value, *after)
 
 
 def spread_kernel(heads, place_ref, *refs):
@@ -209,7 +229,9 @@
 def spread(place, mine, others, heads):
     return pl.pallas_call(
         lambda *refs: spread_kernel(heads, *refs),
-        in_specs=[SCALAR] + [pl.BlockSpec(a.shape) for a in (mine, *others)],
+        in_specs=[SCALAR]
+        + [pl.BlockSpec(a.shape) for a in (mine, *others)],
+        cost_estimate=takes(3.4),
         out_shape=jax.ShapeDtypeStruct((2 * F, 2 * mine.shape[0] * D), bf16),
     )(place, mine, *others)
 
@@ -296,19 +318,26 @@
             piece = got_at(qg_in, s)
             pair_ref[head, block, 0:T, 0:D] = piece[0:T, lanes]
             pair_ref[head, block, T:, D:] = piece[T : 2 * T, lanes]
+        turned = kv_ref[head].T
         for b in range(G):
             band = slice(b * T, b * T + BAND)
             both = kv_ref[head, band]
             pair = pair_ref[head, b]
-            product = dot(both, pair, NT)
-            score, dprobs = product[:, :T] * (scale * LOG2E) + bias_ref[b], product[:, T:]
-            expo = jnp.exp2(score - jnp.max(score, axis=0, keepdims=True))
-            probs = expo * (1.0 / jnp.sum(expo, axis=0, keepdims=True))
-            probs_low = probs.astype(bf16)
-            inner = jnp.sum(probs * dprobs, axis=0, keepdims=True)
-            dscore = (probs * (dprobs - inner)).astype(bf16)
-            a_ref[head, b] = dot(probs_low, both[:, D:], TN).astype(bf16)
-            b_ref[head, b] = (dot(dscore, both[:, :D], TN) * scale).astype(bf16)
+            halves = [slice(i * BAND // 2, (i + 1) * BAND // 2) for i in range(2)]
+            score, dprobs = [], []
+            for half in halves:
+                product = dot(both[half], pair, NT)
+                score.append(product[:, :T] * (scale * LOG2E) + bias_ref[b, half])
+                dprobs.append(product[:, T:])
+            most = jnp.maximum(*(jnp.max(part, axis=0, keepdims=True) for part in score))
+            expo = [jnp.exp2(part - most) for part in score]
+            share = 1.0 / sum(jnp.sum(part, axis=0, keepdims=True) for part in expo)
+            probs = [part * share for part in expo]
+            inner = sum(jnp.sum(p * d, axis=0, keepdims=True) for p, d in zip(probs, dprobs))
+            dscore = jnp.concatenate([(p * (d - inner)).astype(bf16) for p, d in zip(probs, dprobs)], axis=0)
+            probs_low = jnp.concatenate([p.astype(bf16) for p in probs], axis=0)
+            a_ref[head, b] = dot(turned[D:, band], probs_low).astype(bf16).T
+            b_ref[head, b] = (dot(turned[:D, band], dscore) * scale).astype(bf16).T
             grad = dot(jnp.concatenate([dscore, probs_low], axis=1), pair)
             old = slice(b * T, b * T + BAND - T)
             new = slice(b * T + BAND - T, b * T + BAND)
@@ -343,9 +372,10 @@
     rows = pl.BlockSpec((2 * T, lanes), lambda h, own: (0, h))
     third = pl.BlockSpec((1, 2 * T, lanes), lambda h, own: (0, 0, h))
     early = pl.BlockSpec((HOPS, 2 * T, lanes), lambda h, own: (0, 0, h))
-    sig = pl.BlockSpec((T, width), lambda h, own: (2, 0))
-    third_sig = pl.BlockSpec((1, T, width), lambda h, own: (0, 2, 0))
-    early_sig = pl.BlockSpec((HOPS, T, width), lambda h, own: (0, 2, 0))
+    tail = pl.Element(PIECE_ROWS - 2 * T)
+    sig = pl.BlockSpec((tail, pl.Element(width)), lambda h, own: (2 * T, 0))
+    third_sig = pl.BlockSpec((pl.Element(1), tail, pl.Element(width)), lambda h, own: (0, 2 * T, 0))
+    early_sig = pl.BlockSpec((pl.Element(HOPS), tail, pl.Element(width)), lambda h, own: (0, 2 * T, 0))
     got = lambda spec, third: [spec, spec, third, spec]
     grads = lambda n: pl.BlockSpec((2, n, T, lanes), lambda h, own: (0, 0, 0, h))
     per_head = lambda *shape: pltpu.VMEM((HEADS_AT_ONCE,) + shape[:-1], shape[-1])
@@ -381,9 +411,7 @@
         compiler_params=pltpu.CompilerParams(
             dimension_semantics=("arbitrary",), vmem_limit_bytes=56 * 1024 * 1024
         ),
-        cost_estimate=pl.CostEstimate(
-            flops=3_000_000_000, bytes_accessed=12_000_000, transcendentals=1_000_000
-        ),
+        cost_estimate=takes(15),
     )(own, stat, pmean, pvar, pcount, halo, *kv, halo, *kv, *qg, w)
     return out[:3], out[3], out[4], out[5]
 
@@ -414,16 +442,15 @@
         second = second_of(crossed, after) if after else crossed[1]
         return [pieces[0], swap(pieces[1]), crossed, swap(second)]
 
-    kv, qg = pack(
-        place, key_states[0], value_states[0], queries[0], cotangent[0], signal[0],
-        embodiment, token_type, earliest,
-    )
+    kv = pack(place, key_states[0], value_states[0], signal[0], embodiment, token_type, earliest)
+    qg = pack(place, queries[0], cotangent[0])
     kv, qg = regroup(kv, across(kv)), regroup(qg, across(qg))
 
     stat = pl.pallas_call(
         stats_kernel,
         in_specs=[pl.BlockSpec((T, F)), pl.BlockSpec((1, T)), pl.BlockSpec((1, T))]
         + [pl.BlockSpec(memory_space=pl.ANY)],
+        cost_estimate=takes(1.6),
         out_shape=jax.ShapeDtypeStruct((n_zc, STAT_ROWS, T), f32),
     )(signal[0], embodiment, token_type, kv[1])
     stat = exchange(stat, ZC)
@@ -439,7 +466,7 @@
 
     back = lax.ppermute(back, Z, [(z + 1, z) for z in range(n_z - 1)])
     added = add_back(place, mine, back)
-    crossed = across(first)
+    crossed, crossed_g = across(first), across(added)
 
     heads = share // D
     tokens = T * lax.axis_size(("x", "yh") + CTX)
@@ -448,11 +475,12 @@
     dw = resum(exchange(dw, PARTS), lax.axis_size("zh"))
     first = regroup(first, crossed, [dw])
     dw = exchange(dw, ("zh",))
-    dw = resum(dw, lax.axis_size(GATHER), 1.0 / math.sqrt(tokens), after=[added[0], crossed])
+    dw = resum(dw, lax.axis_size(GATHER), 1.0 / math.sqrt(tokens), after=[crossed, crossed_g])
     dw = exchange(dw, GATHER).reshape(n_xy, 2 * F, D)
-    d_weight = spread(place, dw, [swap(part) for part in jnp.split(dw, SWAPS)], heads)
-    attended, d_queries = unpack(place, first, after=[d_weight])
-    d_keys, d_values = unpack(place, regroup(added, across(added), [d_weight]))
+    attended, d_queries = unpack(place, first)
+    d_keys, d_values = unpack(place, regroup(added, crossed_g))
+    dw = once(dw, [attended, d_keys])
+    d_weight = spread(place, dw, [swap(dw)], heads)
     d_weight = d_weight.reshape(2, F, 2 * width)
     return attended[None], d_queries[None], d_keys[None], d_values[None], d_weight
 

time: 157 us -> 153 us (0.975)
  waiting for transfers between devices: 46.4 us -> 39.9 us
  starting transfers between devices: 50.8 us -> 53.1 us
    all_to_all x5, waiting for transfers between devices: 33.3 us -> 20.8 us  [exchange(): return lax.all_to_all(value, axes, 0, 0)]
    ppermute x12 -> x9, starting transfers between devices: 8.06 us -> 11.8 us  [swap(): return lax.ppermute(value, 'c', [(0, 1), (1, 0)])]
    ppermute x12 -> x9, waiting for transfers between devices: 1.47 us -> 5.07 us  [swap(): return lax.ppermute(value, 'c', [(0, 1), (1, 0)])]
    pallas_call x2 -> x1, Pallas kernels: 3.52 us -> 1.76 us  [second_of(): pl.pallas_call(second_kernel, in_specs=[pl.BlockSpec(pair.shape)] + [pl.B...]
    ppermute x1, waiting for transfers between devices: 9.4 us -> 11 us  [on_device(): back = lax.ppermute(back, Z, [(z + 1, z) for z in range(n_z - 1)])]
    pallas_call x1 -> x2, Pallas kernels: 3.09 us -> 4.61 us  [pack(): pl.pallas_call(pack_kernel, in_specs=[SCALAR] + [pl.BlockSpec(a.shape) fo...]
    unnamed x47 -> x45, local copies, waits for them, and re-layouts: 9.38 us -> 10.8 us
  transfers between devices with their start and end apart: 23 -> 20, of which waited for: 7 -> 9; matrix products, arithmetic and copies ran while one was open for 5% -> 4% of each run, Pallas kernels for 13% -> 12%
where the time goes in v3:
time: 153 us; the launch traced here: 152 us
  starting transfers between devices  53.1 us (35%)
  Pallas kernels  41 us (27%)
  waiting for transfers between devices  39.9 us (26%)
  local copies, waits for them, and re-layouts  16.7 us (11%)
    all_to_all x5, starting transfers between devices, exchange(): return lax.all_to_all(value, axes, 0, 0)  34.8 us
    all_to_all x5, waiting for transfers between devices, exchange(): return lax.all_to_all(value, axes, 0, 0)  20.8 us
    pallas_call x1, Pallas kernels, main_call(): pl.pallas_call(main_kernel, grid_spec=pltpu.PrefetchScalarGridSpec(num_sc...  14.3 us
    ppermute x9, starting transfers between devices, swap(): return lax.ppermute(value, 'c', [(0, 1), (1, 0)])  11.8 us
    ppermute x1, waiting for transfers between devices, on_device(): back = lax.ppermute(back, Z, [(z + 1, z) for z in range(n_z - 1)])  11 us
    unnamed x45, local copies, waits for them, and re-layouts  10.8 us
    pallas_call x3, Pallas kernels, resum(): pl.pallas_call(lambda *refs: resum_kernel(scale, *refs), in_specs=[pl.Blo...  5.5 us
    ppermute x9, waiting for transfers between devices, swap(): return lax.ppermute(value, 'c', [(0, 1), (1, 0)])  5.07 us
  transfers between devices with their start and end apart: 20, of which 9 were waited for; matrix products, arithmetic and copies ran while one was open for 4% of the time, Pallas kernels for 12%

profile of v3, /device:TPU:1, one launch (start us, length us, event | category | flops | bytes accessed | tf_op | source)
XLA Modules:
  0.0 152.2 jit_solution(5621481882150186608)
XLA Ops:
  1.2 2.3 %shard_map.155 = (bf16[304,512]{1,0:T(8,128)(2,1)}, bf16[304,512]{1,0:T(8,128)(2,1)}, bf16[2,304,512]{2,1,0:T(8,128)(2,1)}) custom-call(s32[3]{0:T(128)} %pad_add_fusion.own_ref.refs_0_, bf16[128,2048]{1,0:T(8,128)(2,1)} %bitcast.29, bf16[128,2048]{1,0:T(8,128)(2,1)} %bitcast.30, bf16[128,128]{1,0:T(8,128)(2,1)} %bitcast.36, s32[1,128]{1,0:T(1,128)} %emb_ref.1, ...), custom_call_target="tpu_custom_call" | custom-call | bytes 7200000 | tf_op jit(solution)/shard_map/pallas_call | solution.py:118
  3.6 2.1 %collective-permute-start.2 = (bf16[2,304,512]{2,1,0:T(8,128)(2,1)}, bf16[2,304,512]{2,1,0:T(8,128)(2,1)S(1)}, u32[]{:S(2)}, u32[]{:S(2)}) collective-permute-start(bf16[2,304,512]{2,1,0:T(8,128)(2,1)} %get-tuple-element.27), channel_id=1, source_target_pairs={{0,2},{2,0},{1,3},{3,1},{4,6},{6,4},{5,7},{7,5},{8,10},{10,8},{9,1... | collective-permute-start | bytes 1867784 | tf_op jit(solution)/shard_map/ppermute | solution.py:439
  9.0 1.7 %shard_map.156 = f32[16,40,128]{2,1,0:T(8,128)} custom-call(bf16[128,128]{1,0:T(8,128)(2,1)} %bitcast.37, s32[1,128]{1,0:T(1,128)} %emb_ref.1, s32[1,128]{1,0:T(1,128)} %typ_ref.1, bf16[304,512]{1,0:T(8,128)(2,1)} %copy-done.2), custom_call_target="tpu_custom_call" | custom-call | bytes 5760000 | tf_op jit(solution)/shard_map/pallas_call | solution.py:449
  10.7 8.7 %all-to-all-start = ((f32[16,40,128]{2,1,0:T(8,128)}), f32[16,40,128]{2,1,0:T(8,128)S(1)}, u32[]{:S(2)}, u32[]{:S(2)}) async-start(f32[16,40,128]{2,1,0:T(8,128)} %shard_map.156), calls=%async_computation | async-start | bytes 655360 | tf_op jit(solution)/shard_map/all_to_all | solution.py:420
  19.4 1.6 %collective-permute-start.3 = (bf16[304,512]{1,0:T(8,128)(2,1)S(1)}, bf16[304,512]{1,0:T(8,128)(2,1)S(1)}, u32[]{:S(2)}, u32[]{:S(2)}) collective-permute-start(bf16[304,512]{1,0:T(8,128)(2,1)S(1)} %slice_bitcast_fusion), channel_id=1, source_target_pairs={{0,1},{1,0},{2,3},{3,2},{4,5},{5,4},{6,7},{7,6},{8,9},{9,8},{10,11... | collective-permute-start | bytes 933896 | tf_op jit(solution)/shard_map/ppermute | solution.py:436
  21.0 2.3 %shard_map.157 = (bf16[256,512]{1,0:T(8,128)(2,1)}, bf16[256,512]{1,0:T(8,128)(2,1)}, bf16[2,256,512]{2,1,0:T(8,128)(2,1)}) custom-call(s32[3]{0:T(128)} %pad_add_fusion.own_ref.refs_0_, bf16[128,2048]{1,0:T(8,128)(2,1)} %bitcast.32, bf16[128,2048]{1,0:T(8,128)(2,1)} %bitcast.33), custom_call_target="tpu_custom_call" | custom-call | bytes 7200000 | tf_op jit(solution)/shard_map/pallas_call | solution.py:118
  23.3 1.5 collective-permute-start.1
  24.7 7.7 %all-to-all-done.refs_0_.refs_4_ = f32[16,40,128]{2,1,0:T(8,128)S(1)} async-done(((f32[16,40,128]{2,1,0:T(8,128)}), f32[16,40,128]{2,1,0:T(8,128)S(1)}, u32[]{:S(2)}, u32[]{:S(2)}) %all-to-all-start) | async-done | bytes 327712 | tf_op jit(solution)/shard_map/all_to_all | solution.py:420
  33.3 2.4 %shard_map.159 = bf16[3,304,512]{2,1,0:T(8,128)(2,1)} custom-call(s32[3]{0:T(128)} %pad_add_fusion.own_ref.refs_0_, bf16[304,512]{1,0:T(8,128)(2,1)} %get-tuple-element.26.refs_0_.refs_1_.refs_6_, bf16[304,512]{1,0:T(8,128)(2,1)} %copy-done.2, bf16[2,304,512]{2,1,0:T(8,128)(2,1)} %copy-done.1, bf16[304,512]{1,0:T(8,128)(2,1)} %copy-done.9, ...), custom_call_target="tpu_custom_call" | custom-call | bytes 8640000 | tf_op jit(solution)/shard_map/pallas_call | solution.py:137
  38.1 1.7 %shard_map.158 = f32[16,40,128]{2,1,0:T(8,128)} custom-call(f32[16,40,128]{2,1,0:T(8,128)} %copy-done.8, bf16[2,256,512]{2,1,0:T(8,128)(2,1)} %copy-done.7), custom_call_target="tpu_custom_call" | custom-call | bytes 6840000 | tf_op jit(solution)/shard_map/pallas_call | solution.py:69
  39.9 6.5 %all-to-all-start.1 = ((f32[16,40,128]{2,1,0:T(8,128)}), f32[16,40,128]{2,1,0:T(8,128)S(1)}, u32[]{:S(2)}, u32[]{:S(2)}) async-start(f32[16,40,128]{2,1,0:T(8,128)} %shard_map.158), calls=%async_computation.1 | async-start | bytes 655360 | tf_op jit(solution)/shard_map/all_to_all | solution.py:420
  46.3 1.7 %slice_bitcast_fusion.2 = bf16[256,512]{1,0:T(8,128)(2,1)} fusion(bf16[2,256,512]{2,1,0:T(8,128)(2,1)} %copy-done.7), kind=kLoop, calls=%fused_computation.3 | loop fusion | bytes 524288 | tf_op jit(solution)/shard_map/squeeze | solution.py:442
  49.2 3.3 %reshape_reshape.3 = bf16[256,2,2048]{2,1,0:T(2,128)(2,1)S(1)} reshape(bf16[2,128,4096]{2,1,0:T(8,128)(2,1)} %param.17) | data formatting | bytes 4194304 | tf_op jit(solution)/shard_map/reshape;reshape | solution.py:461
  54.4 3.0 %collective-permute-done.4.refs_0_.refs_5_ = bf16[3,304,512]{2,1,0:T(8,128)(2,1)S(1)} collective-permute-done((bf16[3,304,512]{2,1,0:T(8,128)(2,1)}, bf16[3,304,512]{2,1,0:T(8,128)(2,1)S(1)}, u32[]{:S(2)}, u32[]{:S(2)}) %collective-permute-start.4) | collective-permute-done | bytes 933920 | tf_op jit(solution)/shard_map/ppermute | solution.py:457
  58.3 14.3 %shard_map.160 = (bf16[2,128,512]{2,1,0:T(8,128)(2,1)}, bf16[2,128,512]{2,1,0:T(8,128)(2,1)}, bf16[2,2,128,512]{3,2,1,0:T(8,128)(2,1)}, bf16[2,3,128,512]{3,2,1,...) custom-call(s32[3]{0:T(128)} %pad_add_fusion.own_ref.refs_0_, ...), custom_call_target="tpu_custom_call" | custom-call | bytes 54000000 | tf_op jit(solution)/shard_map/pallas_call | solution.py:382
  73.9 8.9 %all-to-all-start.2 = ((bf16[16,128,128]{2,1,0:T(8,128)(2,1)}), bf16[16,128,128]{2,1,0:T(8,128)(2,1)S(1)}, u32[]{:S(2)}, u32[]{:S(2)}) async-start(bf16[16,128,128]{2,1,0:T(8,128)(2,1)} %bitcast.31), calls=%async_computation.2 | async-start | bytes 1048576 | tf_op jit(solution)/shard_map/all_to_all | solution.py:420
  82.9 11.0 %collective-permute-done.10.back_ref = bf16[2,3,128,512]{3,2,1,0:T(8,128)(2,1)S(1)} collective-permute-done((bf16[2,3,128,512]{3,2,1,0:T(8,128)(2,1)}, bf16[2,3,128,512]{3,2,1,0:T(8,128)(2,1)S(1)}, u32[]{:S(2)}, u32[]{:S(2)}) %collective-permute-start.10) | collective-permute-done | bytes 786464 | tf_op jit(solution)/shard_map/ppermute | solution.py:467
  94.9 2.7 %shard_map.164 = (bf16[2,128,512]{2,1,0:T(8,128)(2,1)}, bf16[2,128,512]{2,1,0:T(8,128)(2,1)}, bf16[2,2,128,512]{3,2,1,0:T(8,128)(2,1)}) custom-call(s32[3]{0:T(128)} %pad_add_fusion.own_ref.refs_0_, bf16[2,4,128,512]{3,2,1,0:T(8,128)(2,1)} %get-tuple-element.36.mine_ref, bf16[2,3,128,512]{3,2,1,0:T(8,128)(2,1)} %copy-done.13), custom_call_target="tpu_custom_call" | custom-call | bytes 9720000 | tf_op jit(solution)/shard_map/pallas_call | solution.py:198
  97.7 3.6 %all-to-all-done.2.refs_0_ = bf16[16,128,128]{2,1,0:T(8,128)(2,1)S(1)} async-done(((bf16[16,128,128]{2,1,0:T(8,128)(2,1)}), bf16[16,128,128]{2,1,0:T(8,128)(2,1)S(1)}, u32[]{:S(2)}, u32[]{:S(2)}) %all-to-all-start.2) | async-done | bytes 524320 | tf_op jit(solution)/shard_map/all_to_all | solution.py:420
  102.1 1.8 %shard_map.161.refs_0_ = bf16[4,128,128]{2,1,0:T(8,128)(2,1)} custom-call(bf16[16,128,128]{2,1,0:T(8,128)(2,1)} %copy-done.10), custom_call_target="tpu_custom_call" | custom-call | bytes 6840000 | tf_op jit(solution)/shard_map/pallas_call | solution.py:69
  103.9 4.4 %all-to-all-start.3 = ((bf16[4,128,128]{2,1,0:T(8,128)(2,1)}), bf16[4,128,128]{2,1,0:T(8,128)(2,1)S(1)}, u32[]{:S(2)}, u32[]{:S(2)}) async-start(bf16[4,128,128]{2,1,0:T(8,128)(2,1)} %shard_map.161.refs_0_), calls=%async_computation.3 | async-start | bytes 262144 | tf_op jit(solution)/shard_map/all_to_all | solution.py:420
  108.3 7.3 %all-to-all-done.3.refs_0_ = bf16[4,128,128]{2,1,0:T(8,128)(2,1)S(1)} async-done(((bf16[4,128,128]{2,1,0:T(8,128)(2,1)}), bf16[4,128,128]{2,1,0:T(8,128)(2,1)S(1)}, u32[]{:S(2)}, u32[]{:S(2)}) %all-to-all-start.3) | async-done | bytes 131104 | tf_op jit(solution)/shard_map/all_to_all | solution.py:420
  117.0 2.0 %shard_map.166 = bf16[32,128,128]{2,1,0:T(8,128)(2,1)} custom-call(bf16[4,128,128]{2,1,0:T(8,128)(2,1)} %copy-done.14, bf16[2,2,128,512]{3,2,1,0:T(8,128)(2,1)} %copy-done.3, bf16[2,2,128,512]{3,2,1,0:T(8,128)(2,1)} %copy-done.5), custom_call_target="tpu_custom_call" | custom-call | bytes 6840000 | tf_op jit(solution)/shard_map/pallas_call | solution.py:69
  119.0 6.4 %all-to-all-start.4 = ((bf16[32,128,128]{2,1,0:T(8,128)(2,1)}), bf16[32,128,128]{2,1,0:T(8,128)(2,1)S(1)}, u32[]{:S(2)}, u32[]{:S(2)}) async-start(bf16[32,128,128]{2,1,0:T(8,128)(2,1)} %shard_map.166), calls=%async_computation.4 | async-start | bytes 2097152 | tf_op jit(solution)/shard_map/all_to_all | solution.py:420
  125.4 3.9 %collective-permute-start.7 = (bf16[2,128,512]{2,1,0:T(8,128)(2,1)S(1)}, bf16[2,128,512]{2,1,0:T(8,128)(2,1)S(1)}, u32[]{:S(2)}, u32[]{:S(2)}) collective-permute-start(bf16[2,128,512]{2,1,0:T(8,128)(2,1)S(1)} %copy-done.19), channel_id=1, source_target_pairs={{0,1},{1,0},{2,3},{3,2},{4,5},{5,4},{6,7},{7,6},{8,9},{9,8},{10,11... | collective-permute-start | bytes 786440 | tf_op jit(solution)/shard_map/ppermute | solution.py:436
  129.6 1.8 %shard_map.162 = bf16[2,128,512]{2,1,0:T(8,128)(2,1)} custom-call(bf16[2,2,128,512]{3,2,1,0:T(8,128)(2,1)} %copy-done.3, bf16[4,128,128]{2,1,0:T(8,128)(2,1)} %shard_map.161.refs_0_), custom_call_target="tpu_custom_call" | custom-call | bytes 6120000 | tf_op jit(solution)/shard_map/pallas_call | solution.py:152
  133.8 2.3 %shard_map.163 = (bf16[128,2048]{1,0:T(8,128)(2,1)}, bf16[128,2048]{1,0:T(8,128)(2,1)}) custom-call(s32[3]{0:T(128)} %pad_add_fusion.own_ref.refs_0_, bf16[2,128,512]{2,1,0:T(8,128)(2,1)} %get-tuple-element.30.refs_0_, bf16[2,128,512]{2,1,0:T(8,128)(2,1)} %copy-done.17, bf16[2,2,128,512]{3,2,1,0:T(8,128)(2,1)} %copy-done.3, bf16[2,128,512]{2,1,0:T(8,128)(2,1)} %copy-done.18), custom_call_target="tpu_custom_call" | custom-call | bytes 7920000 | tf_op jit(solution)/shard_map/pallas_call | solution.py:172
  136.9 2.3 %shard_map.165 = (bf16[128,2048]{1,0:T(8,128)(2,1)}, bf16[128,2048]{1,0:T(8,128)(2,1)}) custom-call(s32[3]{0:T(128)} %pad_add_fusion.own_ref.refs_0_, bf16[2,128,512]{2,1,0:T(8,128)(2,1)} %get-tuple-element.38.refs_0_, bf16[2,128,512]{2,1,0:T(8,128)(2,1)} %copy-done.15, bf16[2,2,128,512]{3,2,1,0:T(8,128)(2,1)} %copy-done.5, bf16[2,128,512]{2,1,0:T(8,128)(2,1)} %copy-done.16), custom_call_target="tpu_custom_call" | custom-call | bytes 7920000 | tf_op jit(solution)/shard_map/pallas_call | solution.py:172
  139.2 2.3 %all-to-all-done.4 = bf16[32,128,128]{2,1,0:T(8,128)(2,1)S(1)} async-done(((bf16[32,128,128]{2,1,0:T(8,128)(2,1)}), bf16[32,128,128]{2,1,0:T(8,128)(2,1)S(1)}, u32[]{:S(2)}, u32[]{:S(2)}) %all-to-all-start.4) | async-done | bytes 1048608 | tf_op jit(solution)/shard_map/all_to_all | solution.py:420
  142.5 2.7 %collective-permute-start.14 = (bf16[16,256,128]{2,1,0:T(8,128)(2,1)}, bf16[16,256,128]{2,1,0:T(8,128)(2,1)S(1)}, u32[]{:S(2)}, u32[]{:S(2)}) collective-permute-start(bf16[16,256,128]{2,1,0:T(8,128)(2,1)} %shard_map.167.refs_1_), channel_id=1, source_target_pairs={{0,1},{1,0},{2,3},{3,2},{4,5},{5,4},{6,7},{7,6},{8,9},{9,8},{10,11... | collective-permute-start | bytes 3145736 | tf_op jit(solution)/shard_map/ppermute | solution.py:436
  145.2 2.5 %collective-permute-done.14.refs_2_ = bf16[16,256,128]{2,1,0:T(8,128)(2,1)S(1)} collective-permute-done((bf16[16,256,128]{2,1,0:T(8,128)(2,1)}, bf16[16,256,128]{2,1,0:T(8,128)(2,1)S(1)}, u32[]{:S(2)}, u32[]{:S(2)}) %collective-permute-start.14) | collective-permute-done | bytes 1048608 | tf_op jit(solution)/shard_map/ppermute | solution.py:436
  148.7 3.5 %shard_map.168 = bf16[256,4096]{1,0:T(8,128)(2,1)} custom-call(s32[3]{0:T(128)} %pad_add_fusion.own_ref.refs_0_, bf16[16,256,128]{2,1,0:T(8,128)(2,1)} %shard_map.167.refs_1_, bf16[16,256,128]{2,1,0:T(8,128)(2,1)} %copy-done.12), custom_call_target="tpu_custom_call" | custom-call | bytes 12240000 | tf_op jit(solution)/shard_map/pallas_call | solution.py:230
  (74 shorter events, 21.4 us)
Async XLA Ops:
  3.6 15.8 %collective-permute-start.2 = (bf16[2,304,512]{2,1,0:T(8,128)(2,1)}, bf16[2,304,512]{2,1,0:T(8,128)(2,1)S(1)}, u32[]{:S(2)}, u32[]{:S(2)}) collective-permute-start(bf16[2,304,512]{2,1,0:T(8,128)(2,1)} %get-tuple-element.27), channel_id=1, source_target_pairs={{0,2},{2,0},{1,3},{3,1},{4,6},{6,4},{5,7},{7,5},{8,10},{10,8},{9,1... | collective-permute-start | bytes 1867784 | tf_op jit(solution)/shard_map/ppermute | solution.py:439
  5.7 2.6 %collective-permute-start = (bf16[304,512]{1,0:T(8,128)(2,1)}, bf16[304,512]{1,0:T(8,128)(2,1)S(1)}, u32[]{:S(2)}, u32[]{:S(2)}) collective-permute-start(bf16[304,512]{1,0:T(8,128)(2,1)} %get-tuple-element.24), channel_id=1, source_target_pairs={{0,1},{1,0},{2,3},{3,2},{4,5},{5,4},{6,7},{7,6},{8,9},{9,8},{10,11... | collective-permute-start | bytes 933896 | tf_op jit(solution)/shard_map/ppermute | solution.py:436
  10.7 21.8 %all-to-all-start = ((f32[16,40,128]{2,1,0:T(8,128)}), f32[16,40,128]{2,1,0:T(8,128)S(1)}, u32[]{:S(2)}, u32[]{:S(2)}) async-start(f32[16,40,128]{2,1,0:T(8,128)} %shard_map.156), calls=%async_computation | async-start | bytes 655360 | tf_op jit(solution)/shard_map/all_to_all | solution.py:420
  19.4 13.1 %copy-start.1 = (bf16[2,304,512]{2,1,0:T(8,128)(2,1)}, bf16[2,304,512]{2,1,0:T(8,128)(2,1)S(1)}, u32[]{:S(2)}) copy-start(bf16[2,304,512]{2,1,0:T(8,128)(2,1)S(1)} %collective-permute-done.2.refs_2_.refs_3_.refs_8_) | copy-start | bytes 1867780
  19.4 13.0 %collective-permute-start.3 = (bf16[304,512]{1,0:T(8,128)(2,1)S(1)}, bf16[304,512]{1,0:T(8,128)(2,1)S(1)}, u32[]{:S(2)}, u32[]{:S(2)}) collective-permute-start(bf16[304,512]{1,0:T(8,128)(2,1)S(1)} %slice_bitcast_fusion), channel_id=1, source_target_pairs={{0,1},{1,0},{2,3},{3,2},{4,5},{5,4},{6,7},{7,6},{8,9},{9,8},{10,11... | collective-permute-start | bytes 933896 | tf_op jit(solution)/shard_map/ppermute | solution.py:436
  23.3 14.1 %collective-permute-start.1 = (bf16[2,256,512]{2,1,0:T(8,128)(2,1)}, bf16[2,256,512]{2,1,0:T(8,128)(2,1)S(1)}, u32[]{:S(2)}, u32[]{:S(2)}) collective-permute-start(bf16[2,256,512]{2,1,0:T(8,128)(2,1)} %get-tuple-element.25), channel_id=1, source_target_pairs={{0,2},{2,0},{1,3},{3,1},{4,6},{6,4},{5,7},{7,5},{8,10},{10,8},{9,1... | collective-permute-start | bytes 1572872 | tf_op jit(solution)/shard_map/ppermute | solution.py:439
  35.6 21.7 %collective-permute-start.4 = (bf16[3,304,512]{2,1,0:T(8,128)(2,1)}, bf16[3,304,512]{2,1,0:T(8,128)(2,1)S(1)}, u32[]{:S(2)}, u32[]{:S(2)}) collective-permute-start(bf16[3,304,512]{2,1,0:T(8,128)(2,1)} %shard_map.159), channel_id=1, source_target_pairs={{0,4},{4,8},{8,12},{12,16},{16,20},{20,24},{24,28},{1,5},{5,9},{9,... | collective-permute-start | bytes 2801672 | tf_op jit(solution)/shard_map/ppermute | solution.py:457
  37.0 17.4 %collective-permute-start.5 = (bf16[256,512]{1,0:T(8,128)(2,1)}, bf16[256,512]{1,0:T(8,128)(2,1)}, u32[]{:S(2)}, u32[]{:S(2)}) collective-permute-start(bf16[256,512]{1,0:T(8,128)(2,1)} %get-tuple-element.29), channel_id=1, source_target_pairs={{0,1},{1,0},{2,3},{3,2},{4,5},{5,4},{6,7},{7,6},{8,9},{9,8},{10,11... | collective-permute-start | bytes 786440 | tf_op jit(solution)/shard_map/ppermute | solution.py:436
  39.9 14.5 %all-to-all-start.1 = ((f32[16,40,128]{2,1,0:T(8,128)}), f32[16,40,128]{2,1,0:T(8,128)S(1)}, u32[]{:S(2)}, u32[]{:S(2)}) async-start(f32[16,40,128]{2,1,0:T(8,128)} %shard_map.158), calls=%async_computation.1 | async-start | bytes 655360 | tf_op jit(solution)/shard_map/all_to_all | solution.py:420
  48.0 6.3 %collective-permute-start.6 = (bf16[256,512]{1,0:T(8,128)(2,1)}, bf16[256,512]{1,0:T(8,128)(2,1)}, u32[]{:S(2)}, u32[]{:S(2)}) collective-permute-start(bf16[256,512]{1,0:T(8,128)(2,1)} %slice_bitcast_fusion.2), channel_id=1, source_target_pairs={{0,1},{1,0},{2,3},{3,2},{4,5},{5,4},{6,7},{7,6},{8,9},{9,8},{10,11... | collective-permute-start | bytes 786440 | tf_op jit(solution)/shard_map/ppermute | solution.py:436
  52.5 1.2 copy-start.21
  54.4 3.0 %copy-start.11 = (f32[16,40,128]{2,1,0:T(8,128)}, f32[16,40,128]{2,1,0:T(8,128)S(1)}, u32[]{:S(2)}) copy-start(f32[16,40,128]{2,1,0:T(8,128)S(1)} %all-to-all-done.1.stat_ref) | copy-start | bytes 983044
  57.3 1.0 copy-start.4
  72.6 21.3 %collective-permute-start.10 = (bf16[2,3,128,512]{3,2,1,0:T(8,128)(2,1)}, bf16[2,3,128,512]{3,2,1,0:T(8,128)(2,1)S(1)}, u32[]{:S(2)}, u32[]{:S(2)}) collective-permute-start(bf16[2,3,128,512]{3,2,1,0:T(8,128)(2,1)} %get-tuple-element.37), channel_id=1, source_target_pairs={{4,0},{8,4},{12,8},{16,12},{20,16},{24,20},{28,24},{5,1},{9,5},{13... | collective-permute-start | bytes 2359304 | tf_op jit(solution)/shard_map/ppermute | solution.py:467
  73.9 27.4 %all-to-all-start.2 = ((bf16[16,128,128]{2,1,0:T(8,128)(2,1)}), bf16[16,128,128]{2,1,0:T(8,128)(2,1)S(1)}, u32[]{:S(2)}, u32[]{:S(2)}) async-start(bf16[16,128,128]{2,1,0:T(8,128)(2,1)} %bitcast.31), calls=%async_computation.2 | async-start | bytes 1048576 | tf_op jit(solution)/shard_map/all_to_all | solution.py:420
  82.8 25.5 %collective-permute-start.8 = (bf16[2,2,128,512]{3,2,1,0:T(8,128)(2,1)}, bf16[2,2,128,512]{3,2,1,0:T(8,128)(2,1)S(1)}, u32[]{:S(2)}, u32[]{:S(2)}) collective-permute-start(bf16[2,2,128,512]{3,2,1,0:T(8,128)(2,1)} %get-tuple-element.32), channel_id=1, source_target_pairs={{0,2},{2,0},{1,3},{3,1},{4,6},{6,4},{5,7},{7,5},{8,10},{10,8},{9,1... | collective-permute-start | bytes 1572872 | tf_op jit(solution)/shard_map/ppermute | solution.py:439
  94.0 0.9 copy-start.13
  97.6 18.0 %collective-permute-start.12 = (bf16[2,2,128,512]{3,2,1,0:T(8,128)(2,1)}, bf16[2,2,128,512]{3,2,1,0:T(8,128)(2,1)S(1)}, u32[]{:S(2)}, u32[]{:S(2)}) collective-permute-start(bf16[2,2,128,512]{3,2,1,0:T(8,128)(2,1)} %get-tuple-element.40), channel_id=1, source_target_pairs={{0,2},{2,0},{1,3},{3,1},{4,6},{6,4},{5,7},{7,5},{8,10},{10,8},{9,1... | collective-permute-start | bytes 1572872 | tf_op jit(solution)/shard_map/ppermute | solution.py:439
  103.9 11.7 %all-to-all-start.3 = ((bf16[4,128,128]{2,1,0:T(8,128)(2,1)}), bf16[4,128,128]{2,1,0:T(8,128)(2,1)S(1)}, u32[]{:S(2)}, u32[]{:S(2)}) async-start(bf16[4,128,128]{2,1,0:T(8,128)(2,1)} %shard_map.161.refs_0_), calls=%async_computation.3 | async-start | bytes 262144 | tf_op jit(solution)/shard_map/all_to_all | solution.py:420
  108.3 17.1 %copy-start.19 = (bf16[2,128,512]{2,1,0:T(8,128)(2,1)S(1)}, bf16[2,128,512]{2,1,0:T(8,128)(2,1)}, u32[]{:S(2)}) copy-start(bf16[2,128,512]{2,1,0:T(8,128)(2,1)} %get-tuple-element.31) | copy-start | bytes 786436
  108.3 21.0 %copy-start.20 = (bf16[2,128,512]{2,1,0:T(8,128)(2,1)S(1)}, bf16[2,128,512]{2,1,0:T(8,128)(2,1)}, u32[]{:S(2)}) copy-start(bf16[2,128,512]{2,1,0:T(8,128)(2,1)} %get-tuple-element.39) | copy-start | bytes 786436
  108.3 7.3 %copy-start.3 = (bf16[2,2,128,512]{3,2,1,0:T(8,128)(2,1)}, bf16[2,2,128,512]{3,2,1,0:T(8,128)(2,1)S(1)}, u32[]{:S(2)}) copy-start(bf16[2,2,128,512]{3,2,1,0:T(8,128)(2,1)S(1)} %collective-permute-done.8.in_ref.refs_2_.refs_1_) | copy-start | bytes 1572868
  119.0 12.6 %copy-start.6 = (bf16[2,2,128,512]{3,2,1,0:T(8,128)(2,1)S(1)}, bf16[2,2,128,512]{3,2,1,0:T(8,128)(2,1)}, u32[]{:S(2)}) copy-start(bf16[2,2,128,512]{3,2,1,0:T(8,128)(2,1)} %copy-done.5) | copy-start | bytes 1572868
  119.0 22.5 %all-to-all-start.4 = ((bf16[32,128,128]{2,1,0:T(8,128)(2,1)}), bf16[32,128,128]{2,1,0:T(8,128)(2,1)S(1)}, u32[]{:S(2)}, u32[]{:S(2)}) async-start(bf16[32,128,128]{2,1,0:T(8,128)(2,1)} %shard_map.166), calls=%async_computation.4 | async-start | bytes 2097152 | tf_op jit(solution)/shard_map/all_to_all | solution.py:420
  125.4 6.6 %collective-permute-start.7 = (bf16[2,128,512]{2,1,0:T(8,128)(2,1)S(1)}, bf16[2,128,512]{2,1,0:T(8,128)(2,1)S(1)}, u32[]{:S(2)}, u32[]{:S(2)}) collective-permute-start(bf16[2,128,512]{2,1,0:T(8,128)(2,1)S(1)} %copy-done.19), channel_id=1, source_target_pairs={{0,1},{1,0},{2,3},{3,2},{4,5},{5,4},{6,7},{7,6},{8,9},{9,8},{10,11... | collective-permute-start | bytes 786440 | tf_op jit(solution)/shard_map/ppermute | solution.py:436
  129.3 6.8 %collective-permute-start.11 = (bf16[2,128,512]{2,1,0:T(8,128)(2,1)S(1)}, bf16[2,128,512]{2,1,0:T(8,128)(2,1)S(1)}, u32[]{:S(2)}, u32[]{:S(2)}) collective-permute-start(bf16[2,128,512]{2,1,0:T(8,128)(2,1)S(1)} %copy-done.20), channel_id=1, source_target_pairs={{0,1},{1,0},{2,3},{3,2},{4,5},{5,4},{6,7},{7,6},{8,9},{9,8},{10,11... | collective-permute-start | bytes 786440 | tf_op jit(solution)/shard_map/ppermute | solution.py:436
  131.4 1.7 %collective-permute-start.9 = (bf16[2,128,512]{2,1,0:T(8,128)(2,1)}, bf16[2,128,512]{2,1,0:T(8,128)(2,1)S(1)}, u32[]{:S(2)}, u32[]{:S(2)}) collective-permute-start(bf16[2,128,512]{2,1,0:T(8,128)(2,1)} %shard_map.162), channel_id=1, source_target_pairs={{0,1},{1,0},{2,3},{3,2},{4,5},{5,4},{6,7},{7,6},{8,9},{9,8},{10,11... | collective-permute-start | bytes 786440 | tf_op jit(solution)/shard_map/ppermute | solution.py:436
  131.6 4.5 %collective-permute-start.13 = (bf16[2,128,512]{2,1,0:T(8,128)(2,1)S(1)}, bf16[2,128,512]{2,1,0:T(8,128)(2,1)S(1)}, u32[]{:S(2)}, u32[]{:S(2)}) collective-permute-start(bf16[2,128,512]{2,1,0:T(8,128)(2,1)S(1)} %slice_bitcast_fusion.1), channel_id=1, source_target_pairs={{0,1},{1,0},{2,3},{3,2},{4,5},{5,4},{6,7},{7,6},{8,9},{9,8},{10,11... | collective-permute-start | bytes 786440 | tf_op jit(solution)/shard_map/ppermute | solution.py:436
  132.0 1.1 copy-start.17
  141.5 1.0 copy-start
  142.5 5.2 %collective-permute-start.14 = (bf16[16,256,128]{2,1,0:T(8,128)(2,1)}, bf16[16,256,128]{2,1,0:T(8,128)(2,1)S(1)}, u32[]{:S(2)}, u32[]{:S(2)}) collective-permute-start(bf16[16,256,128]{2,1,0:T(8,128)(2,1)} %shard_map.167.refs_1_), channel_id=1, source_target_pairs={{0,1},{1,0},{2,3},{3,2},{4,5},{5,4},{6,7},{7,6},{8,9},{9,8},{10,11... | collective-permute-start | bytes 3145736 | tf_op jit(solution)/shard_map/ppermute | solution.py:436
  147.7 1.0 copy-start.12
  (10 other events, 7.5 us)

commit v4 on v3

--- a/solution.py
+++ b/solution.py
@@ -158,25 +158,24 @@
 
 
 def unpack_kernel(own_ref, *refs):
-    pieces, (a_ref, b_ref) = refs[:G], refs[-2:]
-    width = pieces[0].shape[2]
-    for s in range(G):
-        columns = columns_of(own_ref, s, width)
-        piece = got_at(pieces, s)
-        a_ref[:, columns] = piece[0]
-        b_ref[:, columns] = piece[1]
-
-
-def unpack(own, pieces, after=()):
+    width = refs[0].shape[2]
+    for pair in range(2):
+        pieces, (a_ref, b_ref) = refs[pair * G : (pair + 1) * G], refs[2 * G + 2 * pair :][:2]
+        for s in range(G):
+            columns = columns_of(own_ref, s, width)
+            piece = got_at(pieces, s)
+            a_ref[:, columns] = piece[0]
+            b_ref[:, columns] = piece[1]
+
+
+def unpack(own, *pieces):
     shape = jax.ShapeDtypeStruct((T, pieces[0].shape[2] * G), bf16)
     return pl.pallas_call(
         unpack_kernel,
-        in_specs=[SCALAR]
-        + [pl.BlockSpec(a.shape) for a in pieces]
-        + [pl.BlockSpec(memory_space=pl.ANY)] * len(after),
-        cost_estimate=takes(2.2),
-        out_shape=[shape, shape],
-    )(own, *pieces, *after)
+        in_specs=[SCALAR] + [pl.BlockSpec(a.shape) for a in pieces],
+        cost_estimate=takes(3.5),
+        out_shape=4 * [shape],
+    )(own, *pieces)
 
 
 def add_kernel(own_ref, mine_ref, back_ref, *out_refs):
@@ -473,13 +472,12 @@
     n_parts = lax.axis_size(PARTS)
     dw = dw.reshape(n_parts, 2 * heads * 2 * F // n_parts, D)
     dw = resum(exchange(dw, PARTS), lax.axis_size("zh"))
-    first = regroup(first, crossed, [dw])
+    first = regroup(first, crossed)
     dw = exchange(dw, ("zh",))
     dw = resum(dw, lax.axis_size(GATHER), 1.0 / math.sqrt(tokens), after=[crossed, crossed_g])
     dw = exchange(dw, GATHER).reshape(n_xy, 2 * F, D)
-    attended, d_queries = unpack(place, first)
-    d_keys, d_values = unpack(place, regroup(added, crossed_g))
-    dw = once(dw, [attended, d_keys])
+    attended, d_queries, d_keys, d_values = unpack(place, *first, *regroup(added, crossed_g))
+    dw = once(dw, [attended])
     d_weight = spread(place, dw, [swap(dw)], heads)
     d_weight = d_weight.reshape(2, F, 2 * width)
     return attended[None], d_queries[None], d_keys[None], d_values[None], d_weight

time: 153 us -> 153 us (level)
  waiting for transfers between devices: 39.9 us -> 43.9 us
  Pallas kernels: 41 us -> 37.7 us
    all_to_all x5, waiting for transfers between devices: 20.8 us -> 24.4 us  [exchange(): return lax.all_to_all(value, axes, 0, 0)]
    pallas_call x1 -> x0, Pallas kernels: 1.76 us -> none  [second_of(): pl.pallas_call(second_kernel, in_specs=[pl.BlockSpec(pair.shape)] + [pl.B...]
    pallas_call x2 -> x1, Pallas kernels: 4.62 us -> 3.08 us  [unpack(): pl.pallas_call(unpack_kernel, in_specs=[SCALAR] + [pl.BlockSpec(a.shape)...]
    unnamed x45 -> x47, local copies, waits for them, and re-layouts: 10.8 us -> 10 us
  transfers between devices with their start and end apart: 20 -> 20, of which waited for: 9 -> 12; matrix products, arithmetic and copies ran while one was open for 4% -> 4% of each run, Pallas kernels for 12% -> 10%
where the time goes in v4:
time: 153 us; the launch traced here: 152 us
  starting transfers between devices  53.2 us (35%)
  waiting for transfers between devices  43.9 us (29%)
  Pallas kernels  37.7 us (25%)
  local copies, waits for them, and re-layouts  16 us (10%)
    all_to_all x5, starting transfers between devices, exchange(): return lax.all_to_all(value, axes, 0, 0)  34.8 us
    all_to_all x5, waiting for transfers between devices, exchange(): return lax.all_to_all(value, axes, 0, 0)  24.4 us
    pallas_call x1, Pallas kernels, main_call(): pl.pallas_call(main_kernel, grid_spec=pltpu.PrefetchScalarGridSpec(num_sc...  14.3 us
    ppermute x9, starting transfers between devices, swap(): return lax.ppermute(value, 'c', [(0, 1), (1, 0)])  11.9 us
    ppermute x1, waiting for transfers between devices, on_device(): back = lax.ppermute(back, Z, [(z + 1, z) for z in range(n_z - 1)])  11 us
    unnamed x47, local copies, waits for them, and re-layouts  10 us
    pallas_call x3, Pallas kernels, resum(): pl.pallas_call(lambda *refs: resum_kernel(scale, *refs), in_specs=[pl.Blo...  5.5 us
    ppermute x9, waiting for transfers between devices, swap(): return lax.ppermute(value, 'c', [(0, 1), (1, 0)])  5.49 us
  transfers between devices with their start and end apart: 20, of which 12 were waited for; matrix products, arithmetic and copies ran while one was open for 4% of the time, Pallas kernels for 10%

profile of v4, /device:TPU:1, one launch (start us, length us, event | category | flops | bytes accessed | tf_op | source)
XLA Modules:
  0.0 152.2 jit_solution(12197469671201337013)
XLA Ops:
  1.2 2.3 %shard_map.155 = (bf16[304,512]{1,0:T(8,128)(2,1)}, bf16[304,512]{1,0:T(8,128)(2,1)}, bf16[2,304,512]{2,1,0:T(8,128)(2,1)}) custom-call(s32[3]{0:T(128)} %pad_add_fusion.own_ref.refs_0_, bf16[128,2048]{1,0:T(8,128)(2,1)} %bitcast.32, bf16[128,2048]{1,0:T(8,128)(2,1)} %bitcast.33, bf16[128,128]{1,0:T(8,128)(2,1)} %bitcast.37, s32[1,128]{1,0:T(1,128)} %emb_ref.1, ...), custom_call_target="tpu_custom_call" | custom-call | bytes 7200000 | tf_op jit(solution)/shard_map/pallas_call | solution.py:118
  3.6 2.1 %collective-permute-start.2 = (bf16[2,304,512]{2,1,0:T(8,128)(2,1)}, bf16[2,304,512]{2,1,0:T(8,128)(2,1)S(1)}, u32[]{:S(2)}, u32[]{:S(2)}) collective-permute-start(bf16[2,304,512]{2,1,0:T(8,128)(2,1)} %get-tuple-element.27), channel_id=1, source_target_pairs={{0,2},{2,0},{1,3},{3,1},{4,6},{6,4},{5,7},{7,5},{8,10},{10,8},{9,1... | collective-permute-start | bytes 1867784 | tf_op jit(solution)/shard_map/ppermute | solution.py:438
  6.8 1.4 collective-permute-done.refs_0_.refs_1_.refs_2_.refs_7_
  9.0 1.7 %shard_map.156 = f32[16,40,128]{2,1,0:T(8,128)} custom-call(bf16[128,128]{1,0:T(8,128)(2,1)} %bitcast.38, s32[1,128]{1,0:T(1,128)} %emb_ref.1, s32[1,128]{1,0:T(1,128)} %typ_ref.1, bf16[304,512]{1,0:T(8,128)(2,1)} %copy-done.2), custom_call_target="tpu_custom_call" | custom-call | bytes 5760000 | tf_op jit(solution)/shard_map/pallas_call | solution.py:448
  10.7 8.7 %all-to-all-start = ((f32[16,40,128]{2,1,0:T(8,128)}), f32[16,40,128]{2,1,0:T(8,128)S(1)}, u32[]{:S(2)}, u32[]{:S(2)}) async-start(f32[16,40,128]{2,1,0:T(8,128)} %shard_map.156), calls=%async_computation | async-start | bytes 655360 | tf_op jit(solution)/shard_map/all_to_all | solution.py:419
  19.4 1.6 %collective-permute-start.3 = (bf16[304,512]{1,0:T(8,128)(2,1)S(1)}, bf16[304,512]{1,0:T(8,128)(2,1)S(1)}, u32[]{:S(2)}, u32[]{:S(2)}) collective-permute-start(bf16[304,512]{1,0:T(8,128)(2,1)S(1)} %slice_bitcast_fusion), channel_id=1, source_target_pairs={{0,1},{1,0},{2,3},{3,2},{4,5},{5,4},{6,7},{7,6},{8,9},{9,8},{10,11... | collective-permute-start | bytes 933896 | tf_op jit(solution)/shard_map/ppermute | solution.py:435
  21.0 2.3 %shard_map.157 = (bf16[256,512]{1,0:T(8,128)(2,1)}, bf16[256,512]{1,0:T(8,128)(2,1)}, bf16[2,256,512]{2,1,0:T(8,128)(2,1)}) custom-call(s32[3]{0:T(128)} %pad_add_fusion.own_ref.refs_0_, bf16[128,2048]{1,0:T(8,128)(2,1)} %bitcast.35, bf16[128,2048]{1,0:T(8,128)(2,1)} %bitcast.36), custom_call_target="tpu_custom_call" | custom-call | bytes 7200000 | tf_op jit(solution)/shard_map/pallas_call | solution.py:118
  23.3 1.5 collective-permute-start.1
  24.7 7.7 %all-to-all-done.refs_0_.refs_4_ = f32[16,40,128]{2,1,0:T(8,128)S(1)} async-done(((f32[16,40,128]{2,1,0:T(8,128)}), f32[16,40,128]{2,1,0:T(8,128)S(1)}, u32[]{:S(2)}, u32[]{:S(2)}) %all-to-all-start) | async-done | bytes 327712 | tf_op jit(solution)/shard_map/all_to_all | solution.py:419
  33.3 2.4 %shard_map.159 = bf16[3,304,512]{2,1,0:T(8,128)(2,1)} custom-call(s32[3]{0:T(128)} %pad_add_fusion.own_ref.refs_0_, bf16[304,512]{1,0:T(8,128)(2,1)} %get-tuple-element.26.refs_0_.refs_1_.refs_6_, bf16[304,512]{1,0:T(8,128)(2,1)} %copy-done.2, bf16[2,304,512]{2,1,0:T(8,128)(2,1)} %copy-done.1, bf16[304,512]{1,0:T(8,128)(2,1)} %copy-done.10, ...), custom_call_target="tpu_custom_call" | custom-call | bytes 8640000 | tf_op jit(solution)/shard_map/pallas_call | solution.py:137
  35.6 1.3 collective-permute-start.4
  38.1 1.7 %shard_map.158 = f32[16,40,128]{2,1,0:T(8,128)} custom-call(f32[16,40,128]{2,1,0:T(8,128)} %copy-done.9, bf16[2,256,512]{2,1,0:T(8,128)(2,1)} %copy-done.8), custom_call_target="tpu_custom_call" | custom-call | bytes 6840000 | tf_op jit(solution)/shard_map/pallas_call | solution.py:69
  39.9 6.5 %all-to-all-start.1 = ((f32[16,40,128]{2,1,0:T(8,128)}), f32[16,40,128]{2,1,0:T(8,128)S(1)}, u32[]{:S(2)}, u32[]{:S(2)}) async-start(f32[16,40,128]{2,1,0:T(8,128)} %shard_map.158), calls=%async_computation.1 | async-start | bytes 655360 | tf_op jit(solution)/shard_map/all_to_all | solution.py:419
  46.3 1.7 %slice_bitcast_fusion.3 = bf16[256,512]{1,0:T(8,128)(2,1)} fusion(bf16[2,256,512]{2,1,0:T(8,128)(2,1)} %copy-done.8), kind=kLoop, calls=%fused_computation.4 | loop fusion | bytes 524288 | tf_op jit(solution)/shard_map/squeeze | solution.py:441
  49.2 3.3 %reshape_reshape.3 = bf16[256,2,2048]{2,1,0:T(2,128)(2,1)S(1)} reshape(bf16[2,128,4096]{2,1,0:T(8,128)(2,1)} %param.17) | data formatting | bytes 4194304 | tf_op jit(solution)/shard_map/reshape;reshape | solution.py:460
  54.4 3.0 %collective-permute-done.4.refs_0_.refs_5_ = bf16[3,304,512]{2,1,0:T(8,128)(2,1)S(1)} collective-permute-done((bf16[3,304,512]{2,1,0:T(8,128)(2,1)}, bf16[3,304,512]{2,1,0:T(8,128)(2,1)S(1)}, u32[]{:S(2)}, u32[]{:S(2)}) %collective-permute-start.4) | collective-permute-done | bytes 933920 | tf_op jit(solution)/shard_map/ppermute | solution.py:456
  58.3 14.3 %shard_map.160 = (bf16[2,128,512]{2,1,0:T(8,128)(2,1)}, bf16[2,128,512]{2,1,0:T(8,128)(2,1)}, bf16[2,2,128,512]{3,2,1,0:T(8,128)(2,1)}, bf16[2,3,128,512]{3,2,1,...) custom-call(s32[3]{0:T(128)} %pad_add_fusion.own_ref.refs_0_, ...), custom_call_target="tpu_custom_call" | custom-call | bytes 54000000 | tf_op jit(solution)/shard_map/pallas_call | solution.py:381
  73.9 8.9 %all-to-all-start.2 = ((bf16[16,128,128]{2,1,0:T(8,128)(2,1)}), bf16[16,128,128]{2,1,0:T(8,128)(2,1)S(1)}, u32[]{:S(2)}, u32[]{:S(2)}) async-start(bf16[16,128,128]{2,1,0:T(8,128)(2,1)} %bitcast.34), calls=%async_computation.2 | async-start | bytes 1048576 | tf_op jit(solution)/shard_map/all_to_all | solution.py:419
  82.9 11.0 %collective-permute-done.10.back_ref = bf16[2,3,128,512]{3,2,1,0:T(8,128)(2,1)S(1)} collective-permute-done((bf16[2,3,128,512]{3,2,1,0:T(8,128)(2,1)}, bf16[2,3,128,512]{3,2,1,0:T(8,128)(2,1)S(1)}, u32[]{:S(2)}, u32[]{:S(2)}) %collective-permute-start.10) | collective-permute-done | bytes 786464 | tf_op jit(solution)/shard_map/ppermute | solution.py:466
  94.9 2.7 %shard_map.161 = (bf16[2,128,512]{2,1,0:T(8,128)(2,1)}, bf16[2,128,512]{2,1,0:T(8,128)(2,1)}, bf16[2,2,128,512]{3,2,1,0:T(8,128)(2,1)}) custom-call(s32[3]{0:T(128)} %pad_add_fusion.own_ref.refs_0_, bf16[2,4,128,512]{3,2,1,0:T(8,128)(2,1)} %get-tuple-element.33.mine_ref, bf16[2,3,128,512]{3,2,1,0:T(8,128)(2,1)} %copy-done.14), custom_call_target="tpu_custom_call" | custom-call | bytes 9720000 | tf_op jit(solution)/shard_map/pallas_call | solution.py:197
  97.7 3.6 %all-to-all-done.2.refs_0_ = bf16[16,128,128]{2,1,0:T(8,128)(2,1)S(1)} async-done(((bf16[16,128,128]{2,1,0:T(8,128)(2,1)}), bf16[16,128,128]{2,1,0:T(8,128)(2,1)S(1)}, u32[]{:S(2)}, u32[]{:S(2)}) %all-to-all-start.2) | async-done | bytes 524320 | tf_op jit(solution)/shard_map/all_to_all | solution.py:419
  102.1 1.8 %shard_map.163 = bf16[4,128,128]{2,1,0:T(8,128)(2,1)} custom-call(bf16[16,128,128]{2,1,0:T(8,128)(2,1)} %copy-done.11), custom_call_target="tpu_custom_call" | custom-call | bytes 6840000 | tf_op jit(solution)/shard_map/pallas_call | solution.py:69
  103.9 4.4 %all-to-all-start.3 = ((bf16[4,128,128]{2,1,0:T(8,128)(2,1)}), bf16[4,128,128]{2,1,0:T(8,128)(2,1)S(1)}, u32[]{:S(2)}, u32[]{:S(2)}) async-start(bf16[4,128,128]{2,1,0:T(8,128)(2,1)} %shard_map.163), calls=%async_computation.3 | async-start | bytes 262144 | tf_op jit(solution)/shard_map/all_to_all | solution.py:419
  108.3 7.3 %all-to-all-done.3.refs_0_ = bf16[4,128,128]{2,1,0:T(8,128)(2,1)S(1)} async-done(((bf16[4,128,128]{2,1,0:T(8,128)(2,1)}), bf16[4,128,128]{2,1,0:T(8,128)(2,1)S(1)}, u32[]{:S(2)}, u32[]{:S(2)}) %all-to-all-start.3) | async-done | bytes 131104 | tf_op jit(solution)/shard_map/all_to_all | solution.py:419
  117.1 2.0 %shard_map.164 = bf16[32,128,128]{2,1,0:T(8,128)(2,1)} custom-call(bf16[4,128,128]{2,1,0:T(8,128)(2,1)} %copy-done.15, bf16[2,2,128,512]{3,2,1,0:T(8,128)(2,1)} %copy-done.4, bf16[2,2,128,512]{3,2,1,0:T(8,128)(2,1)} %copy-done.6), custom_call_target="tpu_custom_call" | custom-call | bytes 6840000 | tf_op jit(solution)/shard_map/pallas_call | solution.py:69
  119.1 6.4 %all-to-all-start.4 = ((bf16[32,128,128]{2,1,0:T(8,128)(2,1)}), bf16[32,128,128]{2,1,0:T(8,128)(2,1)S(1)}, u32[]{:S(2)}, u32[]{:S(2)}) async-start(bf16[32,128,128]{2,1,0:T(8,128)(2,1)} %shard_map.164), calls=%async_computation.4 | async-start | bytes 2097152 | tf_op jit(solution)/shard_map/all_to_all | solution.py:419
  125.4 3.9 %collective-permute-start.7 = (bf16[2,128,512]{2,1,0:T(8,128)(2,1)S(1)}, bf16[2,128,512]{2,1,0:T(8,128)(2,1)S(1)}, u32[]{:S(2)}, u32[]{:S(2)}) collective-permute-start(bf16[2,128,512]{2,1,0:T(8,128)(2,1)S(1)} %copy-done.20), channel_id=1, source_target_pairs={{0,1},{1,0},{2,3},{3,2},{4,5},{5,4},{6,7},{7,6},{8,9},{9,8},{10,11... | collective-permute-start | bytes 786440 | tf_op jit(solution)/shard_map/ppermute | solution.py:435
  132.6 3.1 %shard_map.162 = (bf16[128,2048]{1,0:T(8,128)(2,1)}, bf16[128,2048]{1,0:T(8,128)(2,1)}, bf16[128,2048]{1,0:T(8,128)(2,1)}, bf16[128,2048]{1,0:T(8,128)(2,1)}) custom-call(s32[3]{0:T(128)} %pad_add_fusion.own_ref.refs_0_, bf16[2,128,512]{2,1,0:T(8,128)(2,1)} %get-tuple-element.30.refs_0_, bf16[2,128,512]{2,1,0:T(8,128)(2,1)} %copy-done.16, ...), custom_call_target="tpu_custom_call" | custom-call | bytes 12600000 | tf_op jit(solution)/shard_map/pallas_call | solution.py:173
  135.7 5.8 %all-to-all-done.4 = bf16[32,128,128]{2,1,0:T(8,128)(2,1)S(1)} async-done(((bf16[32,128,128]{2,1,0:T(8,128)(2,1)}), bf16[32,128,128]{2,1,0:T(8,128)(2,1)S(1)}, u32[]{:S(2)}, u32[]{:S(2)}) %all-to-all-start.4) | async-done | bytes 1048608 | tf_op jit(solution)/shard_map/all_to_all | solution.py:419
  142.5 2.7 %collective-permute-start.14 = (bf16[16,256,128]{2,1,0:T(8,128)(2,1)}, bf16[16,256,128]{2,1,0:T(8,128)(2,1)S(1)}, u32[]{:S(2)}, u32[]{:S(2)}) collective-permute-start(bf16[16,256,128]{2,1,0:T(8,128)(2,1)} %shard_map.165.refs_1_), channel_id=1, source_target_pairs={{0,1},{1,0},{2,3},{3,2},{4,5},{5,4},{6,7},{7,6},{8,9},{9,8},{10,11... | collective-permute-start | bytes 3145736 | tf_op jit(solution)/shard_map/ppermute | solution.py:435
  145.2 2.5 %collective-permute-done.14.refs_2_ = bf16[16,256,128]{2,1,0:T(8,128)(2,1)S(1)} collective-permute-done((bf16[16,256,128]{2,1,0:T(8,128)(2,1)}, bf16[16,256,128]{2,1,0:T(8,128)(2,1)S(1)}, u32[]{:S(2)}, u32[]{:S(2)}) %collective-permute-start.14) | collective-permute-done | bytes 1048608 | tf_op jit(solution)/shard_map/ppermute | solution.py:435
  148.7 3.5 %shard_map.166 = bf16[256,4096]{1,0:T(8,128)(2,1)} custom-call(s32[3]{0:T(128)} %pad_add_fusion.own_ref.refs_0_, bf16[16,256,128]{2,1,0:T(8,128)(2,1)} %shard_map.165.refs_1_, bf16[16,256,128]{2,1,0:T(8,128)(2,1)} %copy-done.13), custom_call_target="tpu_custom_call" | custom-call | bytes 12240000 | tf_op jit(solution)/shard_map/pallas_call | solution.py:229
  (75 shorter events, 18.4 us)
Async XLA Ops:
  3.6 15.8 %collective-permute-start.2 = (bf16[2,304,512]{2,1,0:T(8,128)(2,1)}, bf16[2,304,512]{2,1,0:T(8,128)(2,1)S(1)}, u32[]{:S(2)}, u32[]{:S(2)}) collective-permute-start(bf16[2,304,512]{2,1,0:T(8,128)(2,1)} %get-tuple-element.27), channel_id=1, source_target_pairs={{0,2},{2,0},{1,3},{3,1},{4,6},{6,4},{5,7},{7,5},{8,10},{10,8},{9,1... | collective-permute-start | bytes 1867784 | tf_op jit(solution)/shard_map/ppermute | solution.py:438
  5.7 2.6 %collective-permute-start = (bf16[304,512]{1,0:T(8,128)(2,1)}, bf16[304,512]{1,0:T(8,128)(2,1)S(1)}, u32[]{:S(2)}, u32[]{:S(2)}) collective-permute-start(bf16[304,512]{1,0:T(8,128)(2,1)} %get-tuple-element.24), channel_id=1, source_target_pairs={{0,1},{1,0},{2,3},{3,2},{4,5},{5,4},{6,7},{7,6},{8,9},{9,8},{10,11... | collective-permute-start | bytes 933896 | tf_op jit(solution)/shard_map/ppermute | solution.py:435
  10.7 21.8 %all-to-all-start = ((f32[16,40,128]{2,1,0:T(8,128)}), f32[16,40,128]{2,1,0:T(8,128)S(1)}, u32[]{:S(2)}, u32[]{:S(2)}) async-start(f32[16,40,128]{2,1,0:T(8,128)} %shard_map.156), calls=%async_computation | async-start | bytes 655360 | tf_op jit(solution)/shard_map/all_to_all | solution.py:419
  19.4 13.1 %copy-start.1 = (bf16[2,304,512]{2,1,0:T(8,128)(2,1)}, bf16[2,304,512]{2,1,0:T(8,128)(2,1)S(1)}, u32[]{:S(2)}) copy-start(bf16[2,304,512]{2,1,0:T(8,128)(2,1)S(1)} %collective-permute-done.2.refs_2_.refs_3_.refs_8_) | copy-start | bytes 1867780
  19.4 13.0 %collective-permute-start.3 = (bf16[304,512]{1,0:T(8,128)(2,1)S(1)}, bf16[304,512]{1,0:T(8,128)(2,1)S(1)}, u32[]{:S(2)}, u32[]{:S(2)}) collective-permute-start(bf16[304,512]{1,0:T(8,128)(2,1)S(1)} %slice_bitcast_fusion), channel_id=1, source_target_pairs={{0,1},{1,0},{2,3},{3,2},{4,5},{5,4},{6,7},{7,6},{8,9},{9,8},{10,11... | collective-permute-start | bytes 933896 | tf_op jit(solution)/shard_map/ppermute | solution.py:435
  23.3 14.1 %collective-permute-start.1 = (bf16[2,256,512]{2,1,0:T(8,128)(2,1)}, bf16[2,256,512]{2,1,0:T(8,128)(2,1)S(1)}, u32[]{:S(2)}, u32[]{:S(2)}) collective-permute-start(bf16[2,256,512]{2,1,0:T(8,128)(2,1)} %get-tuple-element.25), channel_id=1, source_target_pairs={{0,2},{2,0},{1,3},{3,1},{4,6},{6,4},{5,7},{7,5},{8,10},{10,8},{9,1... | collective-permute-start | bytes 1572872 | tf_op jit(solution)/shard_map/ppermute | solution.py:438
  35.6 21.7 %collective-permute-start.4 = (bf16[3,304,512]{2,1,0:T(8,128)(2,1)}, bf16[3,304,512]{2,1,0:T(8,128)(2,1)S(1)}, u32[]{:S(2)}, u32[]{:S(2)}) collective-permute-start(bf16[3,304,512]{2,1,0:T(8,128)(2,1)} %shard_map.159), channel_id=1, source_target_pairs={{0,4},{4,8},{8,12},{12,16},{16,20},{20,24},{24,28},{1,5},{5,9},{9,... | collective-permute-start | bytes 2801672 | tf_op jit(solution)/shard_map/ppermute | solution.py:456
  37.0 17.4 %collective-permute-start.5 = (bf16[256,512]{1,0:T(8,128)(2,1)}, bf16[256,512]{1,0:T(8,128)(2,1)}, u32[]{:S(2)}, u32[]{:S(2)}) collective-permute-start(bf16[256,512]{1,0:T(8,128)(2,1)} %get-tuple-element.29), channel_id=1, source_target_pairs={{0,1},{1,0},{2,3},{3,2},{4,5},{5,4},{6,7},{7,6},{8,9},{9,8},{10,11... | collective-permute-start | bytes 786440 | tf_op jit(solution)/shard_map/ppermute | solution.py:435
  39.9 14.5 %all-to-all-start.1 = ((f32[16,40,128]{2,1,0:T(8,128)}), f32[16,40,128]{2,1,0:T(8,128)S(1)}, u32[]{:S(2)}, u32[]{:S(2)}) async-start(f32[16,40,128]{2,1,0:T(8,128)} %shard_map.158), calls=%async_computation.1 | async-start | bytes 655360 | tf_op jit(solution)/shard_map/all_to_all | solution.py:419
  48.0 6.3 %collective-permute-start.6 = (bf16[256,512]{1,0:T(8,128)(2,1)}, bf16[256,512]{1,0:T(8,128)(2,1)}, u32[]{:S(2)}, u32[]{:S(2)}) collective-permute-start(bf16[256,512]{1,0:T(8,128)(2,1)} %slice_bitcast_fusion.3), channel_id=1, source_target_pairs={{0,1},{1,0},{2,3},{3,2},{4,5},{5,4},{6,7},{7,6},{8,9},{9,8},{10,11... | collective-permute-start | bytes 786440 | tf_op jit(solution)/shard_map/ppermute | solution.py:435
  52.5 1.2 copy-start.22
  54.4 3.0 %copy-start.12 = (f32[16,40,128]{2,1,0:T(8,128)}, f32[16,40,128]{2,1,0:T(8,128)S(1)}, u32[]{:S(2)}) copy-start(f32[16,40,128]{2,1,0:T(8,128)S(1)} %all-to-all-done.1.stat_ref) | copy-start | bytes 983044
  57.3 1.0 copy-start.3
  72.6 21.3 %collective-permute-start.10 = (bf16[2,3,128,512]{3,2,1,0:T(8,128)(2,1)}, bf16[2,3,128,512]{3,2,1,0:T(8,128)(2,1)S(1)}, u32[]{:S(2)}, u32[]{:S(2)}) collective-permute-start(bf16[2,3,128,512]{3,2,1,0:T(8,128)(2,1)} %get-tuple-element.34), channel_id=1, source_target_pairs={{4,0},{8,4},{12,8},{16,12},{20,16},{24,20},{28,24},{5,1},{9,5},{13... | collective-permute-start | bytes 2359304 | tf_op jit(solution)/shard_map/ppermute | solution.py:466
  73.9 27.4 %all-to-all-start.2 = ((bf16[16,128,128]{2,1,0:T(8,128)(2,1)}), bf16[16,128,128]{2,1,0:T(8,128)(2,1)S(1)}, u32[]{:S(2)}, u32[]{:S(2)}) async-start(bf16[16,128,128]{2,1,0:T(8,128)(2,1)} %bitcast.34), calls=%async_computation.2 | async-start | bytes 1048576 | tf_op jit(solution)/shard_map/all_to_all | solution.py:419
  82.8 25.5 %collective-permute-start.8 = (bf16[2,2,128,512]{3,2,1,0:T(8,128)(2,1)}, bf16[2,2,128,512]{3,2,1,0:T(8,128)(2,1)S(1)}, u32[]{:S(2)}, u32[]{:S(2)}) collective-permute-start(bf16[2,2,128,512]{3,2,1,0:T(8,128)(2,1)} %get-tuple-element.32), channel_id=1, source_target_pairs={{0,2},{2,0},{1,3},{3,1},{4,6},{6,4},{5,7},{7,5},{8,10},{10,8},{9,1... | collective-permute-start | bytes 1572872 | tf_op jit(solution)/shard_map/ppermute | solution.py:438
  97.6 18.0 %collective-permute-start.12 = (bf16[2,2,128,512]{3,2,1,0:T(8,128)(2,1)}, bf16[2,2,128,512]{3,2,1,0:T(8,128)(2,1)S(1)}, u32[]{:S(2)}, u32[]{:S(2)}) collective-permute-start(bf16[2,2,128,512]{3,2,1,0:T(8,128)(2,1)} %get-tuple-element.37), channel_id=1, source_target_pairs={{0,2},{2,0},{1,3},{3,1},{4,6},{6,4},{5,7},{7,5},{8,10},{10,8},{9,1... | collective-permute-start | bytes 1572872 | tf_op jit(solution)/shard_map/ppermute | solution.py:438
  103.9 11.7 %all-to-all-start.3 = ((bf16[4,128,128]{2,1,0:T(8,128)(2,1)}), bf16[4,128,128]{2,1,0:T(8,128)(2,1)S(1)}, u32[]{:S(2)}, u32[]{:S(2)}) async-start(bf16[4,128,128]{2,1,0:T(8,128)(2,1)} %shard_map.163), calls=%async_computation.3 | async-start | bytes 262144 | tf_op jit(solution)/shard_map/all_to_all | solution.py:419
  108.3 17.1 %copy-start.20 = (bf16[2,128,512]{2,1,0:T(8,128)(2,1)S(1)}, bf16[2,128,512]{2,1,0:T(8,128)(2,1)}, u32[]{:S(2)}) copy-start(bf16[2,128,512]{2,1,0:T(8,128)(2,1)} %get-tuple-element.31) | copy-start | bytes 786436
  108.3 21.4 %copy-start.21 = (bf16[2,128,512]{2,1,0:T(8,128)(2,1)S(1)}, bf16[2,128,512]{2,1,0:T(8,128)(2,1)}, u32[]{:S(2)}) copy-start(bf16[2,128,512]{2,1,0:T(8,128)(2,1)} %get-tuple-element.36) | copy-start | bytes 786436
  108.3 7.3 %copy-start.4 = (bf16[2,2,128,512]{3,2,1,0:T(8,128)(2,1)}, bf16[2,2,128,512]{3,2,1,0:T(8,128)(2,1)S(1)}, u32[]{:S(2)}) copy-start(bf16[2,2,128,512]{3,2,1,0:T(8,128)(2,1)S(1)} %collective-permute-done.8.refs_2_.refs_1_) | copy-start | bytes 1572868
  119.1 10.3 %copy-start.5 = (bf16[2,2,128,512]{3,2,1,0:T(8,128)(2,1)S(1)}, bf16[2,2,128,512]{3,2,1,0:T(8,128)(2,1)}, u32[]{:S(2)}) copy-start(bf16[2,2,128,512]{3,2,1,0:T(8,128)(2,1)} %copy-done.4) | copy-start | bytes 1572868
  119.1 11.1 %copy-start.7 = (bf16[2,2,128,512]{3,2,1,0:T(8,128)(2,1)S(1)}, bf16[2,2,128,512]{3,2,1,0:T(8,128)(2,1)}, u32[]{:S(2)}) copy-start(bf16[2,2,128,512]{3,2,1,0:T(8,128)(2,1)} %copy-done.6) | copy-start | bytes 1572868
  119.1 22.5 %all-to-all-start.4 = ((bf16[32,128,128]{2,1,0:T(8,128)(2,1)}), bf16[32,128,128]{2,1,0:T(8,128)(2,1)S(1)}, u32[]{:S(2)}, u32[]{:S(2)}) async-start(bf16[32,128,128]{2,1,0:T(8,128)(2,1)} %shard_map.164), calls=%async_computation.4 | async-start | bytes 2097152 | tf_op jit(solution)/shard_map/all_to_all | solution.py:419
  125.4 5.1 %collective-permute-start.7 = (bf16[2,128,512]{2,1,0:T(8,128)(2,1)S(1)}, bf16[2,128,512]{2,1,0:T(8,128)(2,1)S(1)}, u32[]{:S(2)}, u32[]{:S(2)}) collective-permute-start(bf16[2,128,512]{2,1,0:T(8,128)(2,1)S(1)} %copy-done.20), channel_id=1, source_target_pairs={{0,1},{1,0},{2,3},{3,2},{4,5},{5,4},{6,7},{7,6},{8,9},{9,8},{10,11... | collective-permute-start | bytes 786440 | tf_op jit(solution)/shard_map/ppermute | solution.py:435
  129.4 1.8 %collective-permute-start.9 = (bf16[2,128,512]{2,1,0:T(8,128)(2,1)S(1)}, bf16[2,128,512]{2,1,0:T(8,128)(2,1)S(1)}, u32[]{:S(2)}, u32[]{:S(2)}) collective-permute-start(bf16[2,128,512]{2,1,0:T(8,128)(2,1)S(1)} %slice_bitcast_fusion.2), channel_id=1, source_target_pairs={{0,1},{1,0},{2,3},{3,2},{4,5},{5,4},{6,7},{7,6},{8,9},{9,8},{10,11... | collective-permute-start | bytes 786440 | tf_op jit(solution)/shard_map/ppermute | solution.py:435
  129.7 1.9 %collective-permute-start.11 = (bf16[2,128,512]{2,1,0:T(8,128)(2,1)S(1)}, bf16[2,128,512]{2,1,0:T(8,128)(2,1)S(1)}, u32[]{:S(2)}, u32[]{:S(2)}) collective-permute-start(bf16[2,128,512]{2,1,0:T(8,128)(2,1)S(1)} %copy-done.21), channel_id=1, source_target_pairs={{0,1},{1,0},{2,3},{3,2},{4,5},{5,4},{6,7},{7,6},{8,9},{9,8},{10,11... | collective-permute-start | bytes 786440 | tf_op jit(solution)/shard_map/ppermute | solution.py:435
  130.2 1.7 %collective-permute-start.13 = (bf16[2,128,512]{2,1,0:T(8,128)(2,1)S(1)}, bf16[2,128,512]{2,1,0:T(8,128)(2,1)S(1)}, u32[]{:S(2)}, u32[]{:S(2)}) collective-permute-start(bf16[2,128,512]{2,1,0:T(8,128)(2,1)S(1)} %slice_bitcast_fusion.1), channel_id=1, source_target_pairs={{0,1},{1,0},{2,3},{3,2},{4,5},{5,4},{6,7},{7,6},{8,9},{9,8},{10,11... | collective-permute-start | bytes 786440 | tf_op jit(solution)/shard_map/ppermute | solution.py:435
  130.5 1.4 copy-start.16
  141.5 1.0 copy-start
  142.5 5.2 %collective-permute-start.14 = (bf16[16,256,128]{2,1,0:T(8,128)(2,1)}, bf16[16,256,128]{2,1,0:T(8,128)(2,1)S(1)}, u32[]{:S(2)}, u32[]{:S(2)}) collective-permute-start(bf16[16,256,128]{2,1,0:T(8,128)(2,1)} %shard_map.165.refs_1_), channel_id=1, source_target_pairs={{0,1},{1,0},{2,3},{3,2},{4,5},{5,4},{6,7},{7,6},{8,9},{9,8},{10,11... | collective-permute-start | bytes 3145736 | tf_op jit(solution)/shard_map/ppermute | solution.py:435
  147.7 1.0 copy-start.13
  (11 other events, 8.4 us)
